TPU v7x, 32 devices: a whole 2x2x4 slice. The times are simulated.
32 devices in a mesh: band: 1, rcol: 4 (over y, core), rrow: 8 (over z, x).
Axes of the slice: x: 2, y: 2, z: 4, core: 2. Of those that a mesh axis runs over, the one named last changes fastest.
Arguments:
- spectra: float32 [6, 2, 1536, 1024], P('band', None, ('rcol', 'rrow')), may hold values from -6 to 6
- valid: int32 [1536, 1024], P(('rcol', 'rrow')), may hold values 0 or 1
Outputs:
- cross: float32 [6, 2, 1536, 1152], P('band', None, 'rcol', 'rrow')
All inputs are finite; a program needn't handle non-finite values. No bound on the sum of `valid` on one device may be relied on, other than what follows from the above.
Results may differ from a plain program's by a relative error of at most 0.0035.
Values may be sent and summed in bfloat16 or wider, within the bound.
No kernel may reach another device: no remote copies, remote signals or barrier semaphores. Data moves between devices by JAX's collectives and lax.ppermute only.
A program may use at most 128 MiB of HBM per device.

v0:
```python
import jax
import jax.numpy as jnp
from jax import lax
from jax.sharding import PartitionSpec as P


def passed_along(value, axis, steps):
    count = lax.axis_size(axis)
    pairs = [(source, (source + steps) % count) for source in range(count)]
    return lax.ppermute(value, axis, pairs)


def whiten(spectra, valid):
    power = jnp.mean(spectra[:, 0] * spectra[:, 0] + spectra[:, 1] * spectra[:, 1], axis=0)
    amplitude = jnp.sqrt(jnp.maximum(power, 1.0))
    factor = valid.astype(jnp.float32) / amplitude
    return (spectra * factor[None, None]).astype(jnp.bfloat16)


def shards(spectra, valid):
    white = whiten(spectra, valid)
    windows = white.shape[-1]
    rows = lax.all_gather(white, "rrow", axis=2, tiled=True)
    reach = lax.axis_size("rcol") // 2 + 1
    blocks = []
    current = white
    for dist in range(reach):
        if dist == 0:
            partner = white
        else:
            current = passed_along(current, "rcol", -1)
            partner = current
        real_part = jnp.einsum(
            "fgw,fbw->fgb", rows[:, 0], partner[:, 0], preferred_element_type=jnp.float32
        ) + jnp.einsum(
            "fgw,fbw->fgb", rows[:, 1], partner[:, 1], preferred_element_type=jnp.float32
        )
        imag_part = jnp.einsum(
            "fgw,fbw->fgb", rows[:, 1], partner[:, 0], preferred_element_type=jnp.float32
        ) - jnp.einsum(
            "fgw,fbw->fgb", rows[:, 0], partner[:, 1], preferred_element_type=jnp.float32
        )
        blocks.append(jnp.stack([real_part, imag_part], axis=1) / jnp.float32(windows))
    return jnp.concatenate(blocks, axis=-1)


def solution(mesh):
    in_specs = (P("band", None, ("rcol", "rrow"), None), P(("rcol", "rrow"), None))
    out_specs = P("band", None, "rcol", "rrow")
    return jax.shard_map(shards, mesh=mesh, in_specs=in_specs, out_specs=out_specs, check_vma=False)
```

profile of v0, /device:TPU:0, one launch (start us, length us, event | category | flops | bytes accessed | tf_op | source)
XLA Modules:
  0.0 184.0 jit_solution(7071606189191820929)
XLA Ops:
  6.5 0.0 copy-start
  6.5 0.0 all-gather.2.cloned.1.call-start
  6.5 2.0 %add_reduce_fusion = f32[48,1024]{1,0:T(8,128)S(1)} fusion(f32[6,2,48,1024]{3,2,1,0:T(8,128)} %param.2), kind=kLoop, calls=%fused_computation.29 | loop fusion | flops 1130496 | bytes 2555904 | tf_op jit(solution)/shard_map/reduce_sum | solution.py:14
  8.6 1.0 rsqrt_multiply_fusion
  9.6 0.0 copy-done
  9.6 1.3 fusion
  10.9 0.0 copy-start.1
  10.9 0.0 all-gather.2.cloned.1.call-update
  10.9 2.5 %collective-permute-start = (bf16[6,2,48,1024]{3,2,0,1:T(8,128)(2,1)}, bf16[6,2,48,1024]{3,2,0,1:T(8,128)(2,1)S(1)}, u32[]{:S(2)}, u32[]{:S(2)}) collective-permute-start(bf16[6,2,48,1024]{3,2,0,1:T(8,128)(2,1)} %fusion), channel_id=1, source_target_pairs={{0,24},{8,0},{16,8},{24,16},{1,25},{9,1},{17,9},{25,17},{2,26},{10... | collective-permute-start | bytes 3538952 | tf_op jit(solution)/shard_map/ppermute | solution.py:10
  13.4 14.0 %collective-permute-done = bf16[6,2,48,1024]{3,2,0,1:T(8,128)(2,1)S(1)} collective-permute-done((bf16[6,2,48,1024]{3,2,0,1:T(8,128)(2,1)}, bf16[6,2,48,1024]{3,2,0,1:T(8,128)(2,1)S(1)}, u32[]{:S(2)}, u32[]{:S(2)}) %collective-permute-start) | collective-permute-done | bytes 1179680 | tf_op jit(solution)/shard_map/ppermute | solution.py:10
  27.4 2.2 %collective-permute-start.1 = (bf16[6,2,48,1024]{3,2,0,1:T(8,128)(2,1)S(1)}, bf16[6,2,48,1024]{3,2,0,1:T(8,128)(2,1)S(1)}, u32[]{:S(2)}, u32[]{:S(2)}) collective-permute-start(bf16[6,2,48,1024]{3,2,0,1:T(8,128)(2,1)S(1)} %collective-permute-done), channel_id=1, source_target_pairs={{0,24},{8,0},{16,8},{24,16},{1,25},{9,1},{17,9},{25,17},{2,26},{10... | collective-permute-start | bytes 3538952 | tf_op jit(solution)/shard_map/ppermute | solution.py:10
  29.6 122.2 %all-gather.2.cloned.1.call-done = bf16[6,2,384,1024]{3,2,0,1:T(8,128)(2,1)} async-done(((bf16[6,2,48,1024]{3,2,0,1:T(8,128)(2,1)}), bf16[6,2,384,1024]{3,2,0,1:T(8,128)(2,1)}) %all-gather.2.cloned.1.call-update) | async-done | bytes 9437200 | tf_op jit(solution)/shard_map/all_gather | solution.py:23
  151.8 4.1 %fusion.5 = f32[6,384,48]{1,2,0:T(8,128)S(1)} fusion(bf16[6,2,384,1024]{3,2,0,1:T(8,128)(2,1)} %all-gather.2.cloned.1.call-done, bf16[6,2,48,1024]{3,2,0,1:T(8,128)(2,1)} %fusion), kind=kOutput, calls=%fused_computation.9 | convolution fusion | flops 226492416 | bytes 5750784 | tf_op jit(solution)/shard_map/fgw,fbw->fgb/dot_general | solution.py:40
  156.0 0.0 copy-done.1
  156.0 4.0 %fusion.6 = f32[6,384,48]{1,2,0:T(8,128)S(1)} fusion(bf16[6,2,384,1024]{3,2,0,1:T(8,128)(2,1)} %all-gather.2.cloned.1.call-done, bf16[6,2,48,1024]{3,2,0,1:T(8,128)(2,1)S(1)} %copy-done.1), kind=kOutput, calls=%fused_computation.10 | convolution fusion | flops 226492416 | bytes 5750784 | tf_op jit(solution)/shard_map/fgw,fbw->fgb/dot_general | solution.py:33
  159.9 0.0 copy-done.2
  160.0 1.5 fusion.3
  161.5 1.5 fusion.10
  163.0 1.5 fusion.16
  164.5 1.5 fusion.14
  166.0 0.1 maximum_multiply_fusion
  166.1 1.5 fusion.18
  167.6 1.5 fusion.22
  169.1 0.1 maximum_multiply_fusion.1
  169.2 0.0 collective-permute-done.1
  169.2 1.5 fusion.1
  170.7 1.5 fusion.8
  172.2 1.5 fusion.20
  173.7 1.5 fusion.24
  175.2 0.1 maximum_multiply_fusion.2
  175.3 0.2 pad_maximum_fusion
  175.5 1.7 copy.4
  (1 shorter events, 0.0 us)
Async XLA Ops:
  6.5 3.0 %copy-start = (f32[6,2,48,1024]{3,2,1,0:T(8,128)S(1)}, f32[6,2,48,1024]{3,2,1,0:T(8,128)}, u32[]{:S(2)}) copy-start(f32[6,2,48,1024]{3,2,1,0:T(8,128)} %param.2) | copy-start | bytes 7077892
  6.5 145.3 %all-gather.2.cloned.1.call-start = ((), (), s32[]{:S(2)}) async-start(), calls=%async_computation | async-start | bytes 10616832 | tf_op jit(solution)/shard_map/all_gather | solution.py:23
  10.9 145.1 %copy-start.1 = (bf16[6,2,48,1024]{3,2,0,1:T(8,128)(2,1)S(1)}, bf16[6,2,48,1024]{3,2,0,1:T(8,128)(2,1)}, u32[]{:S(2)}) copy-start(bf16[6,2,48,1024]{3,2,0,1:T(8,128)(2,1)} %fusion) | copy-start | bytes 3538948
  10.9 16.5 %collective-permute-start = (bf16[6,2,48,1024]{3,2,0,1:T(8,128)(2,1)}, bf16[6,2,48,1024]{3,2,0,1:T(8,128)(2,1)S(1)}, u32[]{:S(2)}, u32[]{:S(2)}) collective-permute-start(bf16[6,2,48,1024]{3,2,0,1:T(8,128)(2,1)} %fusion), channel_id=1, source_target_pairs={{0,24},{8,0},{16,8},{24,16},{1,25},{9,1},{17,9},{25,17},{2,26},{10... | collective-permute-start | bytes 3538952 | tf_op jit(solution)/shard_map/ppermute | solution.py:10
  27.4 141.8 %collective-permute-start.1 = (bf16[6,2,48,1024]{3,2,0,1:T(8,128)(2,1)S(1)}, bf16[6,2,48,1024]{3,2,0,1:T(8,128)(2,1)S(1)}, u32[]{:S(2)}, u32[]{:S(2)}) collective-permute-start(bf16[6,2,48,1024]{3,2,0,1:T(8,128)(2,1)S(1)} %collective-permute-done), channel_id=1, source_target_pairs={{0,24},{8,0},{16,8},{24,16},{1,25},{9,1},{17,9},{25,17},{2,26},{10... | collective-permute-start | bytes 3538952 | tf_op jit(solution)/shard_map/ppermute | solution.py:10
  151.8 8.1 %copy-start.2 = (bf16[6,2,384,1024]{3,2,0,1:T(8,128)(2,1)S(1)}, bf16[6,2,384,1024]{3,2,0,1:T(8,128)(2,1)}, u32[]{:S(2)}) copy-start(bf16[6,2,384,1024]{3,2,0,1:T(8,128)(2,1)} %all-gather.2.cloned.1.call-done) | copy-start | bytes 28311556
Sparse Core Ops, SparseCore 0:
  11.0 140.7 all-gather.1
where the time goes:
time: 184 us
  waiting for transfers between devices  136 us (74%)
  matrix products  23.1 us (13%)
  between operations  13.6 us (7%)
  other arithmetic  4.69 us (3%)
  starting transfers between devices  4.66 us (3%)
    all_gather x1, waiting for transfers between devices, shards(): rows = lax.all_gather(white, 'rrow', axis=2, tiled=True)  122 us
    ppermute x2, waiting for transfers between devices, passed_along(): return lax.ppermute(value, axis, pairs)  14 us
    dot_general x3, matrix products, shards(): jnp.einsum('fgw,fbw->fgb', rows[:, 0], partner[:, 1], preferred_element_t...  7.12 us
    dot_general x3, matrix products, shards(): jnp.einsum('fgw,fbw->fgb', rows[:, 0], partner[:, 0], preferred_element_t...  7 us
    ppermute x2, starting transfers between devices, passed_along(): return lax.ppermute(value, axis, pairs)  4.66 us
    dot_general x3, matrix products, shards(): jnp.einsum('fgw,fbw->fgb', rows[:, 1], partner[:, 1], preferred_element_t...  4.52 us
    dot_general x3, matrix products, shards(): jnp.einsum('fgw,fbw->fgb', rows[:, 1], partner[:, 0], preferred_element_t...  4.51 us
  transfers between devices with their start and end apart: 3, of which 2 were waited for; matrix products, arithmetic and copies ran while one was open for 9% of the time, Pallas kernels for 0%

commit v1 on v0

v1 whole, which is shorter than its diff:
```python
import functools

import jax
import jax.numpy as jnp
from jax import lax
from jax.experimental import pallas as pl
from jax.experimental.pallas import tpu as pltpu
from jax.sharding import PartitionSpec as P

VMEM_BYTES = 40 * 1024 * 1024


def moved_by_xor(value, axis, bits):
    count = lax.axis_size(axis)
    return lax.ppermute(value, axis, [(source, source ^ bits) for source in range(count)])


def moved_by_shift(value, axis, steps):
    count = lax.axis_size(axis)
    return lax.ppermute(value, axis, [(source, (source + steps) % count) for source in range(count)])


def whiten_kernel(half_ref, spectra_ref, valid_ref, *out_refs):
    bins = spectra_ref.shape[0]
    share = bins // 2
    half = half_ref[0]
    total = spectra_ref[0, 0] * spectra_ref[0, 0] + spectra_ref[0, 1] * spectra_ref[0, 1]
    for f in range(1, bins):
        total = total + (spectra_ref[f, 0] * spectra_ref[f, 0] + spectra_ref[f, 1] * spectra_ref[f, 1])
    amplitude = jnp.sqrt(jnp.maximum(total / bins, 1.0))
    factor = valid_ref[...].astype(jnp.float32) / amplitude
    for k in range(share):
        for part in range(2):
            kept = spectra_ref[half * share + k, part] * factor
            sent = spectra_ref[(1 - half) * share + k, part] * factor
            out_refs[k][part] = kept.astype(jnp.bfloat16)
            out_refs[share + k][part] = sent.astype(jnp.bfloat16)


def whiten(half, spectra, valid):
    bins, _, channels, windows = spectra.shape
    tile = 16 if channels % 16 == 0 else channels
    white = jax.ShapeDtypeStruct((2, channels, windows), jnp.bfloat16)
    return pl.pallas_call(
        whiten_kernel,
        grid_spec=pltpu.PrefetchScalarGridSpec(
            num_scalar_prefetch=1,
            grid=(channels // tile,),
            in_specs=[
                pl.BlockSpec((bins, 2, tile, windows), lambda i, h: (0, 0, i, 0)),
                pl.BlockSpec((tile, windows), lambda i, h: (i, 0)),
            ],
            out_specs=[pl.BlockSpec((2, tile, windows), lambda i, h: (0, i, 0))] * bins,
        ),
        out_shape=[white] * bins,
        compiler_params=pltpu.CompilerParams(vmem_limit_bytes=VMEM_BYTES),
        name="whiten",
    )(half, spectra, valid)


def times(left, right):
    return lax.dot_general(left, right, (((1,), (1,)), ((), ())), preferred_element_type=jnp.float32)


def cross_kernel(pieces, reach, with_out, bin_ref, place_ref, *refs):
    rows = refs[:pieces]
    near = refs[pieces:pieces + reach]
    far = refs[pieces + reach:pieces + 2 * reach]
    out_ref, sent_ref = refs[-2:]
    height = rows[0].shape[1]
    scale = 1.0 / rows[0].shape[2]
    place = place_ref[0]
    left = jnp.concatenate(
        [jnp.concatenate([ref[0] for ref in rows], axis=0), jnp.concatenate([ref[1] for ref in rows], axis=0)], axis=1
    )

    def columns(refs):
        real = jnp.concatenate([ref[0] for ref in refs], axis=0)
        imag = jnp.concatenate([ref[1] for ref in refs], axis=0)
        return jnp.concatenate([real, imag], axis=1), jnp.concatenate([-imag, real], axis=1)

    for part, right in enumerate(columns(far)):
        sent_ref[part] = (times(right, left) * scale).astype(sent_ref.dtype)
    for part, right in enumerate(columns(near)):
        block = times(left, right) * scale
        for label in range(pieces):
            start = pl.multiple_of((place ^ label) * height, 8)
            out_ref[0, part, pl.ds(start, height), :] = block[label * height:(label + 1) * height]


def cross(bin_index, place, rows, near, far, out, bins):
    pieces, reach = len(rows), len(near)
    _, height, windows = rows[0].shape
    group, width = pieces * height, reach * height
    operands = [*rows, *near, *far]
    specs = [pl.BlockSpec(op.shape, lambda i, b, p: (0, 0, 0)) for op in operands]
    aliases = {}
    if out is not None:
        aliases = {2 + len(operands): 0}
        operands.append(out)
        specs.append(pl.BlockSpec(memory_space=pl.ANY))
    flops = 2 * 8 * group * width * windows
    return pl.pallas_call(
        functools.partial(cross_kernel, pieces, reach, out is not None),
        grid_spec=pltpu.PrefetchScalarGridSpec(
            num_scalar_prefetch=2,
            grid=(1,),
            in_specs=specs,
            out_specs=[
                pl.BlockSpec((1, 2, group, width), lambda i, b, p: (b[0], 0, 0, 0)),
                pl.BlockSpec((2, width, group), lambda i, b, p: (0, 0, 0)),
            ],
        ),
        out_shape=[
            jax.ShapeDtypeStruct((bins, 2, group, width), jnp.float32),
            jax.ShapeDtypeStruct((2, width, group), jnp.bfloat16),
        ],
        input_output_aliases=aliases,
        compiler_params=pltpu.CompilerParams(vmem_limit_bytes=VMEM_BYTES),
        cost_estimate=pl.CostEstimate(flops=flops, bytes_accessed=5_000_000, transcendentals=0),
        name="cross",
    )(bin_index, place, *operands)


def place_kernel(pieces, bin_ref, place_ref, came_ref, _, out_ref):
    height = out_ref.shape[2] // pieces
    place = place_ref[0]
    for part in range(2):
        block = came_ref[part].astype(jnp.float32).T
        for label in range(pieces):
            start = pl.multiple_of((place ^ label) * height, 8)
            out_ref[0, part, pl.ds(start, height), :] = block[label * height:(label + 1) * height]


def place_block(bin_index, place, came, out, pieces):
    _, _, group, width = out.shape
    return pl.pallas_call(
        functools.partial(place_kernel, pieces),
        grid_spec=pltpu.PrefetchScalarGridSpec(
            num_scalar_prefetch=2,
            grid=(1,),
            in_specs=[
                pl.BlockSpec((2, width, group), lambda i, b, p: (0, 0, 0)),
                pl.BlockSpec(memory_space=pl.ANY),
            ],
            out_specs=pl.BlockSpec((1, 2, group, width), lambda i, b, p: (b[0], 0, 0, 0)),
        ),
        out_shape=jax.ShapeDtypeStruct(out.shape, jnp.float32),
        input_output_aliases={3: 0},
        compiler_params=pltpu.CompilerParams(vmem_limit_bytes=VMEM_BYTES),
        name="place",
    )(bin_index, place, came, out)


def shards(spectra, valid):
    bins, _, channels, windows = spectra.shape
    share = bins // 2
    count = lax.axis_size("rrow")
    reach = lax.axis_size("rcol") // 2 + 1
    top = count // 2
    me = lax.axis_index("rrow").astype(jnp.int32)
    half = me // top
    white = whiten(half[None], spectra, valid)
    own, other = white[:share], white[share:]
    arrived = [moved_by_xor(piece, "rrow", top) for piece in other]
    out, returned = None, []
    for k in range(share):
        held = {0: own[k], top: arrived[k]}
        bit = top // 2
        while bit:
            for label, piece in list(held.items()):
                held[label ^ bit] = moved_by_xor(piece, "rrow", bit)
            bit //= 2
        near = [own[k]] + [moved_by_shift(own[k], "rcol", -d) for d in range(1, reach)]
        far = [arrived[k]] + [moved_by_shift(arrived[k], "rcol", -d) for d in range(1, reach)]
        rows = [held[label] for label in range(count)]
        out, sent = cross((half * share + k)[None], me[None], rows, near, far, out, bins)
        returned.append(moved_by_xor(sent, "rrow", top))
    for k in range(share):
        out = place_block(((1 - half) * share + k)[None], (me ^ top)[None], returned[k], out, count)
    return out


def solution(mesh):
    in_specs = (P("band", None, ("rcol", "rrow"), None), P(("rcol", "rrow"), None))
    out_specs = P("band", None, "rcol", "rrow")
    return jax.shard_map(shards, mesh=mesh, in_specs=in_specs, out_specs=out_specs, check_vma=False)
```

time: 184 us -> 126 us (0.68)
  waiting for transfers between devices: 136 us -> 41.5 us
  local copies, waits for them, and re-layouts: 1.69 us -> 38.6 us
  starting transfers between devices: 4.66 us -> 36.5 us
  matrix products: 23.1 us -> 0 us
  between operations: 13.6 us -> 0.17 us
  Pallas kernels: 0 us -> 8.08 us
  other arithmetic: 4.69 us -> 0 us
    all_gather x1 -> x0, waiting for transfers between devices: 122 us -> none  [shards(): rows = lax.all_gather(white, 'rrow', axis=2, tiled=True)]
    unnamed x6 -> x70, local copies, waits for them, and re-layouts: 0.01 us -> 33.3 us
    ppermute x2 -> x36, starting transfers between devices: 4.66 us -> 36.5 us  [the longest x24 30.7 us: moved_by_xor(): lax.ppermute(value, axis, [(source, source ^ bits) for source in range(co...]
    ppermute x2 -> x36, waiting for transfers between devices: 14 us -> 41.5 us  [the longest x24 39.5 us: moved_by_xor(): lax.ppermute(value, axis, [(source, source ^ bits) for source in range(co...]
    dot_general x12 -> x0, matrix products: 23.1 us -> none  [the longest x3 7.12 us: shards(): jnp.einsum('fgw,fbw->fgb', rows[:, 0], partner[:, 1], preferred_element_t...]
    pallas_call x0 -> x7, Pallas kernels: none -> 8.08 us  [the longest x3 6.84 us: cross(): pl.pallas_call(functools.partial(cross_kernel, pieces, reach, out is not...]
    pallas_call x0 -> x1, local copies, waits for them, and re-layouts: none -> 5.26 us  [place_block(): pl.pallas_call(functools.partial(place_kernel, pieces), grid_spec=pltpu.P...]
    reduce_sum x1 -> x0, other arithmetic: 2.05 us -> none  [whiten(): jnp.mean(spectra[:, 0] * spectra[:, 0] + spectra[:, 1] * spectra[:, 1], a...]
  transfers between devices with their start and end apart: 3 -> 36, of which waited for: 2 -> 17; matrix products, arithmetic and copies ran while one was open for 9% -> 0% of each run, Pallas kernels for 0% -> 6%
where the time goes in v1:
time: 126 us; the launch traced here: 125 us
  waiting for transfers between devices  41.5 us (33%)
  local copies, waits for them, and re-layouts  38.6 us (31%)
  starting transfers between devices  36.5 us (29%)
  Pallas kernels  8.08 us (6%)
    ppermute x24, waiting for transfers between devices, moved_by_xor(): lax.ppermute(value, axis, [(source, source ^ bits) for source in range(co...  39.5 us
    unnamed x70, local copies, waits for them, and re-layouts  33.3 us
    ppermute x24, starting transfers between devices, moved_by_xor(): lax.ppermute(value, axis, [(source, source ^ bits) for source in range(co...  30.7 us
    pallas_call x3, Pallas kernels, cross(): pl.pallas_call(functools.partial(cross_kernel, pieces, reach, out is not...  6.84 us
    ppermute x12, starting transfers between devices, moved_by_shift(): lax.ppermute(value, axis, [(source, (source + steps) % count) for source...  5.82 us
    pallas_call x1, local copies, waits for them, and re-layouts, place_block(): pl.pallas_call(functools.partial(place_kernel, pieces), grid_spec=pltpu.P...  5.26 us
  transfers between devices with their start and end apart: 36, of which 17 were waited for; matrix products, arithmetic and copies ran while one was open for 0% of the time, Pallas kernels for 6%

profile of v1, /device:TPU:0, one launch (start us, length us, event | category | flops | bytes accessed | tf_op | source)
XLA Modules:
  0.0 124.8 jit_solution(2839023183702263927)
XLA Ops:
  0.0 1.7 %copy-done.3 = f32[6,2,48,1024]{3,2,1,0:T(8,128)S(1)} copy-done((f32[6,2,48,1024]{3,2,1,0:T(8,128)S(1)}, f32[6,2,48,1024]{3,2,1,0:T(8,128)}, u32[]{:S(2)}) %copy-start.3) | copy-done | bytes 2359320
  3.3 4.1 %collective-permute-start.25 = (bf16[2,48,1024]{2,1,0:T(8,128)(2,1)S(1)}, bf16[2,48,1024]{2,1,0:T(8,128)(2,1)S(1)}, u32[]{:S(2)}, u32[]{:S(2)}) collective-permute-start(bf16[2,48,1024]{2,1,0:T(8,128)(2,1)S(1)} %get-tuple-element.22), channel_id=1, source_target_pairs={{0,4},{1,5},{2,6},{3,7},{4,0},{5,1},{6,2},{7,3},{8,12},{9,13},{10,... | collective-permute-start | bytes 589832 | tf_op jit(solution)/shard_map/ppermute | solution.py:15
  7.4 1.6 %collective-permute-start.23 = (bf16[2,48,1024]{2,1,0:T(8,128)(2,1)S(1)}, bf16[2,48,1024]{2,1,0:T(8,128)(2,1)S(1)}, u32[]{:S(2)}, u32[]{:S(2)}) collective-permute-start(bf16[2,48,1024]{2,1,0:T(8,128)(2,1)S(1)} %get-tuple-element.21.refs_0_.refs_8_), channel_id=1, source_target_pairs={{0,2},{1,3},{2,0},{3,1},{4,6},{5,7},{6,4},{7,5},{8,10},{9,11},{10,... | collective-permute-start | bytes 589832 | tf_op jit(solution)/shard_map/ppermute | solution.py:15
  8.9 1.5 %collective-permute-start.22 = (bf16[2,48,1024]{2,1,0:T(8,128)(2,1)S(1)}, bf16[2,48,1024]{2,1,0:T(8,128)(2,1)S(1)}, u32[]{:S(2)}, u32[]{:S(2)}) collective-permute-start(bf16[2,48,1024]{2,1,0:T(8,128)(2,1)S(1)} %get-tuple-element.21.refs_0_.refs_8_), channel_id=1, source_target_pairs={{0,1},{1,0},{2,3},{3,2},{4,5},{5,4},{6,7},{7,6},{8,9},{9,8},{10,11... | collective-permute-start | bytes 589832 | tf_op jit(solution)/shard_map/ppermute | solution.py:15
  10.6 1.4 %collective-permute-start.30 = (bf16[2,48,1024]{2,1,0:T(8,128)(2,1)S(1)}, bf16[2,48,1024]{2,1,0:T(8,128)(2,1)S(1)}, u32[]{:S(2)}, u32[]{:S(2)}) collective-permute-start(bf16[2,48,1024]{2,1,0:T(8,128)(2,1)S(1)} %get-tuple-element.21.refs_0_.refs_8_), channel_id=1, source_target_pairs={{0,16},{8,24},{16,0},{24,8},{1,17},{9,25},{17,1},{25,9},{2,18},{10... | collective-permute-start | bytes 589832 | tf_op jit(solution)/shard_map/ppermute | solution.py:20
  12.6 4.0 %collective-permute-done.25.refs_4_.refs_11_ = bf16[2,48,1024]{2,1,0:T(8,128)(2,1)S(1)} collective-permute-done((bf16[2,48,1024]{2,1,0:T(8,128)(2,1)S(1)}, bf16[2,48,1024]{2,1,0:T(8,128)(2,1)S(1)}, u32[]{:S(2)}, u32[]{:S(2)}) %collective-permute-start.25) | collective-permute-done | bytes 196640 | tf_op jit(solution)/shard_map/ppermute | solution.py:15
  16.8 3.8 %collective-permute-start.12 = (bf16[2,48,1024]{2,1,0:T(8,128)(2,1)S(1)}, bf16[2,48,1024]{2,1,0:T(8,128)(2,1)S(1)}, u32[]{:S(2)}, u32[]{:S(2)}) collective-permute-start(bf16[2,48,1024]{2,1,0:T(8,128)(2,1)S(1)} %get-tuple-element.19.refs_0_.refs_8_), channel_id=1, source_target_pairs={{0,2},{1,3},{2,0},{3,1},{4,6},{5,7},{6,4},{7,5},{8,10},{9,11},{10,... | collective-permute-start | bytes 589832 | tf_op jit(solution)/shard_map/ppermute | solution.py:15
  21.3 1.5 %collective-permute-start.11 = (bf16[2,48,1024]{2,1,0:T(8,128)(2,1)S(1)}, bf16[2,48,1024]{2,1,0:T(8,128)(2,1)S(1)}, u32[]{:S(2)}, u32[]{:S(2)}) collective-permute-start(bf16[2,48,1024]{2,1,0:T(8,128)(2,1)S(1)} %get-tuple-element.19.refs_0_.refs_8_), channel_id=1, source_target_pairs={{0,1},{1,0},{2,3},{3,2},{4,5},{5,4},{6,7},{7,6},{8,9},{9,8},{10,11... | collective-permute-start | bytes 589832 | tf_op jit(solution)/shard_map/ppermute | solution.py:15
  24.4 1.2 collective-permute-start.19
  25.6 2.2 %collective-permute-done.14.refs_4_.refs_11_ = bf16[2,48,1024]{2,1,0:T(8,128)(2,1)S(1)} collective-permute-done((bf16[2,48,1024]{2,1,0:T(8,128)(2,1)S(1)}, bf16[2,48,1024]{2,1,0:T(8,128)(2,1)S(1)}, u32[]{:S(2)}, u32[]{:S(2)}) %collective-permute-start.14) | collective-permute-done | bytes 196640 | tf_op jit(solution)/shard_map/ppermute | solution.py:15
  27.9 1.7 %collective-permute-start.1 = (bf16[2,48,1024]{2,1,0:T(8,128)(2,1)S(1)}, bf16[2,48,1024]{2,1,0:T(8,128)(2,1)S(1)}, u32[]{:S(2)}, u32[]{:S(2)}) collective-permute-start(bf16[2,48,1024]{2,1,0:T(8,128)(2,1)S(1)} %get-tuple-element.17.refs_0_.refs_8_), channel_id=1, source_target_pairs={{0,2},{1,3},{2,0},{3,1},{4,6},{5,7},{6,4},{7,5},{8,10},{9,11},{10,... | collective-permute-start | bytes 589832 | tf_op jit(solution)/shard_map/ppermute | solution.py:15
  31.0 1.8 %collective-permute-done.19.refs_10_ = bf16[2,48,1024]{2,1,0:T(8,128)(2,1)S(1)} collective-permute-done((bf16[2,48,1024]{2,1,0:T(8,128)(2,1)S(1)}, bf16[2,48,1024]{2,1,0:T(8,128)(2,1)S(1)}, u32[]{:S(2)}, u32[]{:S(2)}) %collective-permute-start.19) | collective-permute-done | bytes 196640 | tf_op jit(solution)/shard_map/ppermute | solution.py:20
  33.6 4.5 %collective-permute-done.3.refs_4_.refs_11_ = bf16[2,48,1024]{2,1,0:T(8,128)(2,1)S(1)} collective-permute-done((bf16[2,48,1024]{2,1,0:T(8,128)(2,1)S(1)}, bf16[2,48,1024]{2,1,0:T(8,128)(2,1)S(1)}, u32[]{:S(2)}, u32[]{:S(2)}) %collective-permute-start.3) | collective-permute-done | bytes 196640 | tf_op jit(solution)/shard_map/ppermute | solution.py:15
  39.4 1.5 %collective-permute-start.26 = (bf16[2,48,1024]{2,1,0:T(8,128)(2,1)S(1)}, bf16[2,48,1024]{2,1,0:T(8,128)(2,1)S(1)}, u32[]{:S(2)}, u32[]{:S(2)}) collective-permute-start(bf16[2,48,1024]{2,1,0:T(8,128)(2,1)S(1)} %collective-permute-done.25.refs_4_.refs_11_), channel_id=1, source_target_pairs={{0,1},{1,0},{2,3},{3,2},{4,5},{5,4},{6,7},{7,6},{8,9},{9,8},{10,11... | collective-permute-start | bytes 589832 | tf_op jit(solution)/shard_map/ppermute | solution.py:15
  42.2 2.3 %collective-permute-done.27.refs_6_ = bf16[2,48,1024]{2,1,0:T(8,128)(2,1)S(1)} collective-permute-done((bf16[2,48,1024]{2,1,0:T(8,128)(2,1)S(1)}, bf16[2,48,1024]{2,1,0:T(8,128)(2,1)S(1)}, u32[]{:S(2)}, u32[]{:S(2)}) %collective-permute-start.27) | collective-permute-done | bytes 196640 | tf_op jit(solution)/shard_map/ppermute | solution.py:15
  47.3 2.9 %collective-permute-done.26.refs_5_ = bf16[2,48,1024]{2,1,0:T(8,128)(2,1)S(1)} collective-permute-done((bf16[2,48,1024]{2,1,0:T(8,128)(2,1)S(1)}, bf16[2,48,1024]{2,1,0:T(8,128)(2,1)S(1)}, u32[]{:S(2)}, u32[]{:S(2)}) %collective-permute-start.26) | collective-permute-done | bytes 196640 | tf_op jit(solution)/shard_map/ppermute | solution.py:15
  52.9 3.2 %collective-permute-start.5 = (bf16[2,48,1024]{2,1,0:T(8,128)(2,1)S(1)}, bf16[2,48,1024]{2,1,0:T(8,128)(2,1)S(1)}, u32[]{:S(2)}, u32[]{:S(2)}) collective-permute-start(bf16[2,48,1024]{2,1,0:T(8,128)(2,1)S(1)} %collective-permute-done.3.refs_4_.refs_11_), channel_id=1, source_target_pairs={{0,2},{1,3},{2,0},{3,1},{4,6},{5,7},{6,4},{7,5},{8,10},{9,11},{10,... | collective-permute-start | bytes 589832 | tf_op jit(solution)/shard_map/ppermute | solution.py:15
  57.2 1.6 %collective-permute-start.17 = (bf16[2,48,1024]{2,1,0:T(8,128)(2,1)S(1)}, bf16[2,48,1024]{2,1,0:T(8,128)(2,1)S(1)}, u32[]{:S(2)}, u32[]{:S(2)}) collective-permute-start(bf16[2,48,1024]{2,1,0:T(8,128)(2,1)S(1)} %collective-permute-done.16.refs_6_), channel_id=1, source_target_pairs={{0,1},{1,0},{2,3},{3,2},{4,5},{5,4},{6,7},{7,6},{8,9},{9,8},{10,11... | collective-permute-start | bytes 589832 | tf_op jit(solution)/shard_map/ppermute | solution.py:15
  60.8 1.6 %collective-permute-start.2 = (bf16[2,48,1024]{2,1,0:T(8,128)(2,1)S(1)}, bf16[2,48,1024]{2,1,0:T(8,128)(2,1)}, u32[]{:S(2)}, u32[]{:S(2)}) collective-permute-start(bf16[2,48,1024]{2,1,0:T(8,128)(2,1)S(1)} %collective-permute-done.1.refs_2_), channel_id=1, source_target_pairs={{0,1},{1,0},{2,3},{3,2},{4,5},{5,4},{6,7},{7,6},{8,9},{9,8},{10,11... | collective-permute-start | bytes 589832 | tf_op jit(solution)/shard_map/ppermute | solution.py:15
  64.6 3.5 %collective-permute-done.17.refs_7_ = bf16[2,48,1024]{2,1,0:T(8,128)(2,1)S(1)} collective-permute-done((bf16[2,48,1024]{2,1,0:T(8,128)(2,1)S(1)}, bf16[2,48,1024]{2,1,0:T(8,128)(2,1)S(1)}, u32[]{:S(2)}, u32[]{:S(2)}) %collective-permute-start.17) | collective-permute-done | bytes 196640 | tf_op jit(solution)/shard_map/ppermute | solution.py:15
  80.0 1.9 %cross.3 = (f32[6,2,384,144]{3,2,1,0:T(8,128)S(1)}, bf16[2,144,384]{2,1,0:T(8,128)(2,1)}) custom-call(s32[1]{0:T(128)} %bitcast.6.bin_ref, s32[1]{0:T(128)} %bitcast.3.place_ref, bf16[2,48,1024]{2,1,0:T(8,128)(2,1)S(1)} %copy-done.12, bf16[2,48,1024]{2,1,0:T(8,128)(2,1)S(1)} %copy-done.18, bf16[2,48,1024]{2,1,0:T(8,128)(2,1)S(1)} %copy-done.16, ...), custom_call_target="tpu_custom_call" | custom-call | flops 905969664 | bytes 5000000 | tf_op jit(solution)/shard_map/cross/pallas_call | solution.py:103
  84.7 1.9 %cross.4 = (f32[6,2,384,144]{3,2,1,0:T(8,128)S(1)}, bf16[2,144,384]{2,1,0:T(8,128)(2,1)}) custom-call(s32[1]{0:T(128)} %bitcast.5.bin_ref, s32[1]{0:T(128)} %bitcast.3.place_ref, bf16[2,48,1024]{2,1,0:T(8,128)(2,1)S(1)} %get-tuple-element.19.refs_0_.refs_8_, ...), custom_call_target="tpu_custom_call", output_to_operand_aliasing={{0}: (16, {})} | custom-call | flops 905969664 | bytes 5000000 | tf_op jit(solution)/shard_map/cross/pallas_call | solution.py:103
  86.6 2.5 %collective-permute-start.35 = (bf16[2,144,384]{2,1,0:T(8,128)(2,1)}, bf16[2,144,384]{2,1,0:T(8,128)(2,1)S(1)}, u32[]{:S(2)}, u32[]{:S(2)}) collective-permute-start(bf16[2,144,384]{2,1,0:T(8,128)(2,1)} %get-tuple-element.27), channel_id=1, source_target_pairs={{0,4},{1,5},{2,6},{3,7},{4,0},{5,1},{6,2},{7,3},{8,12},{9,13},{10,... | collective-permute-start | bytes 663560 | tf_op jit(solution)/shard_map/ppermute | solution.py:15
  89.6 3.1 %cross.5 = (f32[6,2,384,144]{3,2,1,0:T(8,128)S(1)}, bf16[2,144,384]{2,1,0:T(8,128)(2,1)S(1)}) custom-call(s32[1]{0:T(128)} %bitcast.2.bin_ref, s32[1]{0:T(128)} %bitcast.3.place_ref, bf16[2,48,1024]{2,1,0:T(8,128)(2,1)S(1)} %get-tuple-element.17.refs_0_.refs_8_, ...), custom_call_target="tpu_custom_call", output_to_operand_aliasing={{0}: (16, {})} | custom-call | flops 905969664 | bytes 5000000 | tf_op jit(solution)/shard_map/cross/pallas_call | solution.py:103
  92.7 2.2 %copy-done = f32[6,2,384,144]{3,2,1,0:T(8,128)} copy-done((f32[6,2,384,144]{3,2,1,0:T(8,128)}, f32[6,2,384,144]{3,2,1,0:T(8,128)S(1)}, u32[]{:S(2)}) %copy-start) | copy-done | bytes 2654232
  94.9 2.4 %collective-permute-start.33 = (bf16[2,144,384]{2,1,0:T(8,128)(2,1)S(1)}, bf16[2,144,384]{2,1,0:T(8,128)(2,1)S(1)}, u32[]{:S(2)}, u32[]{:S(2)}) collective-permute-start(bf16[2,144,384]{2,1,0:T(8,128)(2,1)S(1)} %get-tuple-element.25), channel_id=1, source_target_pairs={{0,4},{1,5},{2,6},{3,7},{4,0},{5,1},{6,2},{7,3},{8,12},{9,13},{10,... | collective-permute-start | bytes 663560 | tf_op jit(solution)/shard_map/ppermute | solution.py:15
  97.3 10.5 %collective-permute-done.35.came_ref = bf16[2,144,384]{2,1,0:T(8,128)(2,1)S(1)} collective-permute-done((bf16[2,144,384]{2,1,0:T(8,128)(2,1)}, bf16[2,144,384]{2,1,0:T(8,128)(2,1)S(1)}, u32[]{:S(2)}, u32[]{:S(2)}) %collective-permute-start.35) | collective-permute-done | bytes 221216 | tf_op jit(solution)/shard_map/ppermute | solution.py:15
  107.8 2.3 %copy-done.1 = f32[6,2,384,144]{3,2,1,0:T(8,128)S(1)} copy-done((f32[6,2,384,144]{3,2,1,0:T(8,128)S(1)}, f32[6,2,384,144]{3,2,1,0:T(8,128)}, u32[]{:S(2)}) %copy-start.1) | copy-done | bytes 2654232
  110.4 2.2 %collective-permute-done.34.came_ref = bf16[2,144,384]{2,1,0:T(8,128)(2,1)S(1)} collective-permute-done((bf16[2,144,384]{2,1,0:T(8,128)(2,1)}, bf16[2,144,384]{2,1,0:T(8,128)(2,1)S(1)}, u32[]{:S(2)}, u32[]{:S(2)}) %collective-permute-start.34) | collective-permute-done | bytes 221216 | tf_op jit(solution)/shard_map/ppermute | solution.py:15
  112.8 4.4 %collective-permute-done.33.came_ref = bf16[2,144,384]{2,1,0:T(8,128)(2,1)S(1)} collective-permute-done((bf16[2,144,384]{2,1,0:T(8,128)(2,1)S(1)}, bf16[2,144,384]{2,1,0:T(8,128)(2,1)S(1)}, u32[]{:S(2)}, u32[]{:S(2)}) %collective-permute-start.33) | collective-permute-done | bytes 221216 | tf_op jit(solution)/shard_map/ppermute | solution.py:15
  117.4 2.2 %copy-done.2 = f32[6,2,384,144]{3,2,1,0:T(8,128)} copy-done((f32[6,2,384,144]{3,2,1,0:T(8,128)}, f32[6,2,384,144]{3,2,1,0:T(8,128)S(1)}, u32[]{:S(2)}) %copy-start.2) | copy-done | bytes 2654232
  119.6 5.3 %copy.8 = f32[6,2,384,144]{2,3,1,0:T(8,128)} copy(f32[6,2,384,144]{3,2,1,0:T(8,128)} %copy-done.2) | data formatting | bytes 5308416 | tf_op jit(solution)/shard_map/place/pallas_call | solution.py:137
  (118 shorter events, 36.3 us)
Async XLA Ops:
  3.3 13.3 %collective-permute-start.25 = (bf16[2,48,1024]{2,1,0:T(8,128)(2,1)S(1)}, bf16[2,48,1024]{2,1,0:T(8,128)(2,1)S(1)}, u32[]{:S(2)}, u32[]{:S(2)}) collective-permute-start(bf16[2,48,1024]{2,1,0:T(8,128)(2,1)S(1)} %get-tuple-element.22), channel_id=1, source_target_pairs={{0,4},{1,5},{2,6},{3,7},{4,0},{5,1},{6,2},{7,3},{8,12},{9,13},{10,... | collective-permute-start | bytes 589832 | tf_op jit(solution)/shard_map/ppermute | solution.py:15
  7.4 9.4 %collective-permute-start.23 = (bf16[2,48,1024]{2,1,0:T(8,128)(2,1)S(1)}, bf16[2,48,1024]{2,1,0:T(8,128)(2,1)S(1)}, u32[]{:S(2)}, u32[]{:S(2)}) collective-permute-start(bf16[2,48,1024]{2,1,0:T(8,128)(2,1)S(1)} %get-tuple-element.21.refs_0_.refs_8_), channel_id=1, source_target_pairs={{0,2},{1,3},{2,0},{3,1},{4,6},{5,7},{6,4},{7,5},{8,10},{9,11},{10,... | collective-permute-start | bytes 589832 | tf_op jit(solution)/shard_map/ppermute | solution.py:15
  8.9 11.6 %collective-permute-start.22 = (bf16[2,48,1024]{2,1,0:T(8,128)(2,1)S(1)}, bf16[2,48,1024]{2,1,0:T(8,128)(2,1)S(1)}, u32[]{:S(2)}, u32[]{:S(2)}) collective-permute-start(bf16[2,48,1024]{2,1,0:T(8,128)(2,1)S(1)} %get-tuple-element.21.refs_0_.refs_8_), channel_id=1, source_target_pairs={{0,1},{1,0},{2,3},{3,2},{4,5},{5,4},{6,7},{7,6},{8,9},{9,8},{10,11... | collective-permute-start | bytes 589832 | tf_op jit(solution)/shard_map/ppermute | solution.py:15
  10.4 12.3 %collective-permute-start.29 = (bf16[2,48,1024]{2,1,0:T(8,128)(2,1)S(1)}, bf16[2,48,1024]{2,1,0:T(8,128)(2,1)S(1)}, u32[]{:S(2)}, u32[]{:S(2)}) collective-permute-start(bf16[2,48,1024]{2,1,0:T(8,128)(2,1)S(1)} %get-tuple-element.21.refs_0_.refs_8_), channel_id=1, source_target_pairs={{0,24},{8,0},{16,8},{24,16},{1,25},{9,1},{17,9},{25,17},{2,26},{10... | collective-permute-start | bytes 589832 | tf_op jit(solution)/shard_map/ppermute | solution.py:20
  10.6 13.2 %collective-permute-start.30 = (bf16[2,48,1024]{2,1,0:T(8,128)(2,1)S(1)}, bf16[2,48,1024]{2,1,0:T(8,128)(2,1)S(1)}, u32[]{:S(2)}, u32[]{:S(2)}) collective-permute-start(bf16[2,48,1024]{2,1,0:T(8,128)(2,1)S(1)} %get-tuple-element.21.refs_0_.refs_8_), channel_id=1, source_target_pairs={{0,16},{8,24},{16,0},{24,8},{1,17},{9,25},{17,1},{25,9},{2,18},{10... | collective-permute-start | bytes 589832 | tf_op jit(solution)/shard_map/ppermute | solution.py:20
  16.6 11.2 %collective-permute-start.14 = (bf16[2,48,1024]{2,1,0:T(8,128)(2,1)S(1)}, bf16[2,48,1024]{2,1,0:T(8,128)(2,1)S(1)}, u32[]{:S(2)}, u32[]{:S(2)}) collective-permute-start(bf16[2,48,1024]{2,1,0:T(8,128)(2,1)S(1)} %get-tuple-element.20), channel_id=1, source_target_pairs={{0,4},{1,5},{2,6},{3,7},{4,0},{5,1},{6,2},{7,3},{8,12},{9,13},{10,... | collective-permute-start | bytes 589832 | tf_op jit(solution)/shard_map/ppermute | solution.py:15
  16.8 11.1 %collective-permute-start.12 = (bf16[2,48,1024]{2,1,0:T(8,128)(2,1)S(1)}, bf16[2,48,1024]{2,1,0:T(8,128)(2,1)S(1)}, u32[]{:S(2)}, u32[]{:S(2)}) collective-permute-start(bf16[2,48,1024]{2,1,0:T(8,128)(2,1)S(1)} %get-tuple-element.19.refs_0_.refs_8_), channel_id=1, source_target_pairs={{0,2},{1,3},{2,0},{3,1},{4,6},{5,7},{6,4},{7,5},{8,10},{9,11},{10,... | collective-permute-start | bytes 589832 | tf_op jit(solution)/shard_map/ppermute | solution.py:15
  21.3 8.3 %collective-permute-start.11 = (bf16[2,48,1024]{2,1,0:T(8,128)(2,1)S(1)}, bf16[2,48,1024]{2,1,0:T(8,128)(2,1)S(1)}, u32[]{:S(2)}, u32[]{:S(2)}) collective-permute-start(bf16[2,48,1024]{2,1,0:T(8,128)(2,1)S(1)} %get-tuple-element.19.refs_0_.refs_8_), channel_id=1, source_target_pairs={{0,1},{1,0},{2,3},{3,2},{4,5},{5,4},{6,7},{7,6},{8,9},{9,8},{10,11... | collective-permute-start | bytes 589832 | tf_op jit(solution)/shard_map/ppermute | solution.py:15
  24.4 8.4 %collective-permute-start.19 = (bf16[2,48,1024]{2,1,0:T(8,128)(2,1)S(1)}, bf16[2,48,1024]{2,1,0:T(8,128)(2,1)S(1)}, u32[]{:S(2)}, u32[]{:S(2)}) collective-permute-start(bf16[2,48,1024]{2,1,0:T(8,128)(2,1)S(1)} %get-tuple-element.19.refs_0_.refs_8_), channel_id=1, source_target_pairs={{0,16},{8,24},{16,0},{24,8},{1,17},{9,25},{17,1},{25,9},{2,18},{10... | collective-permute-start | bytes 589832 | tf_op jit(solution)/shard_map/ppermute | solution.py:20
  27.8 10.3 %collective-permute-start.3 = (bf16[2,48,1024]{2,1,0:T(8,128)(2,1)S(1)}, bf16[2,48,1024]{2,1,0:T(8,128)(2,1)S(1)}, u32[]{:S(2)}, u32[]{:S(2)}) collective-permute-start(bf16[2,48,1024]{2,1,0:T(8,128)(2,1)S(1)} %get-tuple-element.18), channel_id=1, source_target_pairs={{0,4},{1,5},{2,6},{3,7},{4,0},{5,1},{6,2},{7,3},{8,12},{9,13},{10,... | collective-permute-start | bytes 589832 | tf_op jit(solution)/shard_map/ppermute | solution.py:15
  27.9 10.3 %collective-permute-start.1 = (bf16[2,48,1024]{2,1,0:T(8,128)(2,1)S(1)}, bf16[2,48,1024]{2,1,0:T(8,128)(2,1)S(1)}, u32[]{:S(2)}, u32[]{:S(2)}) collective-permute-start(bf16[2,48,1024]{2,1,0:T(8,128)(2,1)S(1)} %get-tuple-element.17.refs_0_.refs_8_), channel_id=1, source_target_pairs={{0,2},{1,3},{2,0},{3,1},{4,6},{5,7},{6,4},{7,5},{8,10},{9,11},{10,... | collective-permute-start | bytes 589832 | tf_op jit(solution)/shard_map/ppermute | solution.py:15
  29.6 9.8 %collective-permute-start = (bf16[2,48,1024]{2,1,0:T(8,128)(2,1)S(1)}, bf16[2,48,1024]{2,1,0:T(8,128)(2,1)S(1)}, u32[]{:S(2)}, u32[]{:S(2)}) collective-permute-start(bf16[2,48,1024]{2,1,0:T(8,128)(2,1)S(1)} %get-tuple-element.17.refs_0_.refs_8_), channel_id=1, source_target_pairs={{0,1},{1,0},{2,3},{3,2},{4,5},{5,4},{6,7},{7,6},{8,9},{9,8},{10,11... | collective-permute-start | bytes 589832 | tf_op jit(solution)/shard_map/ppermute | solution.py:15
  30.8 10.1 %collective-permute-start.7 = (bf16[2,48,1024]{2,1,0:T(8,128)(2,1)S(1)}, bf16[2,48,1024]{2,1,0:T(8,128)(2,1)S(1)}, u32[]{:S(2)}, u32[]{:S(2)}) collective-permute-start(bf16[2,48,1024]{2,1,0:T(8,128)(2,1)S(1)} %get-tuple-element.17.refs_0_.refs_8_), channel_id=1, source_target_pairs={{0,24},{8,0},{16,8},{24,16},{1,25},{9,1},{17,9},{25,17},{2,26},{10... | collective-permute-start | bytes 589832 | tf_op jit(solution)/shard_map/ppermute | solution.py:20
  32.8 8.1 %collective-permute-start.8 = (bf16[2,48,1024]{2,1,0:T(8,128)(2,1)S(1)}, bf16[2,48,1024]{2,1,0:T(8,128)(2,1)S(1)}, u32[]{:S(2)}, u32[]{:S(2)}) collective-permute-start(bf16[2,48,1024]{2,1,0:T(8,128)(2,1)S(1)} %get-tuple-element.17.refs_0_.refs_8_), channel_id=1, source_target_pairs={{0,16},{8,24},{16,0},{24,8},{1,17},{9,25},{17,1},{25,9},{2,18},{10... | collective-permute-start | bytes 589832 | tf_op jit(solution)/shard_map/ppermute | solution.py:20
  38.2 7.8 %collective-permute-start.24 = (bf16[2,48,1024]{2,1,0:T(8,128)(2,1)S(1)}, bf16[2,48,1024]{2,1,0:T(8,128)(2,1)S(1)}, u32[]{:S(2)}, u32[]{:S(2)}) collective-permute-start(bf16[2,48,1024]{2,1,0:T(8,128)(2,1)S(1)} %collective-permute-done.23.refs_2_), channel_id=1, source_target_pairs={{0,1},{1,0},{2,3},{3,2},{4,5},{5,4},{6,7},{7,6},{8,9},{9,8},{10,11... | collective-permute-start | bytes 589832 | tf_op jit(solution)/shard_map/ppermute | solution.py:15
  39.4 10.7 %collective-permute-start.26 = (bf16[2,48,1024]{2,1,0:T(8,128)(2,1)S(1)}, bf16[2,48,1024]{2,1,0:T(8,128)(2,1)S(1)}, u32[]{:S(2)}, u32[]{:S(2)}) collective-permute-start(bf16[2,48,1024]{2,1,0:T(8,128)(2,1)S(1)} %collective-permute-done.25.refs_4_.refs_11_), channel_id=1, source_target_pairs={{0,1},{1,0},{2,3},{3,2},{4,5},{5,4},{6,7},{7,6},{8,9},{9,8},{10,11... | collective-permute-start | bytes 589832 | tf_op jit(solution)/shard_map/ppermute | solution.py:15
  40.9 9.9 %collective-permute-start.31 = (bf16[2,48,1024]{2,1,0:T(8,128)(2,1)S(1)}, bf16[2,48,1024]{2,1,0:T(8,128)(2,1)S(1)}, u32[]{:S(2)}, u32[]{:S(2)}) collective-permute-start(bf16[2,48,1024]{2,1,0:T(8,128)(2,1)S(1)} %collective-permute-done.25.refs_4_.refs_11_), channel_id=1, source_target_pairs={{0,24},{8,0},{16,8},{24,16},{1,25},{9,1},{17,9},{25,17},{2,26},{10... | collective-permute-start | bytes 589832 | tf_op jit(solution)/shard_map/ppermute | solution.py:20
  40.9 10.6 %collective-permute-start.32 = (bf16[2,48,1024]{2,1,0:T(8,128)(2,1)S(1)}, bf16[2,48,1024]{2,1,0:T(8,128)(2,1)S(1)}, u32[]{:S(2)}, u32[]{:S(2)}) collective-permute-start(bf16[2,48,1024]{2,1,0:T(8,128)(2,1)S(1)} %collective-permute-done.25.refs_4_.refs_11_), channel_id=1, source_target_pairs={{0,16},{8,24},{16,0},{24,8},{1,17},{9,25},{17,1},{25,9},{2,18},{10... | collective-permute-start | bytes 589832 | tf_op jit(solution)/shard_map/ppermute | solution.py:20
  44.6 8.4 %collective-permute-start.16 = (bf16[2,48,1024]{2,1,0:T(8,128)(2,1)S(1)}, bf16[2,48,1024]{2,1,0:T(8,128)(2,1)S(1)}, u32[]{:S(2)}, u32[]{:S(2)}) collective-permute-start(bf16[2,48,1024]{2,1,0:T(8,128)(2,1)S(1)} %collective-permute-done.14.refs_4_.refs_11_), channel_id=1, source_target_pairs={{0,2},{1,3},{2,0},{3,1},{4,6},{5,7},{6,4},{7,5},{8,10},{9,11},{10,... | collective-permute-start | bytes 589832 | tf_op jit(solution)/shard_map/ppermute | solution.py:15
  46.7 9.4 %collective-permute-start.13 = (bf16[2,48,1024]{2,1,0:T(8,128)(2,1)S(1)}, bf16[2,48,1024]{2,1,0:T(8,128)(2,1)S(1)}, u32[]{:S(2)}, u32[]{:S(2)}) collective-permute-start(bf16[2,48,1024]{2,1,0:T(8,128)(2,1)S(1)} %collective-permute-done.12.refs_2_), channel_id=1, source_target_pairs={{0,1},{1,0},{2,3},{3,2},{4,5},{5,4},{6,7},{7,6},{8,9},{9,8},{10,11... | collective-permute-start | bytes 589832 | tf_op jit(solution)/shard_map/ppermute | solution.py:15
  52.2 7.9 %collective-permute-start.21 = (bf16[2,48,1024]{2,1,0:T(8,128)(2,1)S(1)}, bf16[2,48,1024]{2,1,0:T(8,128)(2,1)S(1)}, u32[]{:S(2)}, u32[]{:S(2)}) collective-permute-start(bf16[2,48,1024]{2,1,0:T(8,128)(2,1)S(1)} %collective-permute-done.14.refs_4_.refs_11_), channel_id=1, source_target_pairs={{0,16},{8,24},{16,0},{24,8},{1,17},{9,25},{17,1},{25,9},{2,18},{10... | collective-permute-start | bytes 589832 | tf_op jit(solution)/shard_map/ppermute | solution.py:20
  52.9 9.4 %collective-permute-start.5 = (bf16[2,48,1024]{2,1,0:T(8,128)(2,1)S(1)}, bf16[2,48,1024]{2,1,0:T(8,128)(2,1)S(1)}, u32[]{:S(2)}, u32[]{:S(2)}) collective-permute-start(bf16[2,48,1024]{2,1,0:T(8,128)(2,1)S(1)} %collective-permute-done.3.refs_4_.refs_11_), channel_id=1, source_target_pairs={{0,2},{1,3},{2,0},{3,1},{4,6},{5,7},{6,4},{7,5},{8,10},{9,11},{10,... | collective-permute-start | bytes 589832 | tf_op jit(solution)/shard_map/ppermute | solution.py:15
  56.1 7.8 %collective-permute-start.28 = (bf16[2,48,1024]{2,1,0:T(8,128)(2,1)S(1)}, bf16[2,48,1024]{2,1,0:T(8,128)(2,1)S(1)}, u32[]{:S(2)}, u32[]{:S(2)}) collective-permute-start(bf16[2,48,1024]{2,1,0:T(8,128)(2,1)S(1)} %collective-permute-done.27.refs_6_), channel_id=1, source_target_pairs={{0,1},{1,0},{2,3},{3,2},{4,5},{5,4},{6,7},{7,6},{8,9},{9,8},{10,11... | collective-permute-start | bytes 589832 | tf_op jit(solution)/shard_map/ppermute | solution.py:15
  57.2 10.9 %collective-permute-start.17 = (bf16[2,48,1024]{2,1,0:T(8,128)(2,1)S(1)}, bf16[2,48,1024]{2,1,0:T(8,128)(2,1)S(1)}, u32[]{:S(2)}, u32[]{:S(2)}) collective-permute-start(bf16[2,48,1024]{2,1,0:T(8,128)(2,1)S(1)} %collective-permute-done.16.refs_6_), channel_id=1, source_target_pairs={{0,1},{1,0},{2,3},{3,2},{4,5},{5,4},{6,7},{7,6},{8,9},{9,8},{10,11... | collective-permute-start | bytes 589832 | tf_op jit(solution)/shard_map/ppermute | solution.py:15
  59.5 27.1 %collective-permute-start.10 = (bf16[2,48,1024]{2,1,0:T(8,128)(2,1)S(1)}, bf16[2,48,1024]{2,1,0:T(8,128)(2,1)S(1)}, u32[]{:S(2)}, u32[]{:S(2)}) collective-permute-start(bf16[2,48,1024]{2,1,0:T(8,128)(2,1)S(1)} %collective-permute-done.3.refs_4_.refs_11_), channel_id=1, source_target_pairs={{0,16},{8,24},{16,0},{24,8},{1,17},{9,25},{17,1},{25,9},{2,18},{10... | collective-permute-start | bytes 589832 | tf_op jit(solution)/shard_map/ppermute | solution.py:20
  60.8 28.3 %collective-permute-start.2 = (bf16[2,48,1024]{2,1,0:T(8,128)(2,1)S(1)}, bf16[2,48,1024]{2,1,0:T(8,128)(2,1)}, u32[]{:S(2)}, u32[]{:S(2)}) collective-permute-start(bf16[2,48,1024]{2,1,0:T(8,128)(2,1)S(1)} %collective-permute-done.1.refs_2_), channel_id=1, source_target_pairs={{0,1},{1,0},{2,3},{3,2},{4,5},{5,4},{6,7},{7,6},{8,9},{9,8},{10,11... | collective-permute-start | bytes 589832 | tf_op jit(solution)/shard_map/ppermute | solution.py:15
  62.4 27.2 %collective-permute-start.4 = (bf16[2,48,1024]{2,1,0:T(8,128)(2,1)S(1)}, bf16[2,48,1024]{2,1,0:T(8,128)(2,1)}, u32[]{:S(2)}, u32[]{:S(2)}) collective-permute-start(bf16[2,48,1024]{2,1,0:T(8,128)(2,1)S(1)} %collective-permute-done.3.refs_4_.refs_11_), channel_id=1, source_target_pairs={{0,1},{1,0},{2,3},{3,2},{4,5},{5,4},{6,7},{7,6},{8,9},{9,8},{10,11... | collective-permute-start | bytes 589832 | tf_op jit(solution)/shard_map/ppermute | solution.py:15
  64.6 25.0 %collective-permute-start.9 = (bf16[2,48,1024]{2,1,0:T(8,128)(2,1)S(1)}, bf16[2,48,1024]{2,1,0:T(8,128)(2,1)}, u32[]{:S(2)}, u32[]{:S(2)}) collective-permute-start(bf16[2,48,1024]{2,1,0:T(8,128)(2,1)S(1)} %collective-permute-done.3.refs_4_.refs_11_), channel_id=1, source_target_pairs={{0,24},{8,0},{16,8},{24,16},{1,25},{9,1},{17,9},{25,17},{2,26},{10... | collective-permute-start | bytes 589832 | tf_op jit(solution)/shard_map/ppermute | solution.py:20
  68.8 20.8 %collective-permute-start.6 = (bf16[2,48,1024]{2,1,0:T(8,128)(2,1)S(1)}, bf16[2,48,1024]{2,1,0:T(8,128)(2,1)}, u32[]{:S(2)}, u32[]{:S(2)}) collective-permute-start(bf16[2,48,1024]{2,1,0:T(8,128)(2,1)S(1)} %collective-permute-done.5.refs_6_), channel_id=1, source_target_pairs={{0,1},{1,0},{2,3},{3,2},{4,5},{5,4},{6,7},{7,6},{8,9},{9,8},{10,11... | collective-permute-start | bytes 589832 | tf_op jit(solution)/shard_map/ppermute | solution.py:15
  86.6 21.2 %collective-permute-start.35 = (bf16[2,144,384]{2,1,0:T(8,128)(2,1)}, bf16[2,144,384]{2,1,0:T(8,128)(2,1)S(1)}, u32[]{:S(2)}, u32[]{:S(2)}) collective-permute-start(bf16[2,144,384]{2,1,0:T(8,128)(2,1)} %get-tuple-element.27), channel_id=1, source_target_pairs={{0,4},{1,5},{2,6},{3,7},{4,0},{5,1},{6,2},{7,3},{8,12},{9,13},{10,... | collective-permute-start | bytes 663560 | tf_op jit(solution)/shard_map/ppermute | solution.py:15
  89.1 23.5 %collective-permute-start.34 = (bf16[2,144,384]{2,1,0:T(8,128)(2,1)}, bf16[2,144,384]{2,1,0:T(8,128)(2,1)S(1)}, u32[]{:S(2)}, u32[]{:S(2)}) collective-permute-start(bf16[2,144,384]{2,1,0:T(8,128)(2,1)} %get-tuple-element.26), channel_id=1, source_target_pairs={{0,4},{1,5},{2,6},{3,7},{4,0},{5,1},{6,2},{7,3},{8,12},{9,13},{10,... | collective-permute-start | bytes 663560 | tf_op jit(solution)/shard_map/ppermute | solution.py:15
  94.9 22.4 %collective-permute-start.33 = (bf16[2,144,384]{2,1,0:T(8,128)(2,1)S(1)}, bf16[2,144,384]{2,1,0:T(8,128)(2,1)S(1)}, u32[]{:S(2)}, u32[]{:S(2)}) collective-permute-start(bf16[2,144,384]{2,1,0:T(8,128)(2,1)S(1)} %get-tuple-element.25), channel_id=1, source_target_pairs={{0,4},{1,5},{2,6},{3,7},{4,0},{5,1},{6,2},{7,3},{8,12},{9,13},{10,... | collective-permute-start | bytes 663560 | tf_op jit(solution)/shard_map/ppermute | solution.py:15
  (39 other events, 60.9 us)

commit v2 on v0

v2 whole, which is shorter than its diff:
```python
import functools

import jax
import jax.numpy as jnp
from jax import lax
from jax.experimental import pallas as pl
from jax.experimental.pallas import tpu as pltpu
from jax.sharding import PartitionSpec as P

COVER = 1
VMEM_BYTES = 64 * 1024 * 1024 - 65536


def moved_by_xor(value, axis, bits):
    count = lax.axis_size(axis)
    return lax.ppermute(value, axis, [(source, source ^ bits) for source in range(count)])


def moved_by_shift(value, axis, steps):
    count = lax.axis_size(axis)
    return lax.ppermute(value, axis, [(source, (source + steps) % count) for source in range(count)])


def after(value, *earlier):
    return lax.optimization_barrier((value, *earlier))[0]


def fence_kernel(token_ref, out_ref):
    out_ref[0] = token_ref[0] + 1


def fence(token, *earlier):
    return pl.pallas_call(
        fence_kernel,
        in_specs=[pl.BlockSpec(memory_space=pltpu.SMEM)],
        out_specs=pl.BlockSpec(memory_space=pltpu.SMEM),
        out_shape=jax.ShapeDtypeStruct((1,), jnp.int32),
        cost_estimate=pl.CostEstimate(flops=COVER, bytes_accessed=1, transcendentals=0),
        name="fence",
    )(after(token, *earlier))


def whiten_kernel(splits, place_ref, spectra_ref, valid_ref, all_ref, front_ref, back_ref, front_other, back_other):
    bins = spectra_ref.shape[0]
    total = spectra_ref[0, 0] * spectra_ref[0, 0] + spectra_ref[0, 1] * spectra_ref[0, 1]
    for f in range(1, bins):
        total = total + (spectra_ref[f, 0] * spectra_ref[f, 0] + spectra_ref[f, 1] * spectra_ref[f, 1])
    amplitude = jnp.sqrt(jnp.maximum(total / bins, 1.0))
    factor = valid_ref[...].astype(jnp.float32) / amplitude
    for k, split in enumerate(splits):
        side = (place_ref[0] // split) % 2
        for part in range(2):
            kept = (spectra_ref[2 * k + side, part] * factor).astype(jnp.bfloat16)
            sent = (spectra_ref[2 * k + 1 - side, part] * factor).astype(jnp.bfloat16)
            all_ref[k, part] = kept
            if k < len(splits) - 1:
                front_ref[k, part] = kept
                front_other[k, part] = sent
            else:
                back_ref[0, part] = kept
                back_other[0, part] = sent


def whiten(splits, place, spectra, valid):
    bins, _, channels, windows = spectra.shape
    tile = windows // 2 if windows % 256 == 0 else windows
    count = len(splits)
    sizes = [count, count - 1, 1, count - 1, 1]
    return pl.pallas_call(
        functools.partial(whiten_kernel, splits),
        grid_spec=pltpu.PrefetchScalarGridSpec(
            num_scalar_prefetch=1,
            grid=(windows // tile,),
            in_specs=[
                pl.BlockSpec((bins, 2, channels, tile), lambda i, p: (0, 0, 0, i)),
                pl.BlockSpec((channels, tile), lambda i, p: (0, i)),
            ],
            out_specs=[pl.BlockSpec((n, 2, channels, tile), lambda i, p: (0, 0, 0, i)) for n in sizes],
        ),
        out_shape=[jax.ShapeDtypeStruct((n, 2, channels, windows), jnp.bfloat16) for n in sizes],
        compiler_params=pltpu.CompilerParams(vmem_limit_bytes=VMEM_BYTES),
        cost_estimate=pl.CostEstimate(flops=1, bytes_accessed=1, transcendentals=0),
        name="whiten",
    )(place, spectra, valid)


def cross_kernel(pieces, reach, slots, before, scalars, *refs):
    slabs = [ref.at[slot] for ref, slot in zip(refs, slots)]
    rows, near, far = slabs[:pieces], slabs[pieces:pieces + reach], slabs[pieces + reach:pieces + 2 * reach]
    out_ref, sent_ref, left_ref, real_ref, imag_ref, mine_ref, theirs_ref, old_ref, new_ref, sems = refs[-10:]
    _, height, windows = rows[0].shape
    width = reach * height
    place, mine_bin, old_bin = scalars[0], scalars[1], scalars[2]
    moves = []

    def move(source, target):
        copy = pltpu.make_async_copy(source, target, sems.at[len(moves)])
        copy.start()
        moves.append(copy)
        return copy

    for side, group in enumerate((near, far)):
        for d, ref in enumerate(group):
            at = pl.ds(side * width + d * height, height)
            move(ref.at[0], real_ref.at[at])
            move(ref.at[1], imag_ref.at[at])
    for label, ref in enumerate(rows):
        start = pl.multiple_of((place ^ label) * height, 16)
        for part in range(2):
            move(ref.at[part], left_ref.at[part, pl.ds(start, height)])
    arriving = list(moves)
    if before:
        came = move(refs[pieces + 2 * reach], old_ref)
        came.wait()
        new_ref[...] = old_ref[...].astype(jnp.float32)
        placed = move(new_ref, out_ref.at[old_bin])
    for copy in arriving:
        copy.wait()

    def times(right, left):
        return lax.dot_general(right, left, (((1,), (1,)), ((), ())), preferred_element_type=jnp.float32)

    real, imag, rows_real, rows_imag = real_ref[...], imag_ref[...], left_ref[0], left_ref[1]
    scale = 1.0 / windows
    for part in range(2):
        if part == 0:
            sums = times(real, rows_real) + times(imag, rows_imag)
        else:
            sums = times(real, rows_imag) - times(imag, rows_real)
        sums = sums * scale
        mine_ref[part] = sums[:width]
        theirs_ref[part] = sums[width:].astype(theirs_ref.dtype)
    ending = [move(theirs_ref, sent_ref), move(mine_ref, out_ref.at[mine_bin])]
    if before:
        ending.append(placed)
    for copy in ending:
        copy.wait()


def cross(scalars, rows, near, far, came, out, bins):
    pieces, reach = len(rows), len(near)
    *_, height, windows = rows[0][0].shape
    group, width = pieces * height, reach * height
    operands = [array for array, _ in (*rows, *near, *far)]
    slots = [slot for _, slot in (*rows, *near, *far)]
    aliases = {}
    if came is not None:
        operands.append(came)
    if out is not None:
        operands.append(out)
        aliases = {len(operands): 0}
    return pl.pallas_call(
        functools.partial(cross_kernel, pieces, reach, slots, came is not None),
        grid_spec=pltpu.PrefetchScalarGridSpec(
            num_scalar_prefetch=1,
            grid=(1,),
            in_specs=[pl.BlockSpec(memory_space=pl.ANY)] * len(operands),
            out_specs=[pl.BlockSpec(memory_space=pl.ANY)] * 2,
            scratch_shapes=[
                pltpu.VMEM((2, group, windows), jnp.bfloat16),
                pltpu.VMEM((2 * width, windows), jnp.bfloat16),
                pltpu.VMEM((2 * width, windows), jnp.bfloat16),
                pltpu.VMEM((2, width, group), jnp.float32),
                pltpu.VMEM((2, width, group), jnp.bfloat16),
                pltpu.VMEM((2, width, group), jnp.bfloat16),
                pltpu.VMEM((2, width, group), jnp.float32),
                pltpu.SemaphoreType.DMA((2 * (pieces + 2 * reach) + 4,)),
            ],
        ),
        out_shape=[
            jax.ShapeDtypeStruct((bins, 2, width, group), jnp.float32),
            jax.ShapeDtypeStruct((2, width, group), jnp.bfloat16),
        ],
        input_output_aliases=aliases,
        compiler_params=pltpu.CompilerParams(vmem_limit_bytes=VMEM_BYTES),
        cost_estimate=pl.CostEstimate(flops=COVER, bytes_accessed=1, transcendentals=0),
        name="cross",
    )(scalars, *operands)


def place_kernel(bin_ref, came_ref, _, out_ref):
    out_ref[0] = came_ref[...].astype(jnp.float32)


def place_block(bin_index, came, out):
    return pl.pallas_call(
        place_kernel,
        grid_spec=pltpu.PrefetchScalarGridSpec(
            num_scalar_prefetch=1,
            grid=(1,),
            in_specs=[
                pl.BlockSpec(came.shape, lambda i, b: (0, 0, 0)),
                pl.BlockSpec(memory_space=pl.ANY),
            ],
            out_specs=pl.BlockSpec((1, *out.shape[1:]), lambda i, b: (b[0], 0, 0, 0)),
        ),
        out_shape=jax.ShapeDtypeStruct(out.shape, jnp.float32),
        input_output_aliases={2: 0},
        compiler_params=pltpu.CompilerParams(vmem_limit_bytes=VMEM_BYTES),
        name="place",
    )(bin_index, came, out)


def shards(spectra, valid):
    bins = spectra.shape[0]
    reach = lax.axis_size("rcol") // 2 + 1
    count = lax.axis_size("rrow")
    me = lax.axis_index("rrow").astype(jnp.int32)
    splits = (4, 4, 2)

    def flip(value, bits, *gates):
        return moved_by_xor(after(value, *gates) if gates else value, "rrow", bits)

    def shift(value, d, *gates):
        return moved_by_shift(after(value, *gates) if gates else value, "rcol", -d)

    def bin_of(k, side):
        return 2 * k + (me // splits[k] + side) % 2

    def rows_of(k, slot, mine_z, mine_d, got, got_x, got_z, got_d):
        split = splits[k]
        other = 6 - split
        held = {
            0: (own, k), 1: (own_x, k), other: (mine_z, slot), other | 1: (mine_d, slot),
            split: (got, slot), split | 1: (got_x, slot), split | other: (got_z, slot), split | other | 1: (got_d, slot),
        }
        return [held[label] for label in range(count)]

    def scalars(k, old):
        return jnp.stack([me, bin_of(k, 0), bin_of(old, 1)])

    own, front, back, front_other, back_other = whiten(splits, me[None], spectra, valid)
    steps = range(1, reach)
    got = flip(front_other, 4)
    own_x = flip(own, 1)
    front_z = flip(front, 2)
    own_y = [own] + [shift(own, d) for d in steps]
    front_d = flip(front_z, 1)
    last = flip(back_other, 2, front_z)
    back_z = flip(back, 4, got)
    got_z = flip(got, 2, last)
    got_x = flip(got, 1, own_x)
    got_y = [got] + [shift(got, d, own_y[d]) for d in steps]
    got_d = flip(got_z, 1, front_d)
    last_z = flip(last, 4, back_z)
    back_d = flip(back_z, 1, got_x)
    last_x = flip(last, 1, got_d)
    last_y = [last] + [shift(last, d, got_y[d]) for d in steps]

    out, sent, came = None, None, []
    for k in range(2):
        rows = rows_of(k, k, front_z, front_d, got, got_x, got_z, got_d)
        near, far = [(x, k) for x in own_y], [(x, k) for x in got_y]
        out, sent = cross(scalars(k, 0), rows, near, far, None, out, bins)
        came.append(flip(sent, 4))
    last_d = flip(last_z, 1, back_d)
    rows = rows_of(2, 0, back_z, back_d, last, last_x, last_z, last_d)
    out, sent = cross(scalars(2, 0), rows, [(x, 2) for x in own_y], [(x, 0) for x in last_y], None, out, bins)
    came.append(flip(sent, 2))
    for k in range(3):
        out = place_block(bin_of(k, 1)[None], after(came[k], sent), out)
    return jnp.swapaxes(out, 2, 3)


def solution(mesh):
    in_specs = (P("band", None, ("rcol", "rrow"), None), P(("rcol", "rrow"), None))
    out_specs = P("band", None, "rcol", "rrow")
    return jax.shard_map(shards, mesh=mesh, in_specs=in_specs, out_specs=out_specs, check_vma=False)
```

time: 184 us -> 89.2 us (0.48)
  waiting for transfers between devices: 136 us -> 36.1 us
  matrix products: 23.1 us -> 0 us
  Pallas kernels: 0 us -> 22.9 us
  starting transfers between devices: 4.66 us -> 27.5 us
  between operations: 13.6 us -> 0.11 us
  other arithmetic: 4.69 us -> 1.24 us
    all_gather x1 -> x0, waiting for transfers between devices: 122 us -> none  [shards(): rows = lax.all_gather(white, 'rrow', axis=2, tiled=True)]
    dot_general x12 -> x0, matrix products: 23.1 us -> none  [the longest x3 7.12 us: shards(): jnp.einsum('fgw,fbw->fgb', rows[:, 0], partner[:, 1], preferred_element_t...]
    pallas_call x0 -> x7, Pallas kernels: none -> 22.9 us  [the longest x3 15 us: cross(): pl.pallas_call(functools.partial(cross_kernel, pieces, reach, slots, came...]
    ppermute x2 -> x22, starting transfers between devices: 4.66 us -> 27.5 us  [the longest x16 22.8 us: moved_by_xor(): lax.ppermute(value, axis, [(source, source ^ bits) for source in range(co...]
    ppermute x2 -> x22, waiting for transfers between devices: 14 us -> 36.1 us  [the longest x16 36.1 us: moved_by_xor(): lax.ppermute(value, axis, [(source, source ^ bits) for source in range(co...]
    reduce_sum x1 -> x0, other arithmetic: 2.05 us -> none  [whiten(): jnp.mean(spectra[:, 0] * spectra[:, 0] + spectra[:, 1] * spectra[:, 1], a...]
  transfers between devices with their start and end apart: 3 -> 22, of which waited for: 2 -> 8; matrix products, arithmetic and copies ran while one was open for 9% -> 1% of each run, Pallas kernels for 0% -> 21%
where the time goes in v2:
time: 89.2 us; the launch traced here: 88.7 us
  waiting for transfers between devices  36.1 us (40%)
  starting transfers between devices  27.5 us (31%)
  Pallas kernels  22.9 us (26%)
  other arithmetic  1.24 us (1%)
  local copies, waits for them, and re-layouts  0.93 us (1%)
    ppermute x16, waiting for transfers between devices, moved_by_xor(): lax.ppermute(value, axis, [(source, source ^ bits) for source in range(co...  36.1 us
    ppermute x16, starting transfers between devices, moved_by_xor(): lax.ppermute(value, axis, [(source, source ^ bits) for source in range(co...  22.8 us
    pallas_call x3, Pallas kernels, cross(): pl.pallas_call(functools.partial(cross_kernel, pieces, reach, slots, came...  15 us
    pallas_call x3, Pallas kernels, place_block(): pl.pallas_call(place_kernel, grid_spec=pltpu.PrefetchScalarGridSpec(num_s...  5.18 us
    ppermute x6, starting transfers between devices, moved_by_shift(): lax.ppermute(value, axis, [(source, (source + steps) % count) for source...  4.62 us
    pallas_call x1, Pallas kernels, whiten(): pl.pallas_call(functools.partial(whiten_kernel, splits), grid_spec=pltpu....  2.72 us
  transfers between devices with their start and end apart: 22, of which 8 were waited for; matrix products, arithmetic and copies ran while one was open for 1% of the time, Pallas kernels for 21%

profile of v2, /device:TPU:0, one launch (start us, length us, event | category | flops | bytes accessed | tf_op | source)
XLA Modules:
  0.0 88.7 jit_solution(9782958493747365575)
XLA Ops:
  0.0 2.7 %whiten.1 = (bf16[3,2,48,1024]{3,2,1,0:T(8,128)(2,1)}, bf16[2,2,48,1024]{3,2,1,0:T(8,128)(2,1)}, bf16[1,2,48,1024]{3,2,1,0:T(8,128)(2,1)}, bf16[2,2,48,1024]{3,2,1,0:T(8,128)(2,1)}, bf16[1,2,48,1024]{3,2,1,0:T(8,128)(2,1)}) custom-call(s32[1]{0:T(128)} %bitcast.1.place_ref, f32[6,2,48,1024]{3,2,1,0:T(8,128)} %spectra_ref.1, s32[48,1024]{1,0:T(8,128)} %valid_ref.1), custom_call_target="tpu_custom_call" | custom-call | flops 1 | bytes 1 | tf_op jit(solution)/shard_map/whiten/pallas_call | solution.py:69
  2.7 3.1 %collective-permute-start.1 = (bf16[2,2,48,1024]{3,2,1,0:T(8,128)(2,1)}, bf16[2,2,48,1024]{3,2,1,0:T(8,128)(2,1)S(1)}, u32[]{:S(2)}, u32[]{:S(2)}) collective-permute-start(bf16[2,2,48,1024]{3,2,1,0:T(8,128)(2,1)} %get-tuple-element.34), channel_id=1, source_target_pairs={{0,2},{1,3},{2,0},{3,1},{4,6},{5,7},{6,4},{7,5},{8,10},{9,11},{10,... | collective-permute-start | bytes 1179656 | tf_op jit(solution)/shard_map/ppermute | solution.py:16
  5.8 2.6 %collective-permute-start.3 = (bf16[2,2,48,1024]{3,2,1,0:T(8,128)(2,1)}, bf16[2,2,48,1024]{3,2,1,0:T(8,128)(2,1)S(1)}, u32[]{:S(2)}, u32[]{:S(2)}) collective-permute-start(bf16[2,2,48,1024]{3,2,1,0:T(8,128)(2,1)} %get-tuple-element.36), channel_id=1, source_target_pairs={{0,4},{1,5},{2,6},{3,7},{4,0},{5,1},{6,2},{7,3},{8,12},{9,13},{10,... | collective-permute-start | bytes 1179656 | tf_op jit(solution)/shard_map/ppermute | solution.py:16
  8.4 1.5 %collective-permute-start = (bf16[3,2,48,1024]{3,2,1,0:T(8,128)(2,1)}, bf16[3,2,48,1024]{3,2,1,0:T(8,128)(2,1)S(1)}, u32[]{:S(2)}, u32[]{:S(2)}) collective-permute-start(bf16[3,2,48,1024]{3,2,1,0:T(8,128)(2,1)} %get-tuple-element.32.refs_0_.refs_8_), channel_id=1, source_target_pairs={{0,1},{1,0},{2,3},{3,2},{4,5},{5,4},{6,7},{7,6},{8,9},{9,8},{10,11... | collective-permute-start | bytes 1769480 | tf_op jit(solution)/shard_map/ppermute | solution.py:16
  9.9 1.5 %collective-permute-start.14 = (bf16[3,2,48,1024]{3,2,1,0:T(8,128)(2,1)}, bf16[3,2,48,1024]{3,2,1,0:T(8,128)(2,1)S(1)}, u32[]{:S(2)}, u32[]{:S(2)}) collective-permute-start(bf16[3,2,48,1024]{3,2,1,0:T(8,128)(2,1)} %get-tuple-element.32.refs_0_.refs_8_), channel_id=1, source_target_pairs={{0,16},{8,24},{16,0},{24,8},{1,17},{9,25},{17,1},{25,9},{2,18},{10... | collective-permute-start | bytes 1769480 | tf_op jit(solution)/shard_map/ppermute | solution.py:21
  11.4 12.0 %collective-permute-done.1.refs_2_ = bf16[2,2,48,1024]{3,2,1,0:T(8,128)(2,1)S(1)} collective-permute-done((bf16[2,2,48,1024]{3,2,1,0:T(8,128)(2,1)}, bf16[2,2,48,1024]{3,2,1,0:T(8,128)(2,1)S(1)}, u32[]{:S(2)}, u32[]{:S(2)}) %collective-permute-start.1) | collective-permute-done | bytes 393248 | tf_op jit(solution)/shard_map/ppermute | solution.py:16
  23.4 2.6 %collective-permute-done.3.refs_4_.refs_11_ = bf16[2,2,48,1024]{3,2,1,0:T(8,128)(2,1)S(1)} collective-permute-done((bf16[2,2,48,1024]{3,2,1,0:T(8,128)(2,1)}, bf16[2,2,48,1024]{3,2,1,0:T(8,128)(2,1)S(1)}, u32[]{:S(2)}, u32[]{:S(2)}) %collective-permute-start.3) | collective-permute-done | bytes 393248 | tf_op jit(solution)/shard_map/ppermute | solution.py:16
  26.1 1.5 %collective-permute-start.5 = (bf16[2,2,48,1024]{3,2,1,0:T(8,128)(2,1)S(1)}, bf16[2,2,48,1024]{3,2,1,0:T(8,128)(2,1)S(1)}, u32[]{:S(2)}, u32[]{:S(2)}) collective-permute-start(bf16[2,2,48,1024]{3,2,1,0:T(8,128)(2,1)S(1)} %collective-permute-done.1.refs_2_), channel_id=1, source_target_pairs={{0,1},{1,0},{2,3},{3,2},{4,5},{5,4},{6,7},{7,6},{8,9},{9,8},{10,11... | collective-permute-start | bytes 1179656 | tf_op jit(solution)/shard_map/ppermute | solution.py:16
  27.6 2.4 %collective-permute-done.2.refs_2_.refs_11_ = bf16[1,2,48,1024]{3,2,1,0:T(8,128)(2,1)} collective-permute-done((bf16[1,2,48,1024]{3,2,1,0:T(8,128)(2,1)}, bf16[1,2,48,1024]{3,2,1,0:T(8,128)(2,1)}, u32[]{:S(2)}, u32[]{:S(2)}) %collective-permute-start.2) | collective-permute-done | bytes 196640 | tf_op jit(solution)/shard_map/ppermute | solution.py:16
  30.1 1.3 %collective-permute-start.9 = (bf16[2,2,48,1024]{3,2,1,0:T(8,128)(2,1)S(1)}, bf16[2,2,48,1024]{3,2,1,0:T(8,128)(2,1)S(1)}, u32[]{:S(2)}, u32[]{:S(2)}) collective-permute-start(bf16[2,2,48,1024]{3,2,1,0:T(8,128)(2,1)S(1)} %collective-permute-done.3.refs_4_.refs_11_), channel_id=1, source_target_pairs={{0,1},{1,0},{2,3},{3,2},{4,5},{5,4},{6,7},{7,6},{8,9},{9,8},{10,11... | collective-permute-start | bytes 1179656 | tf_op jit(solution)/shard_map/ppermute | solution.py:16
  31.5 1.5 %collective-permute-start.17 = (bf16[2,2,48,1024]{3,2,1,0:T(8,128)(2,1)S(1)}, bf16[2,2,48,1024]{3,2,1,0:T(8,128)(2,1)S(1)}, u32[]{:S(2)}, u32[]{:S(2)}) collective-permute-start(bf16[2,2,48,1024]{3,2,1,0:T(8,128)(2,1)S(1)} %collective-permute-done.3.refs_4_.refs_11_), channel_id=1, source_target_pairs={{0,16},{8,24},{16,0},{24,8},{1,17},{9,25},{17,1},{25,9},{2,18},{10... | collective-permute-start | bytes 1179656 | tf_op jit(solution)/shard_map/ppermute | solution.py:21
  33.0 3.3 %collective-permute-start.8 = (bf16[1,2,48,1024]{3,2,1,0:T(8,128)(2,1)}, bf16[1,2,48,1024]{3,2,1,0:T(8,128)(2,1)S(1)}, u32[]{:S(2)}, u32[]{:S(2)}) collective-permute-start(bf16[1,2,48,1024]{3,2,1,0:T(8,128)(2,1)} %get-tuple-element.41), channel_id=1, source_target_pairs={{0,4},{1,5},{2,6},{3,7},{4,0},{5,1},{6,2},{7,3},{8,12},{9,13},{10,... | collective-permute-start | bytes 589832 | tf_op jit(solution)/shard_map/ppermute | solution.py:16
  36.5 7.1 %collective-permute-done.4.refs_6_ = bf16[2,2,48,1024]{3,2,1,0:T(8,128)(2,1)S(1)} collective-permute-done((bf16[2,2,48,1024]{3,2,1,0:T(8,128)(2,1)S(1)}, bf16[2,2,48,1024]{3,2,1,0:T(8,128)(2,1)S(1)}, u32[]{:S(2)}, u32[]{:S(2)}) %collective-permute-start.4) | collective-permute-done | bytes 393248 | tf_op jit(solution)/shard_map/ppermute | solution.py:16
  43.7 1.0 %collective-permute-start.6 = (bf16[2,2,48,1024]{3,2,1,0:T(8,128)(2,1)S(1)}, bf16[2,2,48,1024]{3,2,1,0:T(8,128)(2,1)S(1)}, u32[]{:S(2)}, u32[]{:S(2)}) collective-permute-start(bf16[2,2,48,1024]{3,2,1,0:T(8,128)(2,1)S(1)} %collective-permute-done.4.refs_6_), channel_id=1, source_target_pairs={{0,1},{1,0},{2,3},{3,2},{4,5},{5,4},{6,7},{7,6},{8,9},{9,8},{10,11... | collective-permute-start | bytes 1179656 | tf_op jit(solution)/shard_map/ppermute | solution.py:16
  44.7 1.5 %collective-permute-start.11 = (bf16[1,2,48,1024]{3,2,1,0:T(8,128)(2,1)}, bf16[1,2,48,1024]{3,2,1,0:T(8,128)(2,1)}, u32[]{:S(2)}, u32[]{:S(2)}) collective-permute-start(bf16[1,2,48,1024]{3,2,1,0:T(8,128)(2,1)} %collective-permute-done.2.refs_2_.refs_11_), channel_id=1, source_target_pairs={{0,4},{1,5},{2,6},{3,7},{4,0},{5,1},{6,2},{7,3},{8,12},{9,13},{10,... | collective-permute-start | bytes 589832 | tf_op jit(solution)/shard_map/ppermute | solution.py:16
  46.9 0.7 copy-done.8
  47.7 1.5 %collective-permute-start.18 = (bf16[1,2,48,1024]{3,2,1,0:T(8,128)(2,1)}, bf16[1,2,48,1024]{3,2,1,0:T(8,128)(2,1)}, u32[]{:S(2)}, u32[]{:S(2)}) collective-permute-start(bf16[1,2,48,1024]{3,2,1,0:T(8,128)(2,1)} %collective-permute-done.2.refs_2_.refs_11_), channel_id=1, source_target_pairs={{0,16},{8,24},{16,0},{24,8},{1,17},{9,25},{17,1},{25,9},{2,18},{10... | collective-permute-start | bytes 589832 | tf_op jit(solution)/shard_map/ppermute | solution.py:21
  49.3 4.6 %collective-permute-done.11.refs_6_ = bf16[1,2,48,1024]{3,2,1,0:T(8,128)(2,1)} collective-permute-done((bf16[1,2,48,1024]{3,2,1,0:T(8,128)(2,1)}, bf16[1,2,48,1024]{3,2,1,0:T(8,128)(2,1)}, u32[]{:S(2)}, u32[]{:S(2)}) %collective-permute-start.11) | collective-permute-done | bytes 196640 | tf_op jit(solution)/shard_map/ppermute | solution.py:16
  53.9 2.8 %collective-permute-done.10.refs_5_ = bf16[1,2,48,1024]{3,2,1,0:T(8,128)(2,1)S(1)} collective-permute-done((bf16[1,2,48,1024]{3,2,1,0:T(8,128)(2,1)S(1)}, bf16[1,2,48,1024]{3,2,1,0:T(8,128)(2,1)S(1)}, u32[]{:S(2)}, u32[]{:S(2)}) %collective-permute-start.10) | collective-permute-done | bytes 196640 | tf_op jit(solution)/shard_map/ppermute | solution.py:16
  56.6 1.2 %collective-permute-start.12 = (bf16[1,2,48,1024]{3,2,1,0:T(8,128)(2,1)}, bf16[1,2,48,1024]{3,2,1,0:T(8,128)(2,1)}, u32[]{:S(2)}, u32[]{:S(2)}) collective-permute-start(bf16[1,2,48,1024]{3,2,1,0:T(8,128)(2,1)} %collective-permute-done.11.refs_6_), channel_id=1, source_target_pairs={{0,1},{1,0},{2,3},{3,2},{4,5},{5,4},{6,7},{7,6},{8,9},{9,8},{10,11... | collective-permute-start | bytes 589832 | tf_op jit(solution)/shard_map/ppermute | solution.py:16
  57.9 0.9 collective-permute-start.7
  58.7 0.7 add_add_fusion.1
  59.4 5.0 %cross.3 = (f32[6,2,144,384]{3,2,1,0:T(8,128)}, bf16[2,144,384]{2,1,0:T(8,128)(2,1)}) custom-call(s32[3]{0:T(128)} %get-tuple-element.60.scalars, bf16[3,2,48,1024]{3,2,1,0:T(8,128)(2,1)} %get-tuple-element.32.refs_0_.refs_8_, bf16[3,2,48,1024]{3,2,1,0:T(8,128)(2,1)} %copy-done.1, bf16[2,2,48,1024]{3,2,1,0:T(8,128)(2,1)} %copy-done.4, ...), custom_call_target="tpu_custom_call" | custom-call | flops 1 | bytes 1 | tf_op jit(solution)/shard_map/cross/pallas_call | solution.py:152
  64.4 1.4 %collective-permute-start.21 = (bf16[2,144,384]{2,1,0:T(8,128)(2,1)}, bf16[2,144,384]{2,1,0:T(8,128)(2,1)}, u32[]{:S(2)}, u32[]{:S(2)}) collective-permute-start(bf16[2,144,384]{2,1,0:T(8,128)(2,1)} %get-tuple-element.56), channel_id=1, source_target_pairs={{0,4},{1,5},{2,6},{3,7},{4,0},{5,1},{6,2},{7,3},{8,12},{9,13},{10,... | collective-permute-start | bytes 663560 | tf_op jit(solution)/shard_map/ppermute | solution.py:16
  65.8 5.0 %cross.4 = (f32[6,2,144,384]{3,2,1,0:T(8,128)}, bf16[2,144,384]{2,1,0:T(8,128)(2,1)}) custom-call(s32[3]{0:T(128)} %get-tuple-element.59.scalars, bf16[3,2,48,1024]{3,2,1,0:T(8,128)(2,1)} %get-tuple-element.32.refs_0_.refs_8_, bf16[3,2,48,1024]{3,2,1,0:T(8,128)(2,1)} %copy-done.1, ...), custom_call_target="tpu_custom_call", output_to_operand_aliasing={{0}: (15, {})} | custom-call | flops 1 | bytes 1 | tf_op jit(solution)/shard_map/cross/pallas_call | solution.py:152
  70.8 1.6 %collective-permute-start.20 = (bf16[2,144,384]{2,1,0:T(8,128)(2,1)}, bf16[2,144,384]{2,1,0:T(8,128)(2,1)}, u32[]{:S(2)}, u32[]{:S(2)}) collective-permute-start(bf16[2,144,384]{2,1,0:T(8,128)(2,1)} %get-tuple-element.54), channel_id=1, source_target_pairs={{0,4},{1,5},{2,6},{3,7},{4,0},{5,1},{6,2},{7,3},{8,12},{9,13},{10,... | collective-permute-start | bytes 663560 | tf_op jit(solution)/shard_map/ppermute | solution.py:16
  73.0 5.0 %cross.5 = (f32[6,2,144,384]{3,2,1,0:T(8,128)}, bf16[2,144,384]{2,1,0:T(8,128)(2,1)}) custom-call(s32[3]{0:T(128)} %add_add_fusion.scalars, bf16[3,2,48,1024]{3,2,1,0:T(8,128)(2,1)} %get-tuple-element.32.refs_0_.refs_8_, bf16[3,2,48,1024]{3,2,1,0:T(8,128)(2,1)} %copy-done.1, ...), custom_call_target="tpu_custom_call", output_to_operand_aliasing={{0}: (15, {})} | custom-call | flops 1 | bytes 1 | tf_op jit(solution)/shard_map/cross/pallas_call | solution.py:152
  78.0 1.1 %collective-permute-start.19 = (bf16[2,144,384]{2,1,0:T(8,128)(2,1)}, bf16[2,144,384]{2,1,0:T(8,128)(2,1)}, u32[]{:S(2)}, u32[]{:S(2)}) collective-permute-start(bf16[2,144,384]{2,1,0:T(8,128)(2,1)} %get-tuple-element.52), channel_id=1, source_target_pairs={{0,2},{1,3},{2,0},{3,1},{4,6},{5,7},{6,4},{7,5},{8,10},{9,11},{10,... | collective-permute-start | bytes 663560 | tf_op jit(solution)/shard_map/ppermute | solution.py:16
  79.2 4.4 %collective-permute-done.20.came_ref = bf16[2,144,384]{2,1,0:T(8,128)(2,1)} collective-permute-done((bf16[2,144,384]{2,1,0:T(8,128)(2,1)}, bf16[2,144,384]{2,1,0:T(8,128)(2,1)}, u32[]{:S(2)}, u32[]{:S(2)}) %collective-permute-start.20) | collective-permute-done | bytes 221216 | tf_op jit(solution)/shard_map/ppermute | solution.py:16
  83.5 1.7 %place.3._ = f32[6,2,144,384]{3,2,1,0:T(8,128)} custom-call(s32[1]{0:T(128)} %bitcast.3.bin_ref, bf16[2,144,384]{2,1,0:T(8,128)(2,1)} %collective-permute-done.21.came_ref, f32[6,2,144,384]{3,2,1,0:T(8,128)} %get-tuple-element.58._), custom_call_target="tpu_custom_call", output_to_operand_aliasing={{}: (2, {})} | custom-call | tf_op jit(solution)/shard_map/place/pallas_call | solution.py:186
  85.3 1.7 %place.4._ = f32[6,2,144,384]{3,2,1,0:T(8,128)} custom-call(s32[1]{0:T(128)} %bitcast.6.bin_ref, bf16[2,144,384]{2,1,0:T(8,128)(2,1)} %collective-permute-done.20.came_ref, f32[6,2,144,384]{3,2,1,0:T(8,128)} %place.3._), custom_call_target="tpu_custom_call", output_to_operand_aliasing={{}: (2, {})} | custom-call | tf_op jit(solution)/shard_map/place/pallas_call | solution.py:186
  87.0 1.7 %place.5 = f32[6,2,144,384]{3,2,1,0:T(8,128)} custom-call(s32[1]{0:T(128)} %bitcast.bin_ref, bf16[2,144,384]{2,1,0:T(8,128)(2,1)} %collective-permute-done.19.came_ref, f32[6,2,144,384]{3,2,1,0:T(8,128)} %place.4._), custom_call_target="tpu_custom_call", output_to_operand_aliasing={{}: (2, {})} | custom-call | tf_op jit(solution)/shard_map/place/pallas_call | solution.py:186
  (47 shorter events, 1.8 us)
Async XLA Ops:
  2.7 20.7 %collective-permute-start.1 = (bf16[2,2,48,1024]{3,2,1,0:T(8,128)(2,1)}, bf16[2,2,48,1024]{3,2,1,0:T(8,128)(2,1)S(1)}, u32[]{:S(2)}, u32[]{:S(2)}) collective-permute-start(bf16[2,2,48,1024]{3,2,1,0:T(8,128)(2,1)} %get-tuple-element.34), channel_id=1, source_target_pairs={{0,2},{1,3},{2,0},{3,1},{4,6},{5,7},{6,4},{7,5},{8,10},{9,11},{10,... | collective-permute-start | bytes 1179656 | tf_op jit(solution)/shard_map/ppermute | solution.py:16
  5.8 20.3 %collective-permute-start.3 = (bf16[2,2,48,1024]{3,2,1,0:T(8,128)(2,1)}, bf16[2,2,48,1024]{3,2,1,0:T(8,128)(2,1)S(1)}, u32[]{:S(2)}, u32[]{:S(2)}) collective-permute-start(bf16[2,2,48,1024]{3,2,1,0:T(8,128)(2,1)} %get-tuple-element.36), channel_id=1, source_target_pairs={{0,4},{1,5},{2,6},{3,7},{4,0},{5,1},{6,2},{7,3},{8,12},{9,13},{10,... | collective-permute-start | bytes 1179656 | tf_op jit(solution)/shard_map/ppermute | solution.py:16
  8.4 21.7 %collective-permute-start = (bf16[3,2,48,1024]{3,2,1,0:T(8,128)(2,1)}, bf16[3,2,48,1024]{3,2,1,0:T(8,128)(2,1)S(1)}, u32[]{:S(2)}, u32[]{:S(2)}) collective-permute-start(bf16[3,2,48,1024]{3,2,1,0:T(8,128)(2,1)} %get-tuple-element.32.refs_0_.refs_8_), channel_id=1, source_target_pairs={{0,1},{1,0},{2,3},{3,2},{4,5},{5,4},{6,7},{7,6},{8,9},{9,8},{10,11... | collective-permute-start | bytes 1769480 | tf_op jit(solution)/shard_map/ppermute | solution.py:16
  9.9 21.6 %collective-permute-start.14 = (bf16[3,2,48,1024]{3,2,1,0:T(8,128)(2,1)}, bf16[3,2,48,1024]{3,2,1,0:T(8,128)(2,1)S(1)}, u32[]{:S(2)}, u32[]{:S(2)}) collective-permute-start(bf16[3,2,48,1024]{3,2,1,0:T(8,128)(2,1)} %get-tuple-element.32.refs_0_.refs_8_), channel_id=1, source_target_pairs={{0,16},{8,24},{16,0},{24,8},{1,17},{9,25},{17,1},{25,9},{2,18},{10... | collective-permute-start | bytes 1769480 | tf_op jit(solution)/shard_map/ppermute | solution.py:21
  11.4 21.6 %collective-permute-start.13 = (bf16[3,2,48,1024]{3,2,1,0:T(8,128)(2,1)}, bf16[3,2,48,1024]{3,2,1,0:T(8,128)(2,1)S(1)}, u32[]{:S(2)}, u32[]{:S(2)}) collective-permute-start(bf16[3,2,48,1024]{3,2,1,0:T(8,128)(2,1)} %get-tuple-element.32.refs_0_.refs_8_), channel_id=1, source_target_pairs={{0,24},{8,0},{16,8},{24,16},{1,25},{9,1},{17,9},{25,17},{2,26},{10... | collective-permute-start | bytes 1769480 | tf_op jit(solution)/shard_map/ppermute | solution.py:21
  23.4 23.3 %copy-start.4 = (bf16[2,2,48,1024]{3,2,1,0:T(8,128)(2,1)}, bf16[2,2,48,1024]{3,2,1,0:T(8,128)(2,1)S(1)}, u32[]{:S(2)}) copy-start(bf16[2,2,48,1024]{3,2,1,0:T(8,128)(2,1)S(1)} %collective-permute-done.1.refs_2_) | copy-start | bytes 1179652
  23.4 6.5 %collective-permute-start.2 = (bf16[1,2,48,1024]{3,2,1,0:T(8,128)(2,1)}, bf16[1,2,48,1024]{3,2,1,0:T(8,128)(2,1)}, u32[]{:S(2)}, u32[]{:S(2)}) collective-permute-start(bf16[1,2,48,1024]{3,2,1,0:T(8,128)(2,1)} %get-tuple-element.35), channel_id=1, source_target_pairs={{0,2},{1,3},{2,0},{3,1},{4,6},{5,7},{6,4},{7,5},{8,10},{9,11},{10,... | collective-permute-start | bytes 589832 | tf_op jit(solution)/shard_map/ppermute | solution.py:16
  26.1 10.5 %copy-start = (bf16[2,2,48,1024]{3,2,1,0:T(8,128)(2,1)}, bf16[2,2,48,1024]{3,2,1,0:T(8,128)(2,1)S(1)}, u32[]{:S(2)}) copy-start(bf16[2,2,48,1024]{3,2,1,0:T(8,128)(2,1)S(1)} %collective-permute-done.3.refs_4_.refs_11_) | copy-start | bytes 1179652
  26.1 10.5 %collective-permute-start.5 = (bf16[2,2,48,1024]{3,2,1,0:T(8,128)(2,1)S(1)}, bf16[2,2,48,1024]{3,2,1,0:T(8,128)(2,1)S(1)}, u32[]{:S(2)}, u32[]{:S(2)}) collective-permute-start(bf16[2,2,48,1024]{3,2,1,0:T(8,128)(2,1)S(1)} %collective-permute-done.1.refs_2_), channel_id=1, source_target_pairs={{0,1},{1,0},{2,3},{3,2},{4,5},{5,4},{6,7},{7,6},{8,9},{9,8},{10,11... | collective-permute-start | bytes 1179656 | tf_op jit(solution)/shard_map/ppermute | solution.py:16
  30.0 13.7 %collective-permute-start.4 = (bf16[2,2,48,1024]{3,2,1,0:T(8,128)(2,1)S(1)}, bf16[2,2,48,1024]{3,2,1,0:T(8,128)(2,1)S(1)}, u32[]{:S(2)}, u32[]{:S(2)}) collective-permute-start(bf16[2,2,48,1024]{3,2,1,0:T(8,128)(2,1)S(1)} %collective-permute-done.3.refs_4_.refs_11_), channel_id=1, source_target_pairs={{0,2},{1,3},{2,0},{3,1},{4,6},{5,7},{6,4},{7,5},{8,10},{9,11},{10,... | collective-permute-start | bytes 1179656 | tf_op jit(solution)/shard_map/ppermute | solution.py:16
  30.1 16.6 %copy-start.1 = (bf16[3,2,48,1024]{3,2,1,0:T(8,128)(2,1)}, bf16[3,2,48,1024]{3,2,1,0:T(8,128)(2,1)S(1)}, u32[]{:S(2)}) copy-start(bf16[3,2,48,1024]{3,2,1,0:T(8,128)(2,1)S(1)} %collective-permute-done.refs_1_) | copy-start | bytes 1769476
  30.1 16.1 %collective-permute-start.9 = (bf16[2,2,48,1024]{3,2,1,0:T(8,128)(2,1)S(1)}, bf16[2,2,48,1024]{3,2,1,0:T(8,128)(2,1)S(1)}, u32[]{:S(2)}, u32[]{:S(2)}) collective-permute-start(bf16[2,2,48,1024]{3,2,1,0:T(8,128)(2,1)S(1)} %collective-permute-done.3.refs_4_.refs_11_), channel_id=1, source_target_pairs={{0,1},{1,0},{2,3},{3,2},{4,5},{5,4},{6,7},{7,6},{8,9},{9,8},{10,11... | collective-permute-start | bytes 1179656 | tf_op jit(solution)/shard_map/ppermute | solution.py:16
  31.5 15.3 %copy-start.2 = (bf16[3,2,48,1024]{3,2,1,0:T(8,128)(2,1)}, bf16[3,2,48,1024]{3,2,1,0:T(8,128)(2,1)S(1)}, u32[]{:S(2)}) copy-start(bf16[3,2,48,1024]{3,2,1,0:T(8,128)(2,1)S(1)} %collective-permute-done.14.refs_10_) | copy-start | bytes 1769476
  31.5 15.3 %collective-permute-start.17 = (bf16[2,2,48,1024]{3,2,1,0:T(8,128)(2,1)S(1)}, bf16[2,2,48,1024]{3,2,1,0:T(8,128)(2,1)S(1)}, u32[]{:S(2)}, u32[]{:S(2)}) collective-permute-start(bf16[2,2,48,1024]{3,2,1,0:T(8,128)(2,1)S(1)} %collective-permute-done.3.refs_4_.refs_11_), channel_id=1, source_target_pairs={{0,16},{8,24},{16,0},{24,8},{1,17},{9,25},{17,1},{25,9},{2,18},{10... | collective-permute-start | bytes 1179656 | tf_op jit(solution)/shard_map/ppermute | solution.py:21
  33.0 13.8 %copy-start.3 = (bf16[3,2,48,1024]{3,2,1,0:T(8,128)(2,1)}, bf16[3,2,48,1024]{3,2,1,0:T(8,128)(2,1)S(1)}, u32[]{:S(2)}) copy-start(bf16[3,2,48,1024]{3,2,1,0:T(8,128)(2,1)S(1)} %collective-permute-done.13.refs_9_) | copy-start | bytes 1769476
  33.0 11.7 %collective-permute-start.8 = (bf16[1,2,48,1024]{3,2,1,0:T(8,128)(2,1)}, bf16[1,2,48,1024]{3,2,1,0:T(8,128)(2,1)S(1)}, u32[]{:S(2)}, u32[]{:S(2)}) collective-permute-start(bf16[1,2,48,1024]{3,2,1,0:T(8,128)(2,1)} %get-tuple-element.41), channel_id=1, source_target_pairs={{0,4},{1,5},{2,6},{3,7},{4,0},{5,1},{6,2},{7,3},{8,12},{9,13},{10,... | collective-permute-start | bytes 589832 | tf_op jit(solution)/shard_map/ppermute | solution.py:16
  36.5 10.3 %copy-start.5 = (bf16[2,2,48,1024]{3,2,1,0:T(8,128)(2,1)}, bf16[2,2,48,1024]{3,2,1,0:T(8,128)(2,1)S(1)}, u32[]{:S(2)}) copy-start(bf16[2,2,48,1024]{3,2,1,0:T(8,128)(2,1)S(1)} %collective-permute-done.5.refs_3_) | copy-start | bytes 1179652
  36.5 12.7 %collective-permute-start.15 = (bf16[2,2,48,1024]{3,2,1,0:T(8,128)(2,1)S(1)}, bf16[2,2,48,1024]{3,2,1,0:T(8,128)(2,1)S(1)}, u32[]{:S(2)}, u32[]{:S(2)}) collective-permute-start(bf16[2,2,48,1024]{3,2,1,0:T(8,128)(2,1)S(1)} %collective-permute-done.3.refs_4_.refs_11_), channel_id=1, source_target_pairs={{0,24},{8,0},{16,8},{24,16},{1,25},{9,1},{17,9},{25,17},{2,26},{10... | collective-permute-start | bytes 1179656 | tf_op jit(solution)/shard_map/ppermute | solution.py:21
  43.7 5.5 %copy-start.6 = (bf16[2,2,48,1024]{3,2,1,0:T(8,128)(2,1)}, bf16[2,2,48,1024]{3,2,1,0:T(8,128)(2,1)S(1)}, u32[]{:S(2)}) copy-start(bf16[2,2,48,1024]{3,2,1,0:T(8,128)(2,1)S(1)} %collective-permute-done.4.refs_6_) | copy-start | bytes 1179652
  43.7 14.2 %collective-permute-start.6 = (bf16[2,2,48,1024]{3,2,1,0:T(8,128)(2,1)S(1)}, bf16[2,2,48,1024]{3,2,1,0:T(8,128)(2,1)S(1)}, u32[]{:S(2)}, u32[]{:S(2)}) collective-permute-start(bf16[2,2,48,1024]{3,2,1,0:T(8,128)(2,1)S(1)} %collective-permute-done.4.refs_6_), channel_id=1, source_target_pairs={{0,1},{1,0},{2,3},{3,2},{4,5},{5,4},{6,7},{7,6},{8,9},{9,8},{10,11... | collective-permute-start | bytes 1179656 | tf_op jit(solution)/shard_map/ppermute | solution.py:16
  44.7 14.0 %copy-start.11 = (bf16[1,2,48,1024]{3,2,1,0:T(8,128)(2,1)}, bf16[1,2,48,1024]{3,2,1,0:T(8,128)(2,1)S(1)}, u32[]{:S(2)}) copy-start(bf16[1,2,48,1024]{3,2,1,0:T(8,128)(2,1)S(1)} %collective-permute-done.8.refs_4_) | copy-start | bytes 589828
  44.7 9.2 %collective-permute-start.11 = (bf16[1,2,48,1024]{3,2,1,0:T(8,128)(2,1)}, bf16[1,2,48,1024]{3,2,1,0:T(8,128)(2,1)}, u32[]{:S(2)}, u32[]{:S(2)}) collective-permute-start(bf16[1,2,48,1024]{3,2,1,0:T(8,128)(2,1)} %collective-permute-done.2.refs_2_.refs_11_), channel_id=1, source_target_pairs={{0,4},{1,5},{2,6},{3,7},{4,0},{5,1},{6,2},{7,3},{8,12},{9,13},{10,... | collective-permute-start | bytes 589832 | tf_op jit(solution)/shard_map/ppermute | solution.py:16
  46.2 10.4 %collective-permute-start.10 = (bf16[1,2,48,1024]{3,2,1,0:T(8,128)(2,1)S(1)}, bf16[1,2,48,1024]{3,2,1,0:T(8,128)(2,1)S(1)}, u32[]{:S(2)}, u32[]{:S(2)}) collective-permute-start(bf16[1,2,48,1024]{3,2,1,0:T(8,128)(2,1)S(1)} %collective-permute-done.8.refs_4_), channel_id=1, source_target_pairs={{0,1},{1,0},{2,3},{3,2},{4,5},{5,4},{6,7},{7,6},{8,9},{9,8},{10,11... | collective-permute-start | bytes 589832 | tf_op jit(solution)/shard_map/ppermute | solution.py:16
  47.7 23.1 %collective-permute-start.18 = (bf16[1,2,48,1024]{3,2,1,0:T(8,128)(2,1)}, bf16[1,2,48,1024]{3,2,1,0:T(8,128)(2,1)}, u32[]{:S(2)}, u32[]{:S(2)}) collective-permute-start(bf16[1,2,48,1024]{3,2,1,0:T(8,128)(2,1)} %collective-permute-done.2.refs_2_.refs_11_), channel_id=1, source_target_pairs={{0,16},{8,24},{16,0},{24,8},{1,17},{9,25},{17,1},{25,9},{2,18},{10... | collective-permute-start | bytes 589832 | tf_op jit(solution)/shard_map/ppermute | solution.py:21
  49.2 8.7 %copy-start.9 = (bf16[2,2,48,1024]{3,2,1,0:T(8,128)(2,1)}, bf16[2,2,48,1024]{3,2,1,0:T(8,128)(2,1)S(1)}, u32[]{:S(2)}) copy-start(bf16[2,2,48,1024]{3,2,1,0:T(8,128)(2,1)S(1)} %collective-permute-done.15.refs_12_) | copy-start | bytes 1179652
  49.2 23.8 %collective-permute-start.16 = (bf16[1,2,48,1024]{3,2,1,0:T(8,128)(2,1)}, bf16[1,2,48,1024]{3,2,1,0:T(8,128)(2,1)}, u32[]{:S(2)}, u32[]{:S(2)}) collective-permute-start(bf16[1,2,48,1024]{3,2,1,0:T(8,128)(2,1)} %collective-permute-done.2.refs_2_.refs_11_), channel_id=1, source_target_pairs={{0,24},{8,0},{16,8},{24,16},{1,25},{9,1},{17,9},{25,17},{2,26},{10... | collective-permute-start | bytes 589832 | tf_op jit(solution)/shard_map/ppermute | solution.py:21
  56.6 2.1 %copy-start.12 = (bf16[1,2,48,1024]{3,2,1,0:T(8,128)(2,1)}, bf16[1,2,48,1024]{3,2,1,0:T(8,128)(2,1)S(1)}, u32[]{:S(2)}) copy-start(bf16[1,2,48,1024]{3,2,1,0:T(8,128)(2,1)S(1)} %collective-permute-done.10.refs_5_) | copy-start | bytes 589828
  56.6 16.4 %collective-permute-start.12 = (bf16[1,2,48,1024]{3,2,1,0:T(8,128)(2,1)}, bf16[1,2,48,1024]{3,2,1,0:T(8,128)(2,1)}, u32[]{:S(2)}, u32[]{:S(2)}) collective-permute-start(bf16[1,2,48,1024]{3,2,1,0:T(8,128)(2,1)} %collective-permute-done.11.refs_6_), channel_id=1, source_target_pairs={{0,1},{1,0},{2,3},{3,2},{4,5},{5,4},{6,7},{7,6},{8,9},{9,8},{10,11... | collective-permute-start | bytes 589832 | tf_op jit(solution)/shard_map/ppermute | solution.py:16
  57.9 15.2 %collective-permute-start.7 = (bf16[1,2,48,1024]{3,2,1,0:T(8,128)(2,1)}, bf16[1,2,48,1024]{3,2,1,0:T(8,128)(2,1)}, u32[]{:S(2)}, u32[]{:S(2)}) collective-permute-start(bf16[1,2,48,1024]{3,2,1,0:T(8,128)(2,1)} %collective-permute-done.2.refs_2_.refs_11_), channel_id=1, source_target_pairs={{0,1},{1,0},{2,3},{3,2},{4,5},{5,4},{6,7},{7,6},{8,9},{9,8},{10,11... | collective-permute-start | bytes 589832 | tf_op jit(solution)/shard_map/ppermute | solution.py:16
  64.4 14.8 %collective-permute-start.21 = (bf16[2,144,384]{2,1,0:T(8,128)(2,1)}, bf16[2,144,384]{2,1,0:T(8,128)(2,1)}, u32[]{:S(2)}, u32[]{:S(2)}) collective-permute-start(bf16[2,144,384]{2,1,0:T(8,128)(2,1)} %get-tuple-element.56), channel_id=1, source_target_pairs={{0,4},{1,5},{2,6},{3,7},{4,0},{5,1},{6,2},{7,3},{8,12},{9,13},{10,... | collective-permute-start | bytes 663560 | tf_op jit(solution)/shard_map/ppermute | solution.py:16
  70.8 12.7 %collective-permute-start.20 = (bf16[2,144,384]{2,1,0:T(8,128)(2,1)}, bf16[2,144,384]{2,1,0:T(8,128)(2,1)}, u32[]{:S(2)}, u32[]{:S(2)}) collective-permute-start(bf16[2,144,384]{2,1,0:T(8,128)(2,1)} %get-tuple-element.54), channel_id=1, source_target_pairs={{0,4},{1,5},{2,6},{3,7},{4,0},{5,1},{6,2},{7,3},{8,12},{9,13},{10,... | collective-permute-start | bytes 663560 | tf_op jit(solution)/shard_map/ppermute | solution.py:16
  78.0 9.0 %collective-permute-start.19 = (bf16[2,144,384]{2,1,0:T(8,128)(2,1)}, bf16[2,144,384]{2,1,0:T(8,128)(2,1)}, u32[]{:S(2)}, u32[]{:S(2)}) collective-permute-start(bf16[2,144,384]{2,1,0:T(8,128)(2,1)} %get-tuple-element.52), channel_id=1, source_target_pairs={{0,2},{1,3},{2,0},{3,1},{4,6},{5,7},{6,4},{7,5},{8,10},{9,11},{10,... | collective-permute-start | bytes 663560 | tf_op jit(solution)/shard_map/ppermute | solution.py:16
  (3 other events, 2.4 us)

commit v3 on v0

v3 whole, which is shorter than its diff:
```python
import functools

import jax
import jax.numpy as jnp
from jax import lax
from jax.experimental import pallas as pl
from jax.experimental.pallas import tpu as pltpu
from jax.sharding import PartitionSpec as P

VMEM_BYTES = 64 * 1024 * 1024 - 65536


def moved_by_xor(value, axis, bits):
    count = lax.axis_size(axis)
    return lax.ppermute(value, axis, [(source, source ^ bits) for source in range(count)])


def moved_by_shift(value, axis, steps):
    count = lax.axis_size(axis)
    return lax.ppermute(value, axis, [(source, (source + steps) % count) for source in range(count)])


SPLITS = (4, 4, 2)
WHITE = {
    "own": ((0, 0), (1, 0), (2, 0)),
    "front": ((0, 0), (1, 0)),
    "back": ((2, 0),),
    "front_other": ((0, 1), (1, 1)),
    "back_other": ((2, 1),),
}
SENT = {
    "got": ("front_other", "rrow", 4),
    "own_x": ("own", "rrow", 1),
    "front_z": ("front", "rrow", 2),
    "own_y1": ("own", "rcol", 1),
    "own_y2": ("own", "rcol", 2),
    "front_d": ("front_z", "rrow", 1),
    "last": ("back_other", "rrow", 2),
    "back_z": ("back", "rrow", 4),
    "got_z": ("got", "rrow", 2),
    "got_x": ("got", "rrow", 1),
    "got_y1": ("got", "rcol", 1),
    "got_y2": ("got", "rcol", 2),
    "got_d": ("got_z", "rrow", 1),
    "last_z": ("last", "rrow", 4),
    "back_d": ("back_z", "rrow", 1),
    "last_x": ("last", "rrow", 1),
    "last_y1": ("last", "rcol", 1),
    "last_y2": ("last", "rcol", 2),
    "last_d": ("last_z", "rrow", 1),
    "came0": ("far0", "came", 4),
    "came1": ("far1", "came", 4),
    "came2": ("far2", "came", 2),
}
TAKEN = {}
ROWS = {
    0: [("own", 0), ("own_x", 0), ("front_z", 0), ("front_d", 0), ("got", 0), ("got_x", 0), ("got_z", 0), ("got_d", 0)],
    1: [("own", 1), ("own_x", 1), ("front_z", 1), ("front_d", 1), ("got", 1), ("got_x", 1), ("got_z", 1), ("got_d", 1)],
    2: [("own", 2), ("own_x", 2), ("last", 0), ("last_x", 0), ("back_z", 0), ("back_d", 0), ("last_z", 0), ("last_d", 0)],
}
COLUMNS = {
    0: (("own", 0), ("got", 0)),
    1: (("own", 1), ("got", 1)),
    2: (("own", 2), ("last", 0)),
}
FAR = 2
ORDER = ("got", "own_x", "front_z", "own_y1", "own_y2", "front_d", "last", "back_z", "got_z", "got_x", "got_y1", "got_y2", "got_d", "last_z", "back_d", "last_x", "last_y1", "last_y2", "last_d", "far0", "came0", "far1", "came1", "far2", "came2", "near012", "place01", "place2")
GATES = {
    "last": ["front_z"],
    "back_z": ["got"],
    "got_z": ["last"],
    "got_x": ["own_x"],
    "got_y1": ["own_y1"],
    "got_y2": ["own_y2"],
    "got_d": ["front_d"],
    "last_z": ["back_z"],
    "back_d": ["got_x"],
    "last_x": ["got_d"],
    "last_y1": ["got_y1"],
    "last_y2": ["got_y2"],
    "last_d": ["back_d"],
}


def bin_of(place, pair, split, other):
    return 2 * pair + ((place // split) % 2 + other) % 2


def whiten_kernel(plan, splits, place_ref, spectra_ref, valid_ref, *out_refs):
    bins = spectra_ref.shape[0]
    total = spectra_ref[0, 0] * spectra_ref[0, 0] + spectra_ref[0, 1] * spectra_ref[0, 1]
    for f in range(1, bins):
        total = total + (spectra_ref[f, 0] * spectra_ref[f, 0] + spectra_ref[f, 1] * spectra_ref[f, 1])
    amplitude = jnp.sqrt(jnp.maximum(total / bins, 1.0))
    factor = valid_ref[...].astype(jnp.float32) / amplitude
    place = place_ref[0]
    for pair, split in enumerate(splits):
        for other in range(2):
            for part in range(2):
                value = (spectra_ref[bin_of(place, pair, split, other), part] * factor).astype(jnp.bfloat16)
                for out_ref, slabs in zip(out_refs, plan):
                    if (pair, other) in slabs:
                        out_ref[slabs.index((pair, other)), part] = value


def whiten(plan, splits, place, spectra, valid):
    bins, _, channels, windows = spectra.shape
    tile = windows // 2 if windows % 256 == 0 else windows
    return pl.pallas_call(
        functools.partial(whiten_kernel, plan, splits),
        grid_spec=pltpu.PrefetchScalarGridSpec(
            num_scalar_prefetch=1,
            grid=(windows // tile,),
            in_specs=[
                pl.BlockSpec((bins, 2, channels, tile), lambda i, p: (0, 0, 0, i)),
                pl.BlockSpec((channels, tile), lambda i, p: (0, i)),
            ],
            out_specs=[pl.BlockSpec((len(slabs), 2, channels, tile), lambda i, p: (0, 0, 0, i)) for slabs in plan],
        ),
        out_shape=[jax.ShapeDtypeStruct((len(slabs), 2, channels, windows), jnp.bfloat16) for slabs in plan],
        compiler_params=pltpu.CompilerParams(vmem_limit_bytes=VMEM_BYTES),
        cost_estimate=pl.CostEstimate(flops=1, bytes_accessed=1, transcendentals=0),
        name="whiten",
    )(place, spectra, valid)


def cross_kernel(jobs, place_ref, *refs):
    left_ref, right_ref, mine_ref, theirs_ref, sems = refs[-5:]
    out_ref = refs[-6]
    place = place_ref[0]
    height, windows = refs[0].shape[2:]
    moves, started = [], []

    def move(source, target):
        copy = pltpu.make_async_copy(source, target, sems.at[len(started)])
        copy.start()
        started.append(copy)
        return copy

    given = iter(refs)
    for n, (_, _, kind, row_slots, column_slots) in enumerate(jobs):
        arriving = []
        for label, slot in enumerate(row_slots):
            start = pl.multiple_of((place ^ label) * height, 16)
            arriving.append(move(next(given).at[slot], left_ref.at[n, :, pl.ds(start, height)]))
        for d, slot in enumerate(column_slots):
            arriving.append(move(next(given).at[slot], right_ref.at[n, :, pl.ds(d * height, height)]))
        moves.append(arriving)

    scale = 1.0 / windows
    leaving = []
    for n, (pair, split, kind, _, _) in enumerate(jobs):
        for copy in moves[n]:
            copy.wait()
        group, width = left_ref.shape[2], right_ref.shape[2]
        right = right_ref[n].reshape(2 * width, windows)
        left = left_ref[n].reshape(2 * group, windows)
        sums = scale * lax.dot_general(right, left, (((1,), (1,)), ((), ())), preferred_element_type=jnp.float32)
        block_ref = mine_ref if kind == "near" else theirs_ref
        block_ref[n, 0] = (sums[:width, :group] + sums[width:, group:]).astype(block_ref.dtype)
        block_ref[n, 1] = (sums[:width, group:] - sums[width:, :group]).astype(block_ref.dtype)
        target = out_ref.at[bin_of(place, pair, split, 0)] if kind == "near" else out_ref
        leaving.append(move(block_ref.at[n], target))
    for copy in leaving:
        copy.wait()


def cross(place, kind, jobs, out, bins):
    count = len(jobs)
    operands = [array for _, _, rows, columns in jobs for array, _ in (*rows, *columns)]
    plan = [
        (pair, split, kind, tuple(slot for _, slot in rows), tuple(slot for _, slot in columns))
        for pair, split, rows, columns in jobs
    ]
    _, _, rows, columns = jobs[0]
    *_, height, windows = operands[0].shape
    group, width = len(rows) * height, len(columns) * height
    aliases = {}
    if out is not None:
        operands.append(out)
        aliases = {len(operands): 0}
    shape = jax.ShapeDtypeStruct((2, width, group), jnp.bfloat16)
    if kind == "near":
        shape = jax.ShapeDtypeStruct((bins, 2, width, group), jnp.float32)
    return pl.pallas_call(
        functools.partial(cross_kernel, plan),
        grid_spec=pltpu.PrefetchScalarGridSpec(
            num_scalar_prefetch=1,
            grid=(1,),
            in_specs=[pl.BlockSpec(memory_space=pl.ANY)] * len(operands),
            out_specs=pl.BlockSpec(memory_space=pl.ANY),
            scratch_shapes=[
                pltpu.VMEM((count, 2, group, windows), jnp.bfloat16),
                pltpu.VMEM((count, 2, width, windows), jnp.bfloat16),
                pltpu.VMEM((count, 2, width, group), jnp.float32),
                pltpu.VMEM((count, 2, width, group), jnp.bfloat16),
                pltpu.SemaphoreType.DMA((count * (len(rows) + len(columns) + 1),)),
            ],
        ),
        out_shape=shape,
        input_output_aliases=aliases,
        compiler_params=pltpu.CompilerParams(vmem_limit_bytes=VMEM_BYTES),
        cost_estimate=pl.CostEstimate(flops=1, bytes_accessed=1, transcendentals=0),
        name="cross_" + kind,
    )(place, *operands)


def place_kernel(pairs, place_ref, *refs):
    count = len(pairs)
    came_refs, out_ref = refs[:count], refs[count + 1]
    old_ref, new_ref, sems = refs[count + 2:]
    place = place_ref[0]
    reads = [pltpu.make_async_copy(came_refs[n], old_ref.at[n], sems.at[n]) for n in range(count)]
    for copy in reads:
        copy.start()
    writes = []
    for n, (pair, split) in enumerate(pairs):
        reads[n].wait()
        new_ref[n] = old_ref[n].astype(jnp.float32)
        at = bin_of(place, pair, split, 1)
        writes.append(pltpu.make_async_copy(new_ref.at[n], out_ref.at[at], sems.at[count + n]))
        writes[n].start()
    for copy in writes:
        copy.wait()


def place_blocks(place, pairs, came, out):
    count = len(came)
    return pl.pallas_call(
        functools.partial(place_kernel, pairs),
        grid_spec=pltpu.PrefetchScalarGridSpec(
            num_scalar_prefetch=1,
            grid=(1,),
            in_specs=[pl.BlockSpec(memory_space=pl.ANY)] * (count + 1),
            out_specs=pl.BlockSpec(memory_space=pl.ANY),
            scratch_shapes=[
                pltpu.VMEM((count, *out.shape[1:]), jnp.bfloat16),
                pltpu.VMEM((count, *out.shape[1:]), jnp.float32),
                pltpu.SemaphoreType.DMA((2 * count,)),
            ],
        ),
        out_shape=jax.ShapeDtypeStruct(out.shape, jnp.float32),
        input_output_aliases={count + 1: 0},
        compiler_params=pltpu.CompilerParams(vmem_limit_bytes=VMEM_BYTES),
        cost_estimate=pl.CostEstimate(flops=1, bytes_accessed=1, transcendentals=0),
        name="place",
    )(place, *came, out)


def shards(spectra, valid):
    bins = spectra.shape[0]
    reach = lax.axis_size("rcol") // 2 + 1
    place = lax.axis_index("rrow").astype(jnp.int32)[None]
    held = dict(zip(WHITE, whiten(tuple(WHITE.values()), SPLITS, place, spectra, valid)))

    def move(name):
        if name in TAKEN:
            source, slot = TAKEN[name]
            held[name] = held[source][slot:slot + 1]
            return
        source, axis, step = SENT[name]
        value, gates = held[source], GATES.get(name, ())
        if gates:
            value, *rest = lax.optimization_barrier((value, *(held[gate] for gate in gates)))
            held.update(zip(gates, rest))
        if axis == "came":
            held[name] = moved_by_xor(value, "rrow", step)
            return
        if axis == "rrow":
            held[name] = moved_by_xor(value, axis, step)
            return
        for d in ([step] if step < FAR else range(step, reach)):
            held[name[:-1] + str(d)] = moved_by_shift(value, axis, -d)

    def columns(name, slot):
        return [(held[name], slot)] + [(held[name + "_y" + str(d)], slot) for d in range(1, reach)]

    def job(k, side):
        rows = [(held[name], slot) for name, slot in ROWS[k]]
        return (k, SPLITS[k], rows, columns(*COLUMNS[k][side]))

    out = None
    for name in ORDER:
        if name.startswith("far"):
            k = int(name[3:])
            held[name] = cross(place, "far", [job(k, 1)], None, bins)
        elif name.startswith("near"):
            out = cross(place, "near", [job(int(k), 0) for k in name[4:]], out, bins)
        elif name.startswith("place"):
            pairs = [int(k) for k in name[5:]]
            out = place_blocks(place, [(k, SPLITS[k]) for k in pairs], [held["came" + str(k)] for k in pairs], out)
        else:
            with jax.named_scope(name):
                move(name)
    return jnp.swapaxes(out, 2, 3)


def solution(mesh):
    in_specs = (P("band", None, ("rcol", "rrow"), None), P(("rcol", "rrow"), None))
    out_specs = P("band", None, "rcol", "rrow")
    return jax.shard_map(shards, mesh=mesh, in_specs=in_specs, out_specs=out_specs, check_vma=False)
```

time: 184 us -> 86.2 us (0.47)
  waiting for transfers between devices: 136 us -> 35.8 us
  starting transfers between devices: 4.66 us -> 27.9 us
  matrix products: 23.1 us -> 0 us
  Pallas kernels: 0 us -> 21.2 us
  between operations: 13.6 us -> 0.14 us
  other arithmetic: 4.69 us -> 0 us
    all_gather x1 -> x0, waiting for transfers between devices: 122 us -> none  [shards(): rows = lax.all_gather(white, 'rrow', axis=2, tiled=True)]
    ppermute x2 -> x22, starting transfers between devices: 4.66 us -> 27.9 us  [the longest x16 22.4 us: moved_by_xor(): lax.ppermute(value, axis, [(source, source ^ bits) for source in range(co...]
    dot_general x12 -> x0, matrix products: 23.1 us -> none  [the longest x3 7.12 us: shards(): jnp.einsum('fgw,fbw->fgb', rows[:, 0], partner[:, 1], preferred_element_t...]
    ppermute x2 -> x22, waiting for transfers between devices: 14 us -> 35.8 us  [the longest x16 35.7 us: moved_by_xor(): lax.ppermute(value, axis, [(source, source ^ bits) for source in range(co...]
    pallas_call x0 -> x7, Pallas kernels: none -> 21.2 us  [the longest x4 14.8 us: cross(): pl.pallas_call(functools.partial(cross_kernel, plan), grid_spec=pltpu.Pre...]
    reduce_sum x1 -> x0, other arithmetic: 2.05 us -> none  [whiten(): jnp.mean(spectra[:, 0] * spectra[:, 0] + spectra[:, 1] * spectra[:, 1], a...]
  transfers between devices with their start and end apart: 3 -> 22, of which waited for: 2 -> 10; matrix products, arithmetic and copies ran while one was open for 9% -> 0% of each run, Pallas kernels for 0% -> 19%
where the time goes in v3:
time: 86.2 us; the launch traced here: 85.9 us
  waiting for transfers between devices  35.8 us (42%)
  starting transfers between devices  27.9 us (32%)
  Pallas kernels  21.2 us (25%)
    ppermute x16, waiting for transfers between devices, moved_by_xor(): lax.ppermute(value, axis, [(source, source ^ bits) for source in range(co...  35.7 us
    ppermute x16, starting transfers between devices, moved_by_xor(): lax.ppermute(value, axis, [(source, source ^ bits) for source in range(co...  22.4 us
    pallas_call x4, Pallas kernels, cross(): pl.pallas_call(functools.partial(cross_kernel, plan), grid_spec=pltpu.Pre...  14.8 us
    ppermute x6, starting transfers between devices, moved_by_shift(): lax.ppermute(value, axis, [(source, (source + steps) % count) for source...  5.47 us
    pallas_call x2, Pallas kernels, place_blocks(): pl.pallas_call(functools.partial(place_kernel, pairs), grid_spec=pltpu.Pr...  3.65 us
    pallas_call x1, Pallas kernels, whiten(): pl.pallas_call(functools.partial(whiten_kernel, plan, splits), grid_spec=...  2.72 us
  transfers between devices with their start and end apart: 22, of which 10 were waited for; matrix products, arithmetic and copies ran while one was open for 0% of the time, Pallas kernels for 19%

profile of v3, /device:TPU:0, one launch (start us, length us, event | category | flops | bytes accessed | tf_op | source)
XLA Modules:
  0.0 85.9 jit_solution(4643070075257403195)
XLA Ops:
  0.0 2.7 %whiten.1 = (bf16[3,2,48,1024]{3,2,1,0:T(8,128)(2,1)}, bf16[2,2,48,1024]{3,2,1,0:T(8,128)(2,1)}, bf16[1,2,48,1024]{3,2,1,0:T(8,128)(2,1)}, bf16[2,2,48,1024]{3,2,1,0:T(8,128)(2,1)}, bf16[1,2,48,1024]{3,2,1,0:T(8,128)(2,1)}) custom-call(s32[1]{0:T(128)} %bitcast.place_ref, f32[6,2,48,1024]{3,2,1,0:T(8,128)} %spectra_ref.1, s32[48,1024]{1,0:T(8,128)} %valid_ref.1), custom_call_target="tpu_custom_call" | custom-call | flops 1 | bytes 1 | tf_op jit(solution)/shard_map/whiten/pallas_call | solution.py:109
  2.7 3.1 %collective-permute-start.2 = (bf16[2,2,48,1024]{3,2,1,0:T(8,128)(2,1)}, bf16[2,2,48,1024]{3,2,1,0:T(8,128)(2,1)S(1)}, u32[]{:S(2)}, u32[]{:S(2)}) collective-permute-start(bf16[2,2,48,1024]{3,2,1,0:T(8,128)(2,1)} %get-tuple-element.42), channel_id=1, source_target_pairs={{0,2},{1,3},{2,0},{3,1},{4,6},{5,7},{6,4},{7,5},{8,10},{9,11},{10,... | collective-permute-start | bytes 1179656 | tf_op jit(solution)/shard_map/front_z/ppermute | solution.py:15
  5.8 2.6 %collective-permute-start = (bf16[2,2,48,1024]{3,2,1,0:T(8,128)(2,1)}, bf16[2,2,48,1024]{3,2,1,0:T(8,128)(2,1)S(1)}, u32[]{:S(2)}, u32[]{:S(2)}) collective-permute-start(bf16[2,2,48,1024]{3,2,1,0:T(8,128)(2,1)} %get-tuple-element.38), channel_id=1, source_target_pairs={{0,4},{1,5},{2,6},{3,7},{4,0},{5,1},{6,2},{7,3},{8,12},{9,13},{10,... | collective-permute-start | bytes 1179656 | tf_op jit(solution)/shard_map/got/ppermute | solution.py:15
  8.4 1.5 %collective-permute-start.1 = (bf16[3,2,48,1024]{3,2,1,0:T(8,128)(2,1)}, bf16[3,2,48,1024]{3,2,1,0:T(8,128)(2,1)}, u32[]{:S(2)}, u32[]{:S(2)}) collective-permute-start(bf16[3,2,48,1024]{3,2,1,0:T(8,128)(2,1)} %get-tuple-element.36.refs_0_.refs_8_.refs_11_.refs_19_.refs_22_.refs_30_), channel_id=1, source_target_pairs={{0,1},{1,0},{2,3},{3,2},{4,5},{5,4},{6,7},{7,6},{8,9},{9,8},{10,11... | collective-permute-start | bytes 1769480 | tf_op jit(solution)/shard_map/own_x/ppermute | solution.py:15
  10.0 1.4 %collective-permute-start.16 = (bf16[3,2,48,1024]{3,2,1,0:T(8,128)(2,1)}, bf16[3,2,48,1024]{3,2,1,0:T(8,128)(2,1)S(1)}, u32[]{:S(2)}, u32[]{:S(2)}) collective-permute-start(bf16[3,2,48,1024]{3,2,1,0:T(8,128)(2,1)} %get-tuple-element.36.refs_0_.refs_8_.refs_11_.refs_19_.refs_22_.refs_30_), channel_id=1, source_target_pairs={{0,16},{8,24},{16,0},{24,8},{1,17},{9,25},{17,1},{25,9},{2,18},{10... | collective-permute-start | bytes 1769480 | tf_op jit(solution)/shard_map/own_y2/ppermute | solution.py:20
  11.4 12.0 %collective-permute-done.2.refs_2_.refs_13_ = bf16[2,2,48,1024]{3,2,1,0:T(8,128)(2,1)S(1)} collective-permute-done((bf16[2,2,48,1024]{3,2,1,0:T(8,128)(2,1)}, bf16[2,2,48,1024]{3,2,1,0:T(8,128)(2,1)S(1)}, u32[]{:S(2)}, u32[]{:S(2)}) %collective-permute-start.2) | collective-permute-done | bytes 393248 | tf_op jit(solution)/shard_map/front_z/ppermute | solution.py:15
  23.4 2.6 %collective-permute-done.refs_4_.refs_8_.refs_15_ = bf16[2,2,48,1024]{3,2,1,0:T(8,128)(2,1)S(1)} collective-permute-done((bf16[2,2,48,1024]{3,2,1,0:T(8,128)(2,1)}, bf16[2,2,48,1024]{3,2,1,0:T(8,128)(2,1)S(1)}, u32[]{:S(2)}, u32[]{:S(2)}) %collective-permute-start) | collective-permute-done | bytes 393248 | tf_op jit(solution)/shard_map/got/ppermute | solution.py:15
  26.0 1.5 %collective-permute-start.5 = (bf16[2,2,48,1024]{3,2,1,0:T(8,128)(2,1)S(1)}, bf16[2,2,48,1024]{3,2,1,0:T(8,128)(2,1)S(1)}, u32[]{:S(2)}, u32[]{:S(2)}) collective-permute-start(bf16[2,2,48,1024]{3,2,1,0:T(8,128)(2,1)S(1)} %collective-permute-done.2.refs_2_.refs_13_), channel_id=1, source_target_pairs={{0,1},{1,0},{2,3},{3,2},{4,5},{5,4},{6,7},{7,6},{8,9},{9,8},{10,11... | collective-permute-start | bytes 1179656 | tf_op jit(solution)/shard_map/front_d/ppermute | solution.py:15
  27.5 2.5 %collective-permute-done.3.refs_2_.refs_8_.refs_24_ = bf16[1,2,48,1024]{3,2,1,0:T(8,128)(2,1)} collective-permute-done((bf16[1,2,48,1024]{3,2,1,0:T(8,128)(2,1)}, bf16[1,2,48,1024]{3,2,1,0:T(8,128)(2,1)}, u32[]{:S(2)}, u32[]{:S(2)}) %collective-permute-start.3) | collective-permute-done | bytes 196640 | tf_op jit(solution)/shard_map/last/ppermute | solution.py:15
  30.2 1.3 %collective-permute-start.10 = (bf16[2,2,48,1024]{3,2,1,0:T(8,128)(2,1)S(1)}, bf16[2,2,48,1024]{3,2,1,0:T(8,128)(2,1)S(1)}, u32[]{:S(2)}, u32[]{:S(2)}) collective-permute-start(bf16[2,2,48,1024]{3,2,1,0:T(8,128)(2,1)S(1)} %collective-permute-done.refs_4_.refs_8_.refs_15_), channel_id=1, source_target_pairs={{0,1},{1,0},{2,3},{3,2},{4,5},{5,4},{6,7},{7,6},{8,9},{9,8},{10,11... | collective-permute-start | bytes 1179656 | tf_op jit(solution)/shard_map/got_x/ppermute | solution.py:15
  31.6 3.2 %collective-permute-start.8 = (bf16[1,2,48,1024]{3,2,1,0:T(8,128)(2,1)}, bf16[1,2,48,1024]{3,2,1,0:T(8,128)(2,1)S(1)}, u32[]{:S(2)}, u32[]{:S(2)}) collective-permute-start(bf16[1,2,48,1024]{3,2,1,0:T(8,128)(2,1)} %get-tuple-element.48), channel_id=1, source_target_pairs={{0,4},{1,5},{2,6},{3,7},{4,0},{5,1},{6,2},{7,3},{8,12},{9,13},{10,... | collective-permute-start | bytes 589832 | tf_op jit(solution)/shard_map/back_z/ppermute | solution.py:15
  34.8 1.5 %collective-permute-start.17 = (bf16[2,2,48,1024]{3,2,1,0:T(8,128)(2,1)S(1)}, bf16[2,2,48,1024]{3,2,1,0:T(8,128)(2,1)S(1)}, u32[]{:S(2)}, u32[]{:S(2)}) collective-permute-start(bf16[2,2,48,1024]{3,2,1,0:T(8,128)(2,1)S(1)} %collective-permute-done.refs_4_.refs_8_.refs_15_), channel_id=1, source_target_pairs={{0,16},{8,24},{16,0},{24,8},{1,17},{9,25},{17,1},{25,9},{2,18},{10... | collective-permute-start | bytes 1179656 | tf_op jit(solution)/shard_map/got_y2/ppermute | solution.py:20
  36.5 7.4 %collective-permute-done.4.refs_6_.refs_17_ = bf16[2,2,48,1024]{3,2,1,0:T(8,128)(2,1)S(1)} collective-permute-done((bf16[2,2,48,1024]{3,2,1,0:T(8,128)(2,1)S(1)}, bf16[2,2,48,1024]{3,2,1,0:T(8,128)(2,1)S(1)}, u32[]{:S(2)}, u32[]{:S(2)}) %collective-permute-start.4) | collective-permute-done | bytes 393248 | tf_op jit(solution)/shard_map/got_z/ppermute | solution.py:15
  43.9 1.0 %collective-permute-start.6 = (bf16[2,2,48,1024]{3,2,1,0:T(8,128)(2,1)S(1)}, bf16[2,2,48,1024]{3,2,1,0:T(8,128)(2,1)S(1)}, u32[]{:S(2)}, u32[]{:S(2)}) collective-permute-start(bf16[2,2,48,1024]{3,2,1,0:T(8,128)(2,1)S(1)} %collective-permute-done.4.refs_6_.refs_17_), channel_id=1, source_target_pairs={{0,1},{1,0},{2,3},{3,2},{4,5},{5,4},{6,7},{7,6},{8,9},{9,8},{10,11... | collective-permute-start | bytes 1179656 | tf_op jit(solution)/shard_map/got_d/ppermute | solution.py:15
  44.9 1.3 %collective-permute-start.9 = (bf16[1,2,48,1024]{3,2,1,0:T(8,128)(2,1)}, bf16[1,2,48,1024]{3,2,1,0:T(8,128)(2,1)}, u32[]{:S(2)}, u32[]{:S(2)}) collective-permute-start(bf16[1,2,48,1024]{3,2,1,0:T(8,128)(2,1)} %collective-permute-done.3.refs_2_.refs_8_.refs_24_), channel_id=1, source_target_pairs={{0,4},{1,5},{2,6},{3,7},{4,0},{5,1},{6,2},{7,3},{8,12},{9,13},{10,... | collective-permute-start | bytes 589832 | tf_op jit(solution)/shard_map/last_z/ppermute | solution.py:15
  46.9 1.5 %collective-permute-start.18 = (bf16[1,2,48,1024]{3,2,1,0:T(8,128)(2,1)}, bf16[1,2,48,1024]{3,2,1,0:T(8,128)(2,1)}, u32[]{:S(2)}, u32[]{:S(2)}) collective-permute-start(bf16[1,2,48,1024]{3,2,1,0:T(8,128)(2,1)} %collective-permute-done.3.refs_2_.refs_8_.refs_24_), channel_id=1, source_target_pairs={{0,16},{8,24},{16,0},{24,8},{1,17},{9,25},{17,1},{25,9},{2,18},{10... | collective-permute-start | bytes 589832 | tf_op jit(solution)/shard_map/last_y2/ppermute | solution.py:20
  48.3 1.0 %collective-permute-start.15 = (bf16[1,2,48,1024]{3,2,1,0:T(8,128)(2,1)}, bf16[1,2,48,1024]{3,2,1,0:T(8,128)(2,1)}, u32[]{:S(2)}, u32[]{:S(2)}) collective-permute-start(bf16[1,2,48,1024]{3,2,1,0:T(8,128)(2,1)} %collective-permute-done.3.refs_2_.refs_8_.refs_24_), channel_id=1, source_target_pairs={{0,24},{8,0},{16,8},{24,16},{1,25},{9,1},{17,9},{25,17},{2,26},{10... | collective-permute-start | bytes 589832 | tf_op jit(solution)/shard_map/last_y1/ppermute | solution.py:20
  49.3 5.3 %collective-permute-done.9.refs_6_.refs_28_ = bf16[1,2,48,1024]{3,2,1,0:T(8,128)(2,1)} collective-permute-done((bf16[1,2,48,1024]{3,2,1,0:T(8,128)(2,1)}, bf16[1,2,48,1024]{3,2,1,0:T(8,128)(2,1)}, u32[]{:S(2)}, u32[]{:S(2)}) %collective-permute-start.9) | collective-permute-done | bytes 196640 | tf_op jit(solution)/shard_map/last_z/ppermute | solution.py:15
  54.6 2.5 %collective-permute-done.11.refs_5_.refs_27_ = bf16[1,2,48,1024]{3,2,1,0:T(8,128)(2,1)S(1)} collective-permute-done((bf16[1,2,48,1024]{3,2,1,0:T(8,128)(2,1)S(1)}, bf16[1,2,48,1024]{3,2,1,0:T(8,128)(2,1)S(1)}, u32[]{:S(2)}, u32[]{:S(2)}) %collective-permute-start.11) | collective-permute-done | bytes 196640 | tf_op jit(solution)/shard_map/back_d/ppermute | solution.py:15
  57.0 1.0 %collective-permute-start.12 = (bf16[1,2,48,1024]{3,2,1,0:T(8,128)(2,1)}, bf16[1,2,48,1024]{3,2,1,0:T(8,128)(2,1)}, u32[]{:S(2)}, u32[]{:S(2)}) collective-permute-start(bf16[1,2,48,1024]{3,2,1,0:T(8,128)(2,1)} %collective-permute-done.9.refs_6_.refs_28_), channel_id=1, source_target_pairs={{0,1},{1,0},{2,3},{3,2},{4,5},{5,4},{6,7},{7,6},{8,9},{9,8},{10,11... | collective-permute-start | bytes 589832 | tf_op jit(solution)/shard_map/last_d/ppermute | solution.py:15
  58.1 0.8 copy-done.5
  58.9 1.0 %collective-permute-start.7 = (bf16[1,2,48,1024]{3,2,1,0:T(8,128)(2,1)}, bf16[1,2,48,1024]{3,2,1,0:T(8,128)(2,1)}, u32[]{:S(2)}, u32[]{:S(2)}) collective-permute-start(bf16[1,2,48,1024]{3,2,1,0:T(8,128)(2,1)} %collective-permute-done.3.refs_2_.refs_8_.refs_24_), channel_id=1, source_target_pairs={{0,1},{1,0},{2,3},{3,2},{4,5},{5,4},{6,7},{7,6},{8,9},{9,8},{10,11... | collective-permute-start | bytes 589832 | tf_op jit(solution)/shard_map/last_x/ppermute | solution.py:15
  59.9 3.1 %cross_far.5 = bf16[2,144,384]{2,1,0:T(8,128)(2,1)} custom-call(s32[1]{0:T(128)} %bitcast.place_ref, bf16[3,2,48,1024]{3,2,1,0:T(8,128)(2,1)} %get-tuple-element.36.refs_0_.refs_8_.refs_11_.refs_19_.refs_22_.refs_30_, bf16[3,2,48,1024]{3,2,1,0:T(8,128)(2,1)} %collective-permute-done.1.refs_1_.refs_12_.refs_23_, bf16[2,2,48,1024]{3,2,1,0:T(8,128)(2,1)} %copy-done.1, ...), custom_call_target="tpu_custom_call" | custom-call | flops 1 | bytes 1 | tf_op jit(solution)/shard_map/cross_far/pallas_call | solution.py:185
  63.0 1.6 %collective-permute-start.21 = (bf16[2,144,384]{2,1,0:T(8,128)(2,1)}, bf16[2,144,384]{2,1,0:T(8,128)(2,1)}, u32[]{:S(2)}, u32[]{:S(2)}) collective-permute-start(bf16[2,144,384]{2,1,0:T(8,128)(2,1)} %cross_far.5), channel_id=1, source_target_pairs={{0,4},{1,5},{2,6},{3,7},{4,0},{5,1},{6,2},{7,3},{8,12},{9,13},{10,... | collective-permute-start | bytes 663560 | tf_op jit(solution)/shard_map/came1/ppermute | solution.py:15
  64.6 3.1 %cross_far.4 = bf16[2,144,384]{2,1,0:T(8,128)(2,1)} custom-call(s32[1]{0:T(128)} %bitcast.place_ref, bf16[3,2,48,1024]{3,2,1,0:T(8,128)(2,1)} %get-tuple-element.36.refs_0_.refs_8_.refs_11_.refs_19_.refs_22_.refs_30_, bf16[3,2,48,1024]{3,2,1,0:T(8,128)(2,1)} %collective-permute-done.1.refs_1_.refs_12_.refs_23_, bf16[2,2,48,1024]{3,2,1,0:T(8,128)(2,1)} %copy-done.1, ...), custom_call_target="tpu_custom_call" | custom-call | flops 1 | bytes 1 | tf_op jit(solution)/shard_map/cross_far/pallas_call | solution.py:185
  67.7 1.5 %collective-permute-start.20 = (bf16[2,144,384]{2,1,0:T(8,128)(2,1)}, bf16[2,144,384]{2,1,0:T(8,128)(2,1)}, u32[]{:S(2)}, u32[]{:S(2)}) collective-permute-start(bf16[2,144,384]{2,1,0:T(8,128)(2,1)} %cross_far.4), channel_id=1, source_target_pairs={{0,4},{1,5},{2,6},{3,7},{4,0},{5,1},{6,2},{7,3},{8,12},{9,13},{10,... | collective-permute-start | bytes 663560 | tf_op jit(solution)/shard_map/came0/ppermute | solution.py:15
  69.2 3.1 %cross_far.3 = bf16[2,144,384]{2,1,0:T(8,128)(2,1)} custom-call(s32[1]{0:T(128)} %bitcast.place_ref, bf16[3,2,48,1024]{3,2,1,0:T(8,128)(2,1)} %get-tuple-element.36.refs_0_.refs_8_.refs_11_.refs_19_.refs_22_.refs_30_, bf16[3,2,48,1024]{3,2,1,0:T(8,128)(2,1)} %collective-permute-done.1.refs_1_.refs_12_.refs_23_, ...), custom_call_target="tpu_custom_call" | custom-call | flops 1 | bytes 1 | tf_op jit(solution)/shard_map/cross_far/pallas_call | solution.py:185
  72.3 1.2 %collective-permute-start.19 = (bf16[2,144,384]{2,1,0:T(8,128)(2,1)}, bf16[2,144,384]{2,1,0:T(8,128)(2,1)}, u32[]{:S(2)}, u32[]{:S(2)}) collective-permute-start(bf16[2,144,384]{2,1,0:T(8,128)(2,1)} %cross_far.3), channel_id=1, source_target_pairs={{0,2},{1,3},{2,0},{3,1},{4,6},{5,7},{6,4},{7,5},{8,10},{9,11},{10,... | collective-permute-start | bytes 663560 | tf_op jit(solution)/shard_map/came2/ppermute | solution.py:15
  73.4 5.5 %cross_near.1.refs_2_ = f32[6,2,144,384]{3,2,1,0:T(8,128)} custom-call(s32[1]{0:T(128)} %bitcast.place_ref, bf16[3,2,48,1024]{3,2,1,0:T(8,128)(2,1)} %get-tuple-element.36.refs_0_.refs_8_.refs_11_.refs_19_.refs_22_.refs_30_, bf16[3,2,48,1024]{3,2,1,0:T(8,128)(2,1)} %collective-permute-done.1.refs_1_.refs_12_.refs_23_, bf16[2,2,48,1024]{3,2,1,0:T(8,128)(2,1)} %copy-done.1, ...), custom_call_target="tpu_custom_call" | custom-call | flops 1 | bytes 1 | tf_op jit(solution)/shard_map/cross_near/pallas_call | solution.py:185
  79.3 2.9 %collective-permute-done.20.refs_0_ = bf16[2,144,384]{2,1,0:T(8,128)(2,1)} collective-permute-done((bf16[2,144,384]{2,1,0:T(8,128)(2,1)}, bf16[2,144,384]{2,1,0:T(8,128)(2,1)}, u32[]{:S(2)}, u32[]{:S(2)}) %collective-permute-start.20) | collective-permute-done | bytes 221216 | tf_op jit(solution)/shard_map/came0/ppermute | solution.py:15
  82.2 1.9 %place.2.refs_1_ = f32[6,2,144,384]{3,2,1,0:T(8,128)} custom-call(s32[1]{0:T(128)} %bitcast.place_ref, bf16[2,144,384]{2,1,0:T(8,128)(2,1)} %collective-permute-done.20.refs_0_, bf16[2,144,384]{2,1,0:T(8,128)(2,1)} %collective-permute-done.21.refs_1_, f32[6,2,144,384]{3,2,1,0:T(8,128)} %cross_near.1.refs_2_), custom_call_target="tpu_custom_call", output_to_operand_aliasing={{}: (3, {})} | custom-call | flops 1 | bytes 1 | tf_op jit(solution)/shard_map/place/pallas_call | solution.py:229
  84.1 1.7 %place.3 = f32[6,2,144,384]{3,2,1,0:T(8,128)} custom-call(s32[1]{0:T(128)} %bitcast.place_ref, bf16[2,144,384]{2,1,0:T(8,128)(2,1)} %collective-permute-done.19.refs_0_, f32[6,2,144,384]{3,2,1,0:T(8,128)} %place.2.refs_1_), custom_call_target="tpu_custom_call", output_to_operand_aliasing={{}: (2, {})} | custom-call | flops 1 | bytes 1 | tf_op jit(solution)/shard_map/place/pallas_call | solution.py:229
  (43 shorter events, 1.5 us)
Async XLA Ops:
  2.7 20.7 %collective-permute-start.2 = (bf16[2,2,48,1024]{3,2,1,0:T(8,128)(2,1)}, bf16[2,2,48,1024]{3,2,1,0:T(8,128)(2,1)S(1)}, u32[]{:S(2)}, u32[]{:S(2)}) collective-permute-start(bf16[2,2,48,1024]{3,2,1,0:T(8,128)(2,1)} %get-tuple-element.42), channel_id=1, source_target_pairs={{0,2},{1,3},{2,0},{3,1},{4,6},{5,7},{6,4},{7,5},{8,10},{9,11},{10,... | collective-permute-start | bytes 1179656 | tf_op jit(solution)/shard_map/front_z/ppermute | solution.py:15
  5.8 20.3 %collective-permute-start = (bf16[2,2,48,1024]{3,2,1,0:T(8,128)(2,1)}, bf16[2,2,48,1024]{3,2,1,0:T(8,128)(2,1)S(1)}, u32[]{:S(2)}, u32[]{:S(2)}) collective-permute-start(bf16[2,2,48,1024]{3,2,1,0:T(8,128)(2,1)} %get-tuple-element.38), channel_id=1, source_target_pairs={{0,4},{1,5},{2,6},{3,7},{4,0},{5,1},{6,2},{7,3},{8,12},{9,13},{10,... | collective-permute-start | bytes 1179656 | tf_op jit(solution)/shard_map/got/ppermute | solution.py:15
  8.4 21.8 %collective-permute-start.1 = (bf16[3,2,48,1024]{3,2,1,0:T(8,128)(2,1)}, bf16[3,2,48,1024]{3,2,1,0:T(8,128)(2,1)}, u32[]{:S(2)}, u32[]{:S(2)}) collective-permute-start(bf16[3,2,48,1024]{3,2,1,0:T(8,128)(2,1)} %get-tuple-element.36.refs_0_.refs_8_.refs_11_.refs_19_.refs_22_.refs_30_), channel_id=1, source_target_pairs={{0,1},{1,0},{2,3},{3,2},{4,5},{5,4},{6,7},{7,6},{8,9},{9,8},{10,11... | collective-permute-start | bytes 1769480 | tf_op jit(solution)/shard_map/own_x/ppermute | solution.py:15
  9.9 21.7 %collective-permute-start.13 = (bf16[3,2,48,1024]{3,2,1,0:T(8,128)(2,1)}, bf16[3,2,48,1024]{3,2,1,0:T(8,128)(2,1)S(1)}, u32[]{:S(2)}, u32[]{:S(2)}) collective-permute-start(bf16[3,2,48,1024]{3,2,1,0:T(8,128)(2,1)} %get-tuple-element.36.refs_0_.refs_8_.refs_11_.refs_19_.refs_22_.refs_30_), channel_id=1, source_target_pairs={{0,24},{8,0},{16,8},{24,16},{1,25},{9,1},{17,9},{25,17},{2,26},{10... | collective-permute-start | bytes 1769480 | tf_op jit(solution)/shard_map/own_y1/ppermute | solution.py:20
  10.0 24.8 %collective-permute-start.16 = (bf16[3,2,48,1024]{3,2,1,0:T(8,128)(2,1)}, bf16[3,2,48,1024]{3,2,1,0:T(8,128)(2,1)S(1)}, u32[]{:S(2)}, u32[]{:S(2)}) collective-permute-start(bf16[3,2,48,1024]{3,2,1,0:T(8,128)(2,1)} %get-tuple-element.36.refs_0_.refs_8_.refs_11_.refs_19_.refs_22_.refs_30_), channel_id=1, source_target_pairs={{0,16},{8,24},{16,0},{24,8},{1,17},{9,25},{17,1},{25,9},{2,18},{10... | collective-permute-start | bytes 1769480 | tf_op jit(solution)/shard_map/own_y2/ppermute | solution.py:20
  23.4 23.4 %copy-start.1 = (bf16[2,2,48,1024]{3,2,1,0:T(8,128)(2,1)}, bf16[2,2,48,1024]{3,2,1,0:T(8,128)(2,1)S(1)}, u32[]{:S(2)}) copy-start(bf16[2,2,48,1024]{3,2,1,0:T(8,128)(2,1)S(1)} %collective-permute-done.2.refs_2_.refs_13_) | copy-start | bytes 1179652
  23.4 6.6 %collective-permute-start.3 = (bf16[1,2,48,1024]{3,2,1,0:T(8,128)(2,1)}, bf16[1,2,48,1024]{3,2,1,0:T(8,128)(2,1)}, u32[]{:S(2)}, u32[]{:S(2)}) collective-permute-start(bf16[1,2,48,1024]{3,2,1,0:T(8,128)(2,1)} %get-tuple-element.43), channel_id=1, source_target_pairs={{0,2},{1,3},{2,0},{3,1},{4,6},{5,7},{6,4},{7,5},{8,10},{9,11},{10,... | collective-permute-start | bytes 589832 | tf_op jit(solution)/shard_map/last/ppermute | solution.py:15
  26.0 10.4 %copy-start = (bf16[2,2,48,1024]{3,2,1,0:T(8,128)(2,1)}, bf16[2,2,48,1024]{3,2,1,0:T(8,128)(2,1)S(1)}, u32[]{:S(2)}) copy-start(bf16[2,2,48,1024]{3,2,1,0:T(8,128)(2,1)S(1)} %collective-permute-done.refs_4_.refs_8_.refs_15_) | copy-start | bytes 1179652
  26.0 10.4 %collective-permute-start.5 = (bf16[2,2,48,1024]{3,2,1,0:T(8,128)(2,1)S(1)}, bf16[2,2,48,1024]{3,2,1,0:T(8,128)(2,1)S(1)}, u32[]{:S(2)}, u32[]{:S(2)}) collective-permute-start(bf16[2,2,48,1024]{3,2,1,0:T(8,128)(2,1)S(1)} %collective-permute-done.2.refs_2_.refs_13_), channel_id=1, source_target_pairs={{0,1},{1,0},{2,3},{3,2},{4,5},{5,4},{6,7},{7,6},{8,9},{9,8},{10,11... | collective-permute-start | bytes 1179656 | tf_op jit(solution)/shard_map/front_d/ppermute | solution.py:15
  30.0 13.8 %collective-permute-start.4 = (bf16[2,2,48,1024]{3,2,1,0:T(8,128)(2,1)S(1)}, bf16[2,2,48,1024]{3,2,1,0:T(8,128)(2,1)S(1)}, u32[]{:S(2)}, u32[]{:S(2)}) collective-permute-start(bf16[2,2,48,1024]{3,2,1,0:T(8,128)(2,1)S(1)} %collective-permute-done.refs_4_.refs_8_.refs_15_), channel_id=1, source_target_pairs={{0,2},{1,3},{2,0},{3,1},{4,6},{5,7},{6,4},{7,5},{8,10},{9,11},{10,... | collective-permute-start | bytes 1179656 | tf_op jit(solution)/shard_map/got_z/ppermute | solution.py:15
  30.2 16.0 %collective-permute-start.10 = (bf16[2,2,48,1024]{3,2,1,0:T(8,128)(2,1)S(1)}, bf16[2,2,48,1024]{3,2,1,0:T(8,128)(2,1)S(1)}, u32[]{:S(2)}, u32[]{:S(2)}) collective-permute-start(bf16[2,2,48,1024]{3,2,1,0:T(8,128)(2,1)S(1)} %collective-permute-done.refs_4_.refs_8_.refs_15_), channel_id=1, source_target_pairs={{0,1},{1,0},{2,3},{3,2},{4,5},{5,4},{6,7},{7,6},{8,9},{9,8},{10,11... | collective-permute-start | bytes 1179656 | tf_op jit(solution)/shard_map/got_x/ppermute | solution.py:15
  31.6 4.9 %copy-start.6 = (bf16[3,2,48,1024]{3,2,1,0:T(8,128)(2,1)}, bf16[3,2,48,1024]{3,2,1,0:T(8,128)(2,1)S(1)}, u32[]{:S(2)}) copy-start(bf16[3,2,48,1024]{3,2,1,0:T(8,128)(2,1)S(1)} %collective-permute-done.13.refs_9_.refs_20_.refs_31_) | copy-start | bytes 1769476
  31.6 13.3 %collective-permute-start.8 = (bf16[1,2,48,1024]{3,2,1,0:T(8,128)(2,1)}, bf16[1,2,48,1024]{3,2,1,0:T(8,128)(2,1)S(1)}, u32[]{:S(2)}, u32[]{:S(2)}) collective-permute-start(bf16[1,2,48,1024]{3,2,1,0:T(8,128)(2,1)} %get-tuple-element.48), channel_id=1, source_target_pairs={{0,4},{1,5},{2,6},{3,7},{4,0},{5,1},{6,2},{7,3},{8,12},{9,13},{10,... | collective-permute-start | bytes 589832 | tf_op jit(solution)/shard_map/back_z/ppermute | solution.py:15
  34.8 23.3 %copy-start.7 = (bf16[3,2,48,1024]{3,2,1,0:T(8,128)(2,1)}, bf16[3,2,48,1024]{3,2,1,0:T(8,128)(2,1)S(1)}, u32[]{:S(2)}) copy-start(bf16[3,2,48,1024]{3,2,1,0:T(8,128)(2,1)S(1)} %collective-permute-done.16.refs_10_.refs_21_.refs_32_) | copy-start | bytes 1769476
  34.8 11.9 %collective-permute-start.17 = (bf16[2,2,48,1024]{3,2,1,0:T(8,128)(2,1)S(1)}, bf16[2,2,48,1024]{3,2,1,0:T(8,128)(2,1)S(1)}, u32[]{:S(2)}, u32[]{:S(2)}) collective-permute-start(bf16[2,2,48,1024]{3,2,1,0:T(8,128)(2,1)S(1)} %collective-permute-done.refs_4_.refs_8_.refs_15_), channel_id=1, source_target_pairs={{0,16},{8,24},{16,0},{24,8},{1,17},{9,25},{17,1},{25,9},{2,18},{10... | collective-permute-start | bytes 1179656 | tf_op jit(solution)/shard_map/got_y2/ppermute | solution.py:20
  36.5 11.9 %copy-start.2 = (bf16[2,2,48,1024]{3,2,1,0:T(8,128)(2,1)}, bf16[2,2,48,1024]{3,2,1,0:T(8,128)(2,1)S(1)}, u32[]{:S(2)}) copy-start(bf16[2,2,48,1024]{3,2,1,0:T(8,128)(2,1)S(1)} %collective-permute-done.5.refs_3_.refs_14_) | copy-start | bytes 1179652
  36.5 10.4 %collective-permute-start.14 = (bf16[2,2,48,1024]{3,2,1,0:T(8,128)(2,1)S(1)}, bf16[2,2,48,1024]{3,2,1,0:T(8,128)(2,1)S(1)}, u32[]{:S(2)}, u32[]{:S(2)}) collective-permute-start(bf16[2,2,48,1024]{3,2,1,0:T(8,128)(2,1)S(1)} %collective-permute-done.refs_4_.refs_8_.refs_15_), channel_id=1, source_target_pairs={{0,24},{8,0},{16,8},{24,16},{1,25},{9,1},{17,9},{25,17},{2,26},{10... | collective-permute-start | bytes 1179656 | tf_op jit(solution)/shard_map/got_y1/ppermute | solution.py:20
  43.9 5.4 %copy-start.3 = (bf16[2,2,48,1024]{3,2,1,0:T(8,128)(2,1)}, bf16[2,2,48,1024]{3,2,1,0:T(8,128)(2,1)S(1)}, u32[]{:S(2)}) copy-start(bf16[2,2,48,1024]{3,2,1,0:T(8,128)(2,1)S(1)} %collective-permute-done.4.refs_6_.refs_17_) | copy-start | bytes 1179652
  43.9 14.2 %collective-permute-start.6 = (bf16[2,2,48,1024]{3,2,1,0:T(8,128)(2,1)S(1)}, bf16[2,2,48,1024]{3,2,1,0:T(8,128)(2,1)S(1)}, u32[]{:S(2)}, u32[]{:S(2)}) collective-permute-start(bf16[2,2,48,1024]{3,2,1,0:T(8,128)(2,1)S(1)} %collective-permute-done.4.refs_6_.refs_17_), channel_id=1, source_target_pairs={{0,1},{1,0},{2,3},{3,2},{4,5},{5,4},{6,7},{7,6},{8,9},{9,8},{10,11... | collective-permute-start | bytes 1179656 | tf_op jit(solution)/shard_map/got_d/ppermute | solution.py:15
  44.9 13.2 %copy-start.10 = (bf16[1,2,48,1024]{3,2,1,0:T(8,128)(2,1)}, bf16[1,2,48,1024]{3,2,1,0:T(8,128)(2,1)S(1)}, u32[]{:S(2)}) copy-start(bf16[1,2,48,1024]{3,2,1,0:T(8,128)(2,1)S(1)} %collective-permute-done.8.refs_4_.refs_26_) | copy-start | bytes 589828
  44.9 9.7 %collective-permute-start.9 = (bf16[1,2,48,1024]{3,2,1,0:T(8,128)(2,1)}, bf16[1,2,48,1024]{3,2,1,0:T(8,128)(2,1)}, u32[]{:S(2)}, u32[]{:S(2)}) collective-permute-start(bf16[1,2,48,1024]{3,2,1,0:T(8,128)(2,1)} %collective-permute-done.3.refs_2_.refs_8_.refs_24_), channel_id=1, source_target_pairs={{0,4},{1,5},{2,6},{3,7},{4,0},{5,1},{6,2},{7,3},{8,12},{9,13},{10,... | collective-permute-start | bytes 589832 | tf_op jit(solution)/shard_map/last_z/ppermute | solution.py:15
  46.2 11.9 %copy-start.4 = (bf16[2,2,48,1024]{3,2,1,0:T(8,128)(2,1)}, bf16[2,2,48,1024]{3,2,1,0:T(8,128)(2,1)S(1)}, u32[]{:S(2)}) copy-start(bf16[2,2,48,1024]{3,2,1,0:T(8,128)(2,1)S(1)} %collective-permute-done.10.refs_5_.refs_16_) | copy-start | bytes 1179652
  46.2 10.9 %collective-permute-start.11 = (bf16[1,2,48,1024]{3,2,1,0:T(8,128)(2,1)S(1)}, bf16[1,2,48,1024]{3,2,1,0:T(8,128)(2,1)S(1)}, u32[]{:S(2)}, u32[]{:S(2)}) collective-permute-start(bf16[1,2,48,1024]{3,2,1,0:T(8,128)(2,1)S(1)} %collective-permute-done.8.refs_4_.refs_26_), channel_id=1, source_target_pairs={{0,1},{1,0},{2,3},{3,2},{4,5},{5,4},{6,7},{7,6},{8,9},{9,8},{10,11... | collective-permute-start | bytes 589832 | tf_op jit(solution)/shard_map/back_d/ppermute | solution.py:15
  46.7 11.4 %copy-start.8 = (bf16[2,2,48,1024]{3,2,1,0:T(8,128)(2,1)}, bf16[2,2,48,1024]{3,2,1,0:T(8,128)(2,1)S(1)}, u32[]{:S(2)}) copy-start(bf16[2,2,48,1024]{3,2,1,0:T(8,128)(2,1)S(1)} %collective-permute-done.17.refs_10_) | copy-start | bytes 1179652
  46.9 11.2 %copy-start.9 = (bf16[2,2,48,1024]{3,2,1,0:T(8,128)(2,1)}, bf16[2,2,48,1024]{3,2,1,0:T(8,128)(2,1)S(1)}, u32[]{:S(2)}) copy-start(bf16[2,2,48,1024]{3,2,1,0:T(8,128)(2,1)S(1)} %collective-permute-done.14.refs_9_) | copy-start | bytes 1179652
  46.9 20.8 %collective-permute-start.18 = (bf16[1,2,48,1024]{3,2,1,0:T(8,128)(2,1)}, bf16[1,2,48,1024]{3,2,1,0:T(8,128)(2,1)}, u32[]{:S(2)}, u32[]{:S(2)}) collective-permute-start(bf16[1,2,48,1024]{3,2,1,0:T(8,128)(2,1)} %collective-permute-done.3.refs_2_.refs_8_.refs_24_), channel_id=1, source_target_pairs={{0,16},{8,24},{16,0},{24,8},{1,17},{9,25},{17,1},{25,9},{2,18},{10... | collective-permute-start | bytes 589832 | tf_op jit(solution)/shard_map/last_y2/ppermute | solution.py:20
  48.3 20.8 %collective-permute-start.15 = (bf16[1,2,48,1024]{3,2,1,0:T(8,128)(2,1)}, bf16[1,2,48,1024]{3,2,1,0:T(8,128)(2,1)}, u32[]{:S(2)}, u32[]{:S(2)}) collective-permute-start(bf16[1,2,48,1024]{3,2,1,0:T(8,128)(2,1)} %collective-permute-done.3.refs_2_.refs_8_.refs_24_), channel_id=1, source_target_pairs={{0,24},{8,0},{16,8},{24,16},{1,25},{9,1},{17,9},{25,17},{2,26},{10... | collective-permute-start | bytes 589832 | tf_op jit(solution)/shard_map/last_y1/ppermute | solution.py:20
  57.0 12.1 %collective-permute-start.12 = (bf16[1,2,48,1024]{3,2,1,0:T(8,128)(2,1)}, bf16[1,2,48,1024]{3,2,1,0:T(8,128)(2,1)}, u32[]{:S(2)}, u32[]{:S(2)}) collective-permute-start(bf16[1,2,48,1024]{3,2,1,0:T(8,128)(2,1)} %collective-permute-done.9.refs_6_.refs_28_), channel_id=1, source_target_pairs={{0,1},{1,0},{2,3},{3,2},{4,5},{5,4},{6,7},{7,6},{8,9},{9,8},{10,11... | collective-permute-start | bytes 589832 | tf_op jit(solution)/shard_map/last_d/ppermute | solution.py:15
  58.9 10.3 %collective-permute-start.7 = (bf16[1,2,48,1024]{3,2,1,0:T(8,128)(2,1)}, bf16[1,2,48,1024]{3,2,1,0:T(8,128)(2,1)}, u32[]{:S(2)}, u32[]{:S(2)}) collective-permute-start(bf16[1,2,48,1024]{3,2,1,0:T(8,128)(2,1)} %collective-permute-done.3.refs_2_.refs_8_.refs_24_), channel_id=1, source_target_pairs={{0,1},{1,0},{2,3},{3,2},{4,5},{5,4},{6,7},{7,6},{8,9},{9,8},{10,11... | collective-permute-start | bytes 589832 | tf_op jit(solution)/shard_map/last_x/ppermute | solution.py:15
  63.0 16.3 %collective-permute-start.21 = (bf16[2,144,384]{2,1,0:T(8,128)(2,1)}, bf16[2,144,384]{2,1,0:T(8,128)(2,1)}, u32[]{:S(2)}, u32[]{:S(2)}) collective-permute-start(bf16[2,144,384]{2,1,0:T(8,128)(2,1)} %cross_far.5), channel_id=1, source_target_pairs={{0,4},{1,5},{2,6},{3,7},{4,0},{5,1},{6,2},{7,3},{8,12},{9,13},{10,... | collective-permute-start | bytes 663560 | tf_op jit(solution)/shard_map/came1/ppermute | solution.py:15
  67.7 14.5 %collective-permute-start.20 = (bf16[2,144,384]{2,1,0:T(8,128)(2,1)}, bf16[2,144,384]{2,1,0:T(8,128)(2,1)}, u32[]{:S(2)}, u32[]{:S(2)}) collective-permute-start(bf16[2,144,384]{2,1,0:T(8,128)(2,1)} %cross_far.4), channel_id=1, source_target_pairs={{0,4},{1,5},{2,6},{3,7},{4,0},{5,1},{6,2},{7,3},{8,12},{9,13},{10,... | collective-permute-start | bytes 663560 | tf_op jit(solution)/shard_map/came0/ppermute | solution.py:15
  72.3 11.8 %collective-permute-start.19 = (bf16[2,144,384]{2,1,0:T(8,128)(2,1)}, bf16[2,144,384]{2,1,0:T(8,128)(2,1)}, u32[]{:S(2)}, u32[]{:S(2)}) collective-permute-start(bf16[2,144,384]{2,1,0:T(8,128)(2,1)} %cross_far.3), channel_id=1, source_target_pairs={{0,2},{1,3},{2,0},{3,1},{4,6},{5,7},{6,4},{7,5},{8,10},{9,11},{10,... | collective-permute-start | bytes 663560 | tf_op jit(solution)/shard_map/came2/ppermute | solution.py:15
  (2 other events, 1.8 us)

commit v4 on v3

--- a/solution.py
+++ b/solution.py
@@ -7,7 +7,7 @@
 from jax.experimental.pallas import tpu as pltpu
 from jax.sharding import PartitionSpec as P
 
-VMEM_BYTES = 64 * 1024 * 1024 - 65536
+VMEM_BYTES = 32 * 1024 * 1024
 
 
 def moved_by_xor(value, axis, bits):

time: 86.2 us -> 83.6 us (0.970)
  waiting for transfers between devices: 35.8 us -> 32.7 us
  Pallas kernels: 21.2 us -> 18.8 us
  local copies, waits for them, and re-layouts: 0.81 us -> 2.59 us
  starting transfers between devices: 27.9 us -> 29.1 us
    ppermute x16, waiting for transfers between devices: 35.7 us -> 32.6 us  [moved_by_xor(): lax.ppermute(value, axis, [(source, source ^ bits) for source in range(co...]
    pallas_call x1, Pallas kernels: 2.72 us -> 0.71 us  [whiten(): pl.pallas_call(functools.partial(whiten_kernel, plan, splits), grid_spec=...]
    unnamed x24 -> x4, local copies, waits for them, and re-layouts: 0.81 us -> 2.59 us
    ppermute x16, starting transfers between devices: 22.4 us -> 23.7 us  [moved_by_xor(): lax.ppermute(value, axis, [(source, source ^ bits) for source in range(co...]
    pallas_call x2, Pallas kernels: 3.65 us -> 2.61 us  [place_blocks(): pl.pallas_call(functools.partial(place_kernel, pairs), grid_spec=pltpu.Pr...]
  transfers between devices with their start and end apart: 22 -> 22, of which waited for: 10 -> 9; matrix products, arithmetic and copies ran while one was open for 0% -> 0% of each run, Pallas kernels for 19% -> 20%
where the time goes in v4:
time: 83.6 us; the launch traced here: 83.4 us
  waiting for transfers between devices  32.7 us (39%)
  starting transfers between devices  29.1 us (35%)
  Pallas kernels  18.8 us (22%)
  local copies, waits for them, and re-layouts  2.59 us (3%)
    ppermute x16, waiting for transfers between devices, moved_by_xor(): lax.ppermute(value, axis, [(source, source ^ bits) for source in range(co...  32.6 us
    ppermute x16, starting transfers between devices, moved_by_xor(): lax.ppermute(value, axis, [(source, source ^ bits) for source in range(co...  23.7 us
    pallas_call x4, Pallas kernels, cross(): pl.pallas_call(functools.partial(cross_kernel, plan), grid_spec=pltpu.Pre...  15.5 us
    ppermute x6, starting transfers between devices, moved_by_shift(): lax.ppermute(value, axis, [(source, (source + steps) % count) for source...  5.47 us
    pallas_call x2, Pallas kernels, place_blocks(): pl.pallas_call(functools.partial(place_kernel, pairs), grid_spec=pltpu.Pr...  2.61 us
    unnamed x4, local copies, waits for them, and re-layouts  2.59 us
  transfers between devices with their start and end apart: 22, of which 9 were waited for; matrix products, arithmetic and copies ran while one was open for 0% of the time, Pallas kernels for 20%

profile of v4, /device:TPU:0, one launch (start us, length us, event | category | flops | bytes accessed | tf_op | source)
XLA Modules:
  0.0 83.4 jit_solution(5406160087570452814)
XLA Ops:
  0.0 1.7 %copy-done = f32[6,2,48,1024]{3,2,1,0:T(8,128)S(1)} copy-done((f32[6,2,48,1024]{3,2,1,0:T(8,128)S(1)}, f32[6,2,48,1024]{3,2,1,0:T(8,128)}, u32[]{:S(2)}) %copy-start) | copy-done | bytes 2359320
  1.7 0.9 %copy-done.1 = s32[48,1024]{1,0:T(8,128)S(1)} copy-done((s32[48,1024]{1,0:T(8,128)S(1)}, s32[48,1024]{1,0:T(8,128)}, u32[]{:S(2)}) %copy-start.1) | copy-done | bytes 196632
  3.3 3.1 %collective-permute-start.2 = (bf16[2,2,48,1024]{3,2,1,0:T(8,128)(2,1)S(1)}, bf16[2,2,48,1024]{3,2,1,0:T(8,128)(2,1)S(1)}, u32[]{:S(2)}, u32[]{:S(2)}) collective-permute-start(bf16[2,2,48,1024]{3,2,1,0:T(8,128)(2,1)S(1)} %get-tuple-element.42), channel_id=1, source_target_pairs={{0,2},{1,3},{2,0},{3,1},{4,6},{5,7},{6,4},{7,5},{8,10},{9,11},{10,... | collective-permute-start | bytes 1179656 | tf_op jit(solution)/shard_map/front_z/ppermute | solution.py:15
  6.4 2.6 %collective-permute-start = (bf16[2,2,48,1024]{3,2,1,0:T(8,128)(2,1)S(1)}, bf16[2,2,48,1024]{3,2,1,0:T(8,128)(2,1)S(1)}, u32[]{:S(2)}, u32[]{:S(2)}) collective-permute-start(bf16[2,2,48,1024]{3,2,1,0:T(8,128)(2,1)S(1)} %get-tuple-element.38), channel_id=1, source_target_pairs={{0,4},{1,5},{2,6},{3,7},{4,0},{5,1},{6,2},{7,3},{8,12},{9,13},{10,... | collective-permute-start | bytes 1179656 | tf_op jit(solution)/shard_map/got/ppermute | solution.py:15
  9.0 1.5 %collective-permute-start.1 = (bf16[3,2,48,1024]{3,2,1,0:T(8,128)(2,1)S(1)}, bf16[3,2,48,1024]{3,2,1,0:T(8,128)(2,1)S(1)}, u32[]{:S(2)}, u32[]{:S(2)}) collective-permute-start(bf16[3,2,48,1024]{3,2,1,0:T(8,128)(2,1)S(1)} %get-tuple-element.36.refs_0_.refs_8_.refs_11_.refs_19_.refs_22_.refs_30_), channel_id=1, source_target_pairs={{0,1},{1,0},{2,3},{3,2},{4,5},{5,4},{6,7},{7,6},{8,9},{9,8},{10,11... | collective-permute-start | bytes 1769480 | tf_op jit(solution)/shard_map/own_x/ppermute | solution.py:15
  10.6 1.4 %collective-permute-start.16 = (bf16[3,2,48,1024]{3,2,1,0:T(8,128)(2,1)S(1)}, bf16[3,2,48,1024]{3,2,1,0:T(8,128)(2,1)S(1)}, u32[]{:S(2)}, u32[]{:S(2)}) collective-permute-start(bf16[3,2,48,1024]{3,2,1,0:T(8,128)(2,1)S(1)} %get-tuple-element.36.refs_0_.refs_8_.refs_11_.refs_19_.refs_22_.refs_30_), channel_id=1, source_target_pairs={{0,16},{8,24},{16,0},{24,8},{1,17},{9,25},{17,1},{25,9},{2,18},{10... | collective-permute-start | bytes 1769480 | tf_op jit(solution)/shard_map/own_y2/ppermute | solution.py:20
  12.0 11.8 %collective-permute-done.2.refs_2_.refs_13_ = bf16[2,2,48,1024]{3,2,1,0:T(8,128)(2,1)S(1)} collective-permute-done((bf16[2,2,48,1024]{3,2,1,0:T(8,128)(2,1)S(1)}, bf16[2,2,48,1024]{3,2,1,0:T(8,128)(2,1)S(1)}, u32[]{:S(2)}, u32[]{:S(2)}) %collective-permute-start.2) | collective-permute-done | bytes 393248 | tf_op jit(solution)/shard_map/front_z/ppermute | solution.py:15
  23.8 2.6 %collective-permute-done.refs_4_.refs_8_.refs_15_ = bf16[2,2,48,1024]{3,2,1,0:T(8,128)(2,1)S(1)} collective-permute-done((bf16[2,2,48,1024]{3,2,1,0:T(8,128)(2,1)S(1)}, bf16[2,2,48,1024]{3,2,1,0:T(8,128)(2,1)S(1)}, u32[]{:S(2)}, u32[]{:S(2)}) %collective-permute-start) | collective-permute-done | bytes 393248 | tf_op jit(solution)/shard_map/got/ppermute | solution.py:15
  26.5 1.5 %collective-permute-start.5 = (bf16[2,2,48,1024]{3,2,1,0:T(8,128)(2,1)S(1)}, bf16[2,2,48,1024]{3,2,1,0:T(8,128)(2,1)S(1)}, u32[]{:S(2)}, u32[]{:S(2)}) collective-permute-start(bf16[2,2,48,1024]{3,2,1,0:T(8,128)(2,1)S(1)} %collective-permute-done.2.refs_2_.refs_13_), channel_id=1, source_target_pairs={{0,1},{1,0},{2,3},{3,2},{4,5},{5,4},{6,7},{7,6},{8,9},{9,8},{10,11... | collective-permute-start | bytes 1179656 | tf_op jit(solution)/shard_map/front_d/ppermute | solution.py:15
  27.9 2.1 %collective-permute-done.3.refs_2_.refs_8_.refs_24_ = bf16[1,2,48,1024]{3,2,1,0:T(8,128)(2,1)S(1)} collective-permute-done((bf16[1,2,48,1024]{3,2,1,0:T(8,128)(2,1)S(1)}, bf16[1,2,48,1024]{3,2,1,0:T(8,128)(2,1)S(1)}, u32[]{:S(2)}, u32[]{:S(2)}) %collective-permute-start.3) | collective-permute-done | bytes 196640 | tf_op jit(solution)/shard_map/last/ppermute | solution.py:15
  30.2 1.3 %collective-permute-start.10 = (bf16[2,2,48,1024]{3,2,1,0:T(8,128)(2,1)S(1)}, bf16[2,2,48,1024]{3,2,1,0:T(8,128)(2,1)S(1)}, u32[]{:S(2)}, u32[]{:S(2)}) collective-permute-start(bf16[2,2,48,1024]{3,2,1,0:T(8,128)(2,1)S(1)} %collective-permute-done.refs_4_.refs_8_.refs_15_), channel_id=1, source_target_pairs={{0,1},{1,0},{2,3},{3,2},{4,5},{5,4},{6,7},{7,6},{8,9},{9,8},{10,11... | collective-permute-start | bytes 1179656 | tf_op jit(solution)/shard_map/got_x/ppermute | solution.py:15
  31.5 3.6 %collective-permute-start.8 = (bf16[1,2,48,1024]{3,2,1,0:T(8,128)(2,1)S(1)}, bf16[1,2,48,1024]{3,2,1,0:T(8,128)(2,1)S(1)}, u32[]{:S(2)}, u32[]{:S(2)}) collective-permute-start(bf16[1,2,48,1024]{3,2,1,0:T(8,128)(2,1)S(1)} %get-tuple-element.48), channel_id=1, source_target_pairs={{0,4},{1,5},{2,6},{3,7},{4,0},{5,1},{6,2},{7,3},{8,12},{9,13},{10,... | collective-permute-start | bytes 589832 | tf_op jit(solution)/shard_map/back_z/ppermute | solution.py:15
  35.1 1.5 %collective-permute-start.17 = (bf16[2,2,48,1024]{3,2,1,0:T(8,128)(2,1)S(1)}, bf16[2,2,48,1024]{3,2,1,0:T(8,128)(2,1)S(1)}, u32[]{:S(2)}, u32[]{:S(2)}) collective-permute-start(bf16[2,2,48,1024]{3,2,1,0:T(8,128)(2,1)S(1)} %collective-permute-done.refs_4_.refs_8_.refs_15_), channel_id=1, source_target_pairs={{0,16},{8,24},{16,0},{24,8},{1,17},{9,25},{17,1},{25,9},{2,18},{10... | collective-permute-start | bytes 1179656 | tf_op jit(solution)/shard_map/got_y2/ppermute | solution.py:20
  37.3 6.4 %collective-permute-done.4.refs_6_.refs_17_ = bf16[2,2,48,1024]{3,2,1,0:T(8,128)(2,1)S(1)} collective-permute-done((bf16[2,2,48,1024]{3,2,1,0:T(8,128)(2,1)S(1)}, bf16[2,2,48,1024]{3,2,1,0:T(8,128)(2,1)S(1)}, u32[]{:S(2)}, u32[]{:S(2)}) %collective-permute-start.4) | collective-permute-done | bytes 393248 | tf_op jit(solution)/shard_map/got_z/ppermute | solution.py:15
  43.7 1.0 %collective-permute-start.6 = (bf16[2,2,48,1024]{3,2,1,0:T(8,128)(2,1)S(1)}, bf16[2,2,48,1024]{3,2,1,0:T(8,128)(2,1)S(1)}, u32[]{:S(2)}, u32[]{:S(2)}) collective-permute-start(bf16[2,2,48,1024]{3,2,1,0:T(8,128)(2,1)S(1)} %collective-permute-done.4.refs_6_.refs_17_), channel_id=1, source_target_pairs={{0,1},{1,0},{2,3},{3,2},{4,5},{5,4},{6,7},{7,6},{8,9},{9,8},{10,11... | collective-permute-start | bytes 1179656 | tf_op jit(solution)/shard_map/got_d/ppermute | solution.py:15
  44.8 1.9 %collective-permute-start.9 = (bf16[1,2,48,1024]{3,2,1,0:T(8,128)(2,1)S(1)}, bf16[1,2,48,1024]{3,2,1,0:T(8,128)(2,1)S(1)}, u32[]{:S(2)}, u32[]{:S(2)}) collective-permute-start(bf16[1,2,48,1024]{3,2,1,0:T(8,128)(2,1)S(1)} %collective-permute-done.3.refs_2_.refs_8_.refs_24_), channel_id=1, source_target_pairs={{0,4},{1,5},{2,6},{3,7},{4,0},{5,1},{6,2},{7,3},{8,12},{9,13},{10,... | collective-permute-start | bytes 589832 | tf_op jit(solution)/shard_map/last_z/ppermute | solution.py:15
  47.4 1.4 %collective-permute-start.18 = (bf16[1,2,48,1024]{3,2,1,0:T(8,128)(2,1)S(1)}, bf16[1,2,48,1024]{3,2,1,0:T(8,128)(2,1)S(1)}, u32[]{:S(2)}, u32[]{:S(2)}) collective-permute-start(bf16[1,2,48,1024]{3,2,1,0:T(8,128)(2,1)S(1)} %collective-permute-done.3.refs_2_.refs_8_.refs_24_), channel_id=1, source_target_pairs={{0,16},{8,24},{16,0},{24,8},{1,17},{9,25},{17,1},{25,9},{2,18},{10... | collective-permute-start | bytes 589832 | tf_op jit(solution)/shard_map/last_y2/ppermute | solution.py:20
  48.7 1.0 %collective-permute-start.15 = (bf16[1,2,48,1024]{3,2,1,0:T(8,128)(2,1)S(1)}, bf16[1,2,48,1024]{3,2,1,0:T(8,128)(2,1)S(1)}, u32[]{:S(2)}, u32[]{:S(2)}) collective-permute-start(bf16[1,2,48,1024]{3,2,1,0:T(8,128)(2,1)S(1)} %collective-permute-done.3.refs_2_.refs_8_.refs_24_), channel_id=1, source_target_pairs={{0,24},{8,0},{16,8},{24,16},{1,25},{9,1},{17,9},{25,17},{2,26},{10... | collective-permute-start | bytes 589832 | tf_op jit(solution)/shard_map/last_y1/ppermute | solution.py:20
  49.8 4.7 %collective-permute-done.9.refs_6_.refs_28_ = bf16[1,2,48,1024]{3,2,1,0:T(8,128)(2,1)S(1)} collective-permute-done((bf16[1,2,48,1024]{3,2,1,0:T(8,128)(2,1)S(1)}, bf16[1,2,48,1024]{3,2,1,0:T(8,128)(2,1)S(1)}, u32[]{:S(2)}, u32[]{:S(2)}) %collective-permute-start.9) | collective-permute-done | bytes 196640 | tf_op jit(solution)/shard_map/last_z/ppermute | solution.py:15
  54.5 2.8 %collective-permute-done.11.refs_5_.refs_27_ = bf16[1,2,48,1024]{3,2,1,0:T(8,128)(2,1)S(1)} collective-permute-done((bf16[1,2,48,1024]{3,2,1,0:T(8,128)(2,1)S(1)}, bf16[1,2,48,1024]{3,2,1,0:T(8,128)(2,1)S(1)}, u32[]{:S(2)}, u32[]{:S(2)}) %collective-permute-start.11) | collective-permute-done | bytes 196640 | tf_op jit(solution)/shard_map/back_d/ppermute | solution.py:15
  57.2 1.0 %collective-permute-start.12 = (bf16[1,2,48,1024]{3,2,1,0:T(8,128)(2,1)S(1)}, bf16[1,2,48,1024]{3,2,1,0:T(8,128)(2,1)S(1)}, u32[]{:S(2)}, u32[]{:S(2)}) collective-permute-start(bf16[1,2,48,1024]{3,2,1,0:T(8,128)(2,1)S(1)} %collective-permute-done.9.refs_6_.refs_28_), channel_id=1, source_target_pairs={{0,1},{1,0},{2,3},{3,2},{4,5},{5,4},{6,7},{7,6},{8,9},{9,8},{10,11... | collective-permute-start | bytes 589832 | tf_op jit(solution)/shard_map/last_d/ppermute | solution.py:15
  58.3 1.0 %collective-permute-start.7 = (bf16[1,2,48,1024]{3,2,1,0:T(8,128)(2,1)S(1)}, bf16[1,2,48,1024]{3,2,1,0:T(8,128)(2,1)S(1)}, u32[]{:S(2)}, u32[]{:S(2)}) collective-permute-start(bf16[1,2,48,1024]{3,2,1,0:T(8,128)(2,1)S(1)} %collective-permute-done.3.refs_2_.refs_8_.refs_24_), channel_id=1, source_target_pairs={{0,1},{1,0},{2,3},{3,2},{4,5},{5,4},{6,7},{7,6},{8,9},{9,8},{10,11... | collective-permute-start | bytes 589832 | tf_op jit(solution)/shard_map/last_x/ppermute | solution.py:15
  59.3 2.5 %cross_far.5 = bf16[2,144,384]{2,1,0:T(8,128)(2,1)S(1)} custom-call(s32[1]{0:T(128)} %bitcast.place_ref, bf16[3,2,48,1024]{3,2,1,0:T(8,128)(2,1)S(1)} %get-tuple-element.36.refs_0_.refs_8_.refs_11_.refs_19_.refs_22_.refs_30_, bf16[3,2,48,1024]{3,2,1,0:T(8,128)(2,1)S(1)} %collective-permute-done.1.refs_1_.refs_12_.refs_23_, ...), custom_call_target="tpu_custom_call" | custom-call | flops 1 | bytes 1 | tf_op jit(solution)/shard_map/cross_far/pallas_call | solution.py:185
  61.7 1.8 %collective-permute-start.21 = (bf16[2,144,384]{2,1,0:T(8,128)(2,1)S(1)}, bf16[2,144,384]{2,1,0:T(8,128)(2,1)S(1)}, u32[]{:S(2)}, u32[]{:S(2)}) collective-permute-start(bf16[2,144,384]{2,1,0:T(8,128)(2,1)S(1)} %cross_far.5), channel_id=1, source_target_pairs={{0,4},{1,5},{2,6},{3,7},{4,0},{5,1},{6,2},{7,3},{8,12},{9,13},{10,... | collective-permute-start | bytes 663560 | tf_op jit(solution)/shard_map/came1/ppermute | solution.py:15
  63.5 2.5 %cross_far.4 = bf16[2,144,384]{2,1,0:T(8,128)(2,1)S(1)} custom-call(s32[1]{0:T(128)} %bitcast.place_ref, bf16[3,2,48,1024]{3,2,1,0:T(8,128)(2,1)S(1)} %get-tuple-element.36.refs_0_.refs_8_.refs_11_.refs_19_.refs_22_.refs_30_, bf16[3,2,48,1024]{3,2,1,0:T(8,128)(2,1)S(1)} %collective-permute-done.1.refs_1_.refs_12_.refs_23_, ...), custom_call_target="tpu_custom_call" | custom-call | flops 1 | bytes 1 | tf_op jit(solution)/shard_map/cross_far/pallas_call | solution.py:185
  66.0 1.3 %collective-permute-start.20 = (bf16[2,144,384]{2,1,0:T(8,128)(2,1)S(1)}, bf16[2,144,384]{2,1,0:T(8,128)(2,1)S(1)}, u32[]{:S(2)}, u32[]{:S(2)}) collective-permute-start(bf16[2,144,384]{2,1,0:T(8,128)(2,1)S(1)} %cross_far.4), channel_id=1, source_target_pairs={{0,4},{1,5},{2,6},{3,7},{4,0},{5,1},{6,2},{7,3},{8,12},{9,13},{10,... | collective-permute-start | bytes 663560 | tf_op jit(solution)/shard_map/came0/ppermute | solution.py:15
  67.3 2.5 %cross_far.3 = bf16[2,144,384]{2,1,0:T(8,128)(2,1)S(1)} custom-call(s32[1]{0:T(128)} %bitcast.place_ref, bf16[3,2,48,1024]{3,2,1,0:T(8,128)(2,1)S(1)} %get-tuple-element.36.refs_0_.refs_8_.refs_11_.refs_19_.refs_22_.refs_30_, bf16[3,2,48,1024]{3,2,1,0:T(8,128)(2,1)S(1)} %collective-permute-done.1.refs_1_.refs_12_.refs_23_, ...), custom_call_target="tpu_custom_call" | custom-call | flops 1 | bytes 1 | tf_op jit(solution)/shard_map/cross_far/pallas_call | solution.py:185
  69.8 1.4 %collective-permute-start.19 = (bf16[2,144,384]{2,1,0:T(8,128)(2,1)S(1)}, bf16[2,144,384]{2,1,0:T(8,128)(2,1)S(1)}, u32[]{:S(2)}, u32[]{:S(2)}) collective-permute-start(bf16[2,144,384]{2,1,0:T(8,128)(2,1)S(1)} %cross_far.3), channel_id=1, source_target_pairs={{0,2},{1,3},{2,0},{3,1},{4,6},{5,7},{6,4},{7,5},{8,10},{9,11},{10,... | collective-permute-start | bytes 663560 | tf_op jit(solution)/shard_map/came2/ppermute | solution.py:15
  71.2 8.1 %cross_near.1.refs_2_ = f32[6,2,144,384]{3,2,1,0:T(8,128)} custom-call(s32[1]{0:T(128)} %bitcast.place_ref, bf16[3,2,48,1024]{3,2,1,0:T(8,128)(2,1)S(1)} %get-tuple-element.36.refs_0_.refs_8_.refs_11_.refs_19_.refs_22_.refs_30_, bf16[3,2,48,1024]{3,2,1,0:T(8,128)(2,1)S(1)} %collective-permute-done.1.refs_1_.refs_12_.refs_23_, ...), custom_call_target="tpu_custom_call" | custom-call | flops 1 | bytes 1 | tf_op jit(solution)/shard_map/cross_near/pallas_call | solution.py:185
  79.3 1.5 %collective-permute-done.20.refs_0_ = bf16[2,144,384]{2,1,0:T(8,128)(2,1)S(1)} collective-permute-done((bf16[2,144,384]{2,1,0:T(8,128)(2,1)S(1)}, bf16[2,144,384]{2,1,0:T(8,128)(2,1)S(1)}, u32[]{:S(2)}, u32[]{:S(2)}) %collective-permute-start.20) | collective-permute-done | bytes 221216 | tf_op jit(solution)/shard_map/came0/ppermute | solution.py:15
  80.8 1.5 %place.2.refs_1_ = f32[6,2,144,384]{3,2,1,0:T(8,128)} custom-call(s32[1]{0:T(128)} %bitcast.place_ref, bf16[2,144,384]{2,1,0:T(8,128)(2,1)S(1)} %collective-permute-done.20.refs_0_, bf16[2,144,384]{2,1,0:T(8,128)(2,1)S(1)} %collective-permute-done.21.refs_1_, f32[6,2,144,384]{3,2,1,0:T(8,128)} %cross_near.1.refs_2_), custom_call_target="tpu_custom_call", output_to_operand_aliasing={{}: (3, {})} | custom-call | flops 1 | bytes 1 | tf_op jit(solution)/shard_map/place/pallas_call | solution.py:229
  82.3 1.1 %place.3 = f32[6,2,144,384]{3,2,1,0:T(8,128)} custom-call(s32[1]{0:T(128)} %bitcast.place_ref, bf16[2,144,384]{2,1,0:T(8,128)(2,1)S(1)} %collective-permute-done.19.refs_0_, f32[6,2,144,384]{3,2,1,0:T(8,128)} %place.2.refs_1_), custom_call_target="tpu_custom_call", output_to_operand_aliasing={{}: (2, {})} | custom-call | flops 1 | bytes 1 | tf_op jit(solution)/shard_map/place/pallas_call | solution.py:229
  (23 shorter events, 2.4 us)
Async XLA Ops:
  0.0 1.7 %copy-start = (f32[6,2,48,1024]{3,2,1,0:T(8,128)S(1)}, f32[6,2,48,1024]{3,2,1,0:T(8,128)}, u32[]{:S(2)}) copy-start(f32[6,2,48,1024]{3,2,1,0:T(8,128)} %spectra_ref.1) | copy-start | bytes 7077892
  1.7 0.9 %copy-start.1 = (s32[48,1024]{1,0:T(8,128)S(1)}, s32[48,1024]{1,0:T(8,128)}, u32[]{:S(2)}) copy-start(s32[48,1024]{1,0:T(8,128)} %valid_ref.1) | copy-start | bytes 589828
  3.3 20.5 %collective-permute-start.2 = (bf16[2,2,48,1024]{3,2,1,0:T(8,128)(2,1)S(1)}, bf16[2,2,48,1024]{3,2,1,0:T(8,128)(2,1)S(1)}, u32[]{:S(2)}, u32[]{:S(2)}) collective-permute-start(bf16[2,2,48,1024]{3,2,1,0:T(8,128)(2,1)S(1)} %get-tuple-element.42), channel_id=1, source_target_pairs={{0,2},{1,3},{2,0},{3,1},{4,6},{5,7},{6,4},{7,5},{8,10},{9,11},{10,... | collective-permute-start | bytes 1179656 | tf_op jit(solution)/shard_map/front_z/ppermute | solution.py:15
  6.4 20.1 %collective-permute-start = (bf16[2,2,48,1024]{3,2,1,0:T(8,128)(2,1)S(1)}, bf16[2,2,48,1024]{3,2,1,0:T(8,128)(2,1)S(1)}, u32[]{:S(2)}, u32[]{:S(2)}) collective-permute-start(bf16[2,2,48,1024]{3,2,1,0:T(8,128)(2,1)S(1)} %get-tuple-element.38), channel_id=1, source_target_pairs={{0,4},{1,5},{2,6},{3,7},{4,0},{5,1},{6,2},{7,3},{8,12},{9,13},{10,... | collective-permute-start | bytes 1179656 | tf_op jit(solution)/shard_map/got/ppermute | solution.py:15
  9.0 21.2 %collective-permute-start.1 = (bf16[3,2,48,1024]{3,2,1,0:T(8,128)(2,1)S(1)}, bf16[3,2,48,1024]{3,2,1,0:T(8,128)(2,1)S(1)}, u32[]{:S(2)}, u32[]{:S(2)}) collective-permute-start(bf16[3,2,48,1024]{3,2,1,0:T(8,128)(2,1)S(1)} %get-tuple-element.36.refs_0_.refs_8_.refs_11_.refs_19_.refs_22_.refs_30_), channel_id=1, source_target_pairs={{0,1},{1,0},{2,3},{3,2},{4,5},{5,4},{6,7},{7,6},{8,9},{9,8},{10,11... | collective-permute-start | bytes 1769480 | tf_op jit(solution)/shard_map/own_x/ppermute | solution.py:15
  10.5 21.1 %collective-permute-start.13 = (bf16[3,2,48,1024]{3,2,1,0:T(8,128)(2,1)S(1)}, bf16[3,2,48,1024]{3,2,1,0:T(8,128)(2,1)S(1)}, u32[]{:S(2)}, u32[]{:S(2)}) collective-permute-start(bf16[3,2,48,1024]{3,2,1,0:T(8,128)(2,1)S(1)} %get-tuple-element.36.refs_0_.refs_8_.refs_11_.refs_19_.refs_22_.refs_30_), channel_id=1, source_target_pairs={{0,24},{8,0},{16,8},{24,16},{1,25},{9,1},{17,9},{25,17},{2,26},{10... | collective-permute-start | bytes 1769480 | tf_op jit(solution)/shard_map/own_y1/ppermute | solution.py:20
  10.6 24.5 %collective-permute-start.16 = (bf16[3,2,48,1024]{3,2,1,0:T(8,128)(2,1)S(1)}, bf16[3,2,48,1024]{3,2,1,0:T(8,128)(2,1)S(1)}, u32[]{:S(2)}, u32[]{:S(2)}) collective-permute-start(bf16[3,2,48,1024]{3,2,1,0:T(8,128)(2,1)S(1)} %get-tuple-element.36.refs_0_.refs_8_.refs_11_.refs_19_.refs_22_.refs_30_), channel_id=1, source_target_pairs={{0,16},{8,24},{16,0},{24,8},{1,17},{9,25},{17,1},{25,9},{2,18},{10... | collective-permute-start | bytes 1769480 | tf_op jit(solution)/shard_map/own_y2/ppermute | solution.py:20
  23.8 6.2 %collective-permute-start.3 = (bf16[1,2,48,1024]{3,2,1,0:T(8,128)(2,1)S(1)}, bf16[1,2,48,1024]{3,2,1,0:T(8,128)(2,1)S(1)}, u32[]{:S(2)}, u32[]{:S(2)}) collective-permute-start(bf16[1,2,48,1024]{3,2,1,0:T(8,128)(2,1)S(1)} %get-tuple-element.43), channel_id=1, source_target_pairs={{0,2},{1,3},{2,0},{3,1},{4,6},{5,7},{6,4},{7,5},{8,10},{9,11},{10,... | collective-permute-start | bytes 589832 | tf_op jit(solution)/shard_map/last/ppermute | solution.py:15
  26.5 10.8 %collective-permute-start.5 = (bf16[2,2,48,1024]{3,2,1,0:T(8,128)(2,1)S(1)}, bf16[2,2,48,1024]{3,2,1,0:T(8,128)(2,1)S(1)}, u32[]{:S(2)}, u32[]{:S(2)}) collective-permute-start(bf16[2,2,48,1024]{3,2,1,0:T(8,128)(2,1)S(1)} %collective-permute-done.2.refs_2_.refs_13_), channel_id=1, source_target_pairs={{0,1},{1,0},{2,3},{3,2},{4,5},{5,4},{6,7},{7,6},{8,9},{9,8},{10,11... | collective-permute-start | bytes 1179656 | tf_op jit(solution)/shard_map/front_d/ppermute | solution.py:15
  30.0 13.7 %collective-permute-start.4 = (bf16[2,2,48,1024]{3,2,1,0:T(8,128)(2,1)S(1)}, bf16[2,2,48,1024]{3,2,1,0:T(8,128)(2,1)S(1)}, u32[]{:S(2)}, u32[]{:S(2)}) collective-permute-start(bf16[2,2,48,1024]{3,2,1,0:T(8,128)(2,1)S(1)} %collective-permute-done.refs_4_.refs_8_.refs_15_), channel_id=1, source_target_pairs={{0,2},{1,3},{2,0},{3,1},{4,6},{5,7},{6,4},{7,5},{8,10},{9,11},{10,... | collective-permute-start | bytes 1179656 | tf_op jit(solution)/shard_map/got_z/ppermute | solution.py:15
  30.2 16.5 %collective-permute-start.10 = (bf16[2,2,48,1024]{3,2,1,0:T(8,128)(2,1)S(1)}, bf16[2,2,48,1024]{3,2,1,0:T(8,128)(2,1)S(1)}, u32[]{:S(2)}, u32[]{:S(2)}) collective-permute-start(bf16[2,2,48,1024]{3,2,1,0:T(8,128)(2,1)S(1)} %collective-permute-done.refs_4_.refs_8_.refs_15_), channel_id=1, source_target_pairs={{0,1},{1,0},{2,3},{3,2},{4,5},{5,4},{6,7},{7,6},{8,9},{9,8},{10,11... | collective-permute-start | bytes 1179656 | tf_op jit(solution)/shard_map/got_x/ppermute | solution.py:15
  31.5 13.2 %collective-permute-start.8 = (bf16[1,2,48,1024]{3,2,1,0:T(8,128)(2,1)S(1)}, bf16[1,2,48,1024]{3,2,1,0:T(8,128)(2,1)S(1)}, u32[]{:S(2)}, u32[]{:S(2)}) collective-permute-start(bf16[1,2,48,1024]{3,2,1,0:T(8,128)(2,1)S(1)} %get-tuple-element.48), channel_id=1, source_target_pairs={{0,4},{1,5},{2,6},{3,7},{4,0},{5,1},{6,2},{7,3},{8,12},{9,13},{10,... | collective-permute-start | bytes 589832 | tf_op jit(solution)/shard_map/back_z/ppermute | solution.py:15
  35.1 12.1 %collective-permute-start.17 = (bf16[2,2,48,1024]{3,2,1,0:T(8,128)(2,1)S(1)}, bf16[2,2,48,1024]{3,2,1,0:T(8,128)(2,1)S(1)}, u32[]{:S(2)}, u32[]{:S(2)}) collective-permute-start(bf16[2,2,48,1024]{3,2,1,0:T(8,128)(2,1)S(1)} %collective-permute-done.refs_4_.refs_8_.refs_15_), channel_id=1, source_target_pairs={{0,16},{8,24},{16,0},{24,8},{1,17},{9,25},{17,1},{25,9},{2,18},{10... | collective-permute-start | bytes 1179656 | tf_op jit(solution)/shard_map/got_y2/ppermute | solution.py:20
  37.3 10.1 %collective-permute-start.14 = (bf16[2,2,48,1024]{3,2,1,0:T(8,128)(2,1)S(1)}, bf16[2,2,48,1024]{3,2,1,0:T(8,128)(2,1)S(1)}, u32[]{:S(2)}, u32[]{:S(2)}) collective-permute-start(bf16[2,2,48,1024]{3,2,1,0:T(8,128)(2,1)S(1)} %collective-permute-done.refs_4_.refs_8_.refs_15_), channel_id=1, source_target_pairs={{0,24},{8,0},{16,8},{24,16},{1,25},{9,1},{17,9},{25,17},{2,26},{10... | collective-permute-start | bytes 1179656 | tf_op jit(solution)/shard_map/got_y1/ppermute | solution.py:20
  43.7 14.5 %collective-permute-start.6 = (bf16[2,2,48,1024]{3,2,1,0:T(8,128)(2,1)S(1)}, bf16[2,2,48,1024]{3,2,1,0:T(8,128)(2,1)S(1)}, u32[]{:S(2)}, u32[]{:S(2)}) collective-permute-start(bf16[2,2,48,1024]{3,2,1,0:T(8,128)(2,1)S(1)} %collective-permute-done.4.refs_6_.refs_17_), channel_id=1, source_target_pairs={{0,1},{1,0},{2,3},{3,2},{4,5},{5,4},{6,7},{7,6},{8,9},{9,8},{10,11... | collective-permute-start | bytes 1179656 | tf_op jit(solution)/shard_map/got_d/ppermute | solution.py:15
  44.8 9.7 %collective-permute-start.9 = (bf16[1,2,48,1024]{3,2,1,0:T(8,128)(2,1)S(1)}, bf16[1,2,48,1024]{3,2,1,0:T(8,128)(2,1)S(1)}, u32[]{:S(2)}, u32[]{:S(2)}) collective-permute-start(bf16[1,2,48,1024]{3,2,1,0:T(8,128)(2,1)S(1)} %collective-permute-done.3.refs_2_.refs_8_.refs_24_), channel_id=1, source_target_pairs={{0,4},{1,5},{2,6},{3,7},{4,0},{5,1},{6,2},{7,3},{8,12},{9,13},{10,... | collective-permute-start | bytes 589832 | tf_op jit(solution)/shard_map/last_z/ppermute | solution.py:15
  46.7 10.5 %collective-permute-start.11 = (bf16[1,2,48,1024]{3,2,1,0:T(8,128)(2,1)S(1)}, bf16[1,2,48,1024]{3,2,1,0:T(8,128)(2,1)S(1)}, u32[]{:S(2)}, u32[]{:S(2)}) collective-permute-start(bf16[1,2,48,1024]{3,2,1,0:T(8,128)(2,1)S(1)} %collective-permute-done.8.refs_4_.refs_26_), channel_id=1, source_target_pairs={{0,1},{1,0},{2,3},{3,2},{4,5},{5,4},{6,7},{7,6},{8,9},{9,8},{10,11... | collective-permute-start | bytes 589832 | tf_op jit(solution)/shard_map/back_d/ppermute | solution.py:15
  47.4 18.6 %collective-permute-start.18 = (bf16[1,2,48,1024]{3,2,1,0:T(8,128)(2,1)S(1)}, bf16[1,2,48,1024]{3,2,1,0:T(8,128)(2,1)S(1)}, u32[]{:S(2)}, u32[]{:S(2)}) collective-permute-start(bf16[1,2,48,1024]{3,2,1,0:T(8,128)(2,1)S(1)} %collective-permute-done.3.refs_2_.refs_8_.refs_24_), channel_id=1, source_target_pairs={{0,16},{8,24},{16,0},{24,8},{1,17},{9,25},{17,1},{25,9},{2,18},{10... | collective-permute-start | bytes 589832 | tf_op jit(solution)/shard_map/last_y2/ppermute | solution.py:20
  48.7 18.5 %collective-permute-start.15 = (bf16[1,2,48,1024]{3,2,1,0:T(8,128)(2,1)S(1)}, bf16[1,2,48,1024]{3,2,1,0:T(8,128)(2,1)S(1)}, u32[]{:S(2)}, u32[]{:S(2)}) collective-permute-start(bf16[1,2,48,1024]{3,2,1,0:T(8,128)(2,1)S(1)} %collective-permute-done.3.refs_2_.refs_8_.refs_24_), channel_id=1, source_target_pairs={{0,24},{8,0},{16,8},{24,16},{1,25},{9,1},{17,9},{25,17},{2,26},{10... | collective-permute-start | bytes 589832 | tf_op jit(solution)/shard_map/last_y1/ppermute | solution.py:20
  57.2 10.0 %collective-permute-start.12 = (bf16[1,2,48,1024]{3,2,1,0:T(8,128)(2,1)S(1)}, bf16[1,2,48,1024]{3,2,1,0:T(8,128)(2,1)S(1)}, u32[]{:S(2)}, u32[]{:S(2)}) collective-permute-start(bf16[1,2,48,1024]{3,2,1,0:T(8,128)(2,1)S(1)} %collective-permute-done.9.refs_6_.refs_28_), channel_id=1, source_target_pairs={{0,1},{1,0},{2,3},{3,2},{4,5},{5,4},{6,7},{7,6},{8,9},{9,8},{10,11... | collective-permute-start | bytes 589832 | tf_op jit(solution)/shard_map/last_d/ppermute | solution.py:15
  58.3 9.0 %collective-permute-start.7 = (bf16[1,2,48,1024]{3,2,1,0:T(8,128)(2,1)S(1)}, bf16[1,2,48,1024]{3,2,1,0:T(8,128)(2,1)S(1)}, u32[]{:S(2)}, u32[]{:S(2)}) collective-permute-start(bf16[1,2,48,1024]{3,2,1,0:T(8,128)(2,1)S(1)} %collective-permute-done.3.refs_2_.refs_8_.refs_24_), channel_id=1, source_target_pairs={{0,1},{1,0},{2,3},{3,2},{4,5},{5,4},{6,7},{7,6},{8,9},{9,8},{10,11... | collective-permute-start | bytes 589832 | tf_op jit(solution)/shard_map/last_x/ppermute | solution.py:15
  61.7 17.5 %collective-permute-start.21 = (bf16[2,144,384]{2,1,0:T(8,128)(2,1)S(1)}, bf16[2,144,384]{2,1,0:T(8,128)(2,1)S(1)}, u32[]{:S(2)}, u32[]{:S(2)}) collective-permute-start(bf16[2,144,384]{2,1,0:T(8,128)(2,1)S(1)} %cross_far.5), channel_id=1, source_target_pairs={{0,4},{1,5},{2,6},{3,7},{4,0},{5,1},{6,2},{7,3},{8,12},{9,13},{10,... | collective-permute-start | bytes 663560 | tf_op jit(solution)/shard_map/came1/ppermute | solution.py:15
  66.0 14.8 %collective-permute-start.20 = (bf16[2,144,384]{2,1,0:T(8,128)(2,1)S(1)}, bf16[2,144,384]{2,1,0:T(8,128)(2,1)S(1)}, u32[]{:S(2)}, u32[]{:S(2)}) collective-permute-start(bf16[2,144,384]{2,1,0:T(8,128)(2,1)S(1)} %cross_far.4), channel_id=1, source_target_pairs={{0,4},{1,5},{2,6},{3,7},{4,0},{5,1},{6,2},{7,3},{8,12},{9,13},{10,... | collective-permute-start | bytes 663560 | tf_op jit(solution)/shard_map/came0/ppermute | solution.py:15
  69.8 12.5 %collective-permute-start.19 = (bf16[2,144,384]{2,1,0:T(8,128)(2,1)S(1)}, bf16[2,144,384]{2,1,0:T(8,128)(2,1)S(1)}, u32[]{:S(2)}, u32[]{:S(2)}) collective-permute-start(bf16[2,144,384]{2,1,0:T(8,128)(2,1)S(1)} %cross_far.3), channel_id=1, source_target_pairs={{0,2},{1,3},{2,0},{3,1},{4,6},{5,7},{6,4},{7,5},{8,10},{9,11},{10,... | collective-permute-start | bytes 663560 | tf_op jit(solution)/shard_map/came2/ppermute | solution.py:15

commit v5 on v4

--- a/solution.py
+++ b/solution.py
@@ -64,9 +64,9 @@
     2: (("own", 2), ("last", 0)),
 }
 FAR = 2
-ORDER = ("got", "own_x", "front_z", "own_y1", "own_y2", "front_d", "last", "back_z", "got_z", "got_x", "got_y1", "got_y2", "got_d", "last_z", "back_d", "last_x", "last_y1", "last_y2", "last_d", "far0", "came0", "far1", "came1", "far2", "came2", "near012", "place01", "place2")
+ORDER = ("got", "own_x", "front_z", "own_y1", "own_y2", "front_d", "last", "back_z", "got_z", "got_y1", "got_y2", "got_d", "last_z", "last_y1", "last_y2", "last_x", "got_x", "far1", "came1", "back_d", "last_d", "far0", "came0", "far2", "came2", "near102", "place10", "place2")
 GATES = {
-    "last": ["front_z"],
+    "last": ["own_y2"],
     "back_z": ["got"],
     "got_z": ["last"],
     "got_x": ["own_x"],

time: 83.6 us -> 83.1 us (level)
  waiting for transfers between devices: 32.7 us -> 28.7 us
  starting transfers between devices: 29.1 us -> 32.6 us
    ppermute x16, waiting for transfers between devices: 32.6 us -> 21.1 us  [moved_by_xor(): lax.ppermute(value, axis, [(source, source ^ bits) for source in range(co...]
    ppermute x6, waiting for transfers between devices: 0.16 us -> 7.68 us  [moved_by_shift(): lax.ppermute(value, axis, [(source, (source + steps) % count) for source...]
    ppermute x16, starting transfers between devices: 23.7 us -> 26.8 us  [moved_by_xor(): lax.ppermute(value, axis, [(source, source ^ bits) for source in range(co...]
  transfers between devices with their start and end apart: 22 -> 22, of which waited for: 9 -> 9; matrix products, arithmetic and copies ran while one was open for 0% -> 0% of each run, Pallas kernels for 20% -> 21%
where the time goes in v5:
time: 83.1 us; the launch traced here: 82.9 us
  starting transfers between devices  32.6 us (39%)
  waiting for transfers between devices  28.7 us (35%)
  Pallas kernels  18.9 us (23%)
  local copies, waits for them, and re-layouts  2.59 us (3%)
    ppermute x16, starting transfers between devices, moved_by_xor(): lax.ppermute(value, axis, [(source, source ^ bits) for source in range(co...  26.8 us
    ppermute x16, waiting for transfers between devices, moved_by_xor(): lax.ppermute(value, axis, [(source, source ^ bits) for source in range(co...  21.1 us
    pallas_call x4, Pallas kernels, cross(): pl.pallas_call(functools.partial(cross_kernel, plan), grid_spec=pltpu.Pre...  15.5 us
    ppermute x6, waiting for transfers between devices, moved_by_shift(): lax.ppermute(value, axis, [(source, (source + steps) % count) for source...  7.68 us
    ppermute x6, starting transfers between devices, moved_by_shift(): lax.ppermute(value, axis, [(source, (source + steps) % count) for source...  5.82 us
    pallas_call x2, Pallas kernels, place_blocks(): pl.pallas_call(functools.partial(place_kernel, pairs), grid_spec=pltpu.Pr...  2.61 us
    unnamed x4, local copies, waits for them, and re-layouts  2.59 us
  transfers between devices with their start and end apart: 22, of which 9 were waited for; matrix products, arithmetic and copies ran while one was open for 0% of the time, Pallas kernels for 21%

profile of v5, /device:TPU:0, one launch (start us, length us, event | category | flops | bytes accessed | tf_op | source)
XLA Modules:
  0.0 82.9 jit_solution(2952898373801389638)
XLA Ops:
  0.0 1.7 %copy-done = f32[6,2,48,1024]{3,2,1,0:T(8,128)S(1)} copy-done((f32[6,2,48,1024]{3,2,1,0:T(8,128)S(1)}, f32[6,2,48,1024]{3,2,1,0:T(8,128)}, u32[]{:S(2)}) %copy-start) | copy-done | bytes 2359320
  1.7 0.9 %copy-done.1 = s32[48,1024]{1,0:T(8,128)S(1)} copy-done((s32[48,1024]{1,0:T(8,128)S(1)}, s32[48,1024]{1,0:T(8,128)}, u32[]{:S(2)}) %copy-start.1) | copy-done | bytes 196632
  3.3 3.0 %collective-permute-start.2 = (bf16[3,2,48,1024]{3,2,1,0:T(8,128)(2,1)S(1)}, bf16[3,2,48,1024]{3,2,1,0:T(8,128)(2,1)S(1)}, u32[]{:S(2)}, u32[]{:S(2)}) collective-permute-start(bf16[3,2,48,1024]{3,2,1,0:T(8,128)(2,1)S(1)} %get-tuple-element.36.refs_0_.refs_8_.refs_11_.refs_19_.refs_22_.refs_30_), channel_id=1, source_target_pairs={{0,16},{8,24},{16,0},{24,8},{1,17},{9,25},{17,1},{25,9},{2,18},{10... | collective-permute-start | bytes 1769480 | tf_op jit(solution)/shard_map/own_y2/ppermute | solution.py:20
  6.4 1.6 %collective-permute-start.5 = (bf16[2,2,48,1024]{3,2,1,0:T(8,128)(2,1)S(1)}, bf16[2,2,48,1024]{3,2,1,0:T(8,128)(2,1)S(1)}, u32[]{:S(2)}, u32[]{:S(2)}) collective-permute-start(bf16[2,2,48,1024]{3,2,1,0:T(8,128)(2,1)S(1)} %get-tuple-element.45), channel_id=1, source_target_pairs={{0,2},{1,3},{2,0},{3,1},{4,6},{5,7},{6,4},{7,5},{8,10},{9,11},{10,... | collective-permute-start | bytes 1179656 | tf_op jit(solution)/shard_map/front_z/ppermute | solution.py:15
  7.9 1.5 %collective-permute-start.1 = (bf16[3,2,48,1024]{3,2,1,0:T(8,128)(2,1)S(1)}, bf16[3,2,48,1024]{3,2,1,0:T(8,128)(2,1)S(1)}, u32[]{:S(2)}, u32[]{:S(2)}) collective-permute-start(bf16[3,2,48,1024]{3,2,1,0:T(8,128)(2,1)S(1)} %get-tuple-element.36.refs_0_.refs_8_.refs_11_.refs_19_.refs_22_.refs_30_), channel_id=1, source_target_pairs={{0,1},{1,0},{2,3},{3,2},{4,5},{5,4},{6,7},{7,6},{8,9},{9,8},{10,11... | collective-permute-start | bytes 1769480 | tf_op jit(solution)/shard_map/own_x/ppermute | solution.py:15
  9.4 2.6 %collective-permute-start = (bf16[2,2,48,1024]{3,2,1,0:T(8,128)(2,1)S(1)}, bf16[2,2,48,1024]{3,2,1,0:T(8,128)(2,1)S(1)}, u32[]{:S(2)}, u32[]{:S(2)}) collective-permute-start(bf16[2,2,48,1024]{3,2,1,0:T(8,128)(2,1)S(1)} %get-tuple-element.38), channel_id=1, source_target_pairs={{0,4},{1,5},{2,6},{3,7},{4,0},{5,1},{6,2},{7,3},{8,12},{9,13},{10,... | collective-permute-start | bytes 1179656 | tf_op jit(solution)/shard_map/got/ppermute | solution.py:15
  12.0 7.7 %collective-permute-done.2.refs_10_.refs_21_.refs_32_ = bf16[3,2,48,1024]{3,2,1,0:T(8,128)(2,1)S(1)} collective-permute-done((bf16[3,2,48,1024]{3,2,1,0:T(8,128)(2,1)S(1)}, bf16[3,2,48,1024]{3,2,1,0:T(8,128)(2,1)S(1)}, u32[]{:S(2)}, u32[]{:S(2)}) %collective-permute-start.2) | collective-permute-done | bytes 589856 | tf_op jit(solution)/shard_map/own_y2/ppermute | solution.py:20
  19.7 1.8 %collective-permute-start.3 = (bf16[1,2,48,1024]{3,2,1,0:T(8,128)(2,1)S(1)}, bf16[1,2,48,1024]{3,2,1,0:T(8,128)(2,1)S(1)}, u32[]{:S(2)}, u32[]{:S(2)}) collective-permute-start(bf16[1,2,48,1024]{3,2,1,0:T(8,128)(2,1)S(1)} %get-tuple-element.42), channel_id=1, source_target_pairs={{0,2},{1,3},{2,0},{3,1},{4,6},{5,7},{6,4},{7,5},{8,10},{9,11},{10,... | collective-permute-start | bytes 589832 | tf_op jit(solution)/shard_map/last/ppermute | solution.py:15
  21.5 4.0 %collective-permute-done.5.refs_2_.refs_13_ = bf16[2,2,48,1024]{3,2,1,0:T(8,128)(2,1)S(1)} collective-permute-done((bf16[2,2,48,1024]{3,2,1,0:T(8,128)(2,1)S(1)}, bf16[2,2,48,1024]{3,2,1,0:T(8,128)(2,1)S(1)}, u32[]{:S(2)}, u32[]{:S(2)}) %collective-permute-start.5) | collective-permute-done | bytes 393248 | tf_op jit(solution)/shard_map/front_z/ppermute | solution.py:15
  25.5 2.8 %collective-permute-start.6 = (bf16[2,2,48,1024]{3,2,1,0:T(8,128)(2,1)S(1)}, bf16[2,2,48,1024]{3,2,1,0:T(8,128)(2,1)S(1)}, u32[]{:S(2)}, u32[]{:S(2)}) collective-permute-start(bf16[2,2,48,1024]{3,2,1,0:T(8,128)(2,1)S(1)} %collective-permute-done.5.refs_2_.refs_13_), channel_id=1, source_target_pairs={{0,1},{1,0},{2,3},{3,2},{4,5},{5,4},{6,7},{7,6},{8,9},{9,8},{10,11... | collective-permute-start | bytes 1179656 | tf_op jit(solution)/shard_map/front_d/ppermute | solution.py:15
  28.7 0.8 %collective-permute-done.3.refs_2_.refs_8_.refs_24_ = bf16[1,2,48,1024]{3,2,1,0:T(8,128)(2,1)S(1)} collective-permute-done((bf16[1,2,48,1024]{3,2,1,0:T(8,128)(2,1)S(1)}, bf16[1,2,48,1024]{3,2,1,0:T(8,128)(2,1)S(1)}, u32[]{:S(2)}, u32[]{:S(2)}) %collective-permute-start.3) | collective-permute-done | bytes 196640 | tf_op jit(solution)/shard_map/last/ppermute | solution.py:15
  29.6 1.6 %collective-permute-start.4 = (bf16[2,2,48,1024]{3,2,1,0:T(8,128)(2,1)S(1)}, bf16[2,2,48,1024]{3,2,1,0:T(8,128)(2,1)S(1)}, u32[]{:S(2)}, u32[]{:S(2)}) collective-permute-start(bf16[2,2,48,1024]{3,2,1,0:T(8,128)(2,1)S(1)} %collective-permute-done.refs_4_.refs_8_.refs_15_), channel_id=1, source_target_pairs={{0,2},{1,3},{2,0},{3,1},{4,6},{5,7},{6,4},{7,5},{8,10},{9,11},{10,... | collective-permute-start | bytes 1179656 | tf_op jit(solution)/shard_map/got_z/ppermute | solution.py:15
  31.2 1.5 %collective-permute-start.11 = (bf16[2,2,48,1024]{3,2,1,0:T(8,128)(2,1)S(1)}, bf16[2,2,48,1024]{3,2,1,0:T(8,128)(2,1)S(1)}, u32[]{:S(2)}, u32[]{:S(2)}) collective-permute-start(bf16[2,2,48,1024]{3,2,1,0:T(8,128)(2,1)S(1)} %collective-permute-done.refs_4_.refs_8_.refs_15_), channel_id=1, source_target_pairs={{0,1},{1,0},{2,3},{3,2},{4,5},{5,4},{6,7},{7,6},{8,9},{9,8},{10,11... | collective-permute-start | bytes 1179656 | tf_op jit(solution)/shard_map/got_x/ppermute | solution.py:15
  32.7 2.5 %collective-permute-start.9 = (bf16[1,2,48,1024]{3,2,1,0:T(8,128)(2,1)S(1)}, bf16[1,2,48,1024]{3,2,1,0:T(8,128)(2,1)S(1)}, u32[]{:S(2)}, u32[]{:S(2)}) collective-permute-start(bf16[1,2,48,1024]{3,2,1,0:T(8,128)(2,1)S(1)} %get-tuple-element.48), channel_id=1, source_target_pairs={{0,4},{1,5},{2,6},{3,7},{4,0},{5,1},{6,2},{7,3},{8,12},{9,13},{10,... | collective-permute-start | bytes 589832 | tf_op jit(solution)/shard_map/back_z/ppermute | solution.py:15
  35.7 0.8 %collective-permute-done.6.refs_3_.refs_14_ = bf16[2,2,48,1024]{3,2,1,0:T(8,128)(2,1)S(1)} collective-permute-done((bf16[2,2,48,1024]{3,2,1,0:T(8,128)(2,1)S(1)}, bf16[2,2,48,1024]{3,2,1,0:T(8,128)(2,1)S(1)}, u32[]{:S(2)}, u32[]{:S(2)}) %collective-permute-start.6) | collective-permute-done | bytes 393248 | tf_op jit(solution)/shard_map/front_d/ppermute | solution.py:15
  36.6 6.7 %collective-permute-done.4.refs_6_.refs_17_ = bf16[2,2,48,1024]{3,2,1,0:T(8,128)(2,1)S(1)} collective-permute-done((bf16[2,2,48,1024]{3,2,1,0:T(8,128)(2,1)S(1)}, bf16[2,2,48,1024]{3,2,1,0:T(8,128)(2,1)S(1)}, u32[]{:S(2)}, u32[]{:S(2)}) %collective-permute-start.4) | collective-permute-done | bytes 393248 | tf_op jit(solution)/shard_map/got_z/ppermute | solution.py:15
  43.3 1.6 %collective-permute-start.7 = (bf16[2,2,48,1024]{3,2,1,0:T(8,128)(2,1)S(1)}, bf16[2,2,48,1024]{3,2,1,0:T(8,128)(2,1)S(1)}, u32[]{:S(2)}, u32[]{:S(2)}) collective-permute-start(bf16[2,2,48,1024]{3,2,1,0:T(8,128)(2,1)S(1)} %collective-permute-done.4.refs_6_.refs_17_), channel_id=1, source_target_pairs={{0,1},{1,0},{2,3},{3,2},{4,5},{5,4},{6,7},{7,6},{8,9},{9,8},{10,11... | collective-permute-start | bytes 1179656 | tf_op jit(solution)/shard_map/got_d/ppermute | solution.py:15
  44.9 1.7 %collective-permute-start.10 = (bf16[1,2,48,1024]{3,2,1,0:T(8,128)(2,1)S(1)}, bf16[1,2,48,1024]{3,2,1,0:T(8,128)(2,1)S(1)}, u32[]{:S(2)}, u32[]{:S(2)}) collective-permute-start(bf16[1,2,48,1024]{3,2,1,0:T(8,128)(2,1)S(1)} %collective-permute-done.3.refs_2_.refs_8_.refs_24_), channel_id=1, source_target_pairs={{0,4},{1,5},{2,6},{3,7},{4,0},{5,1},{6,2},{7,3},{8,12},{9,13},{10,... | collective-permute-start | bytes 589832 | tf_op jit(solution)/shard_map/last_z/ppermute | solution.py:15
  48.0 1.8 %collective-permute-start.16 = (bf16[1,2,48,1024]{3,2,1,0:T(8,128)(2,1)S(1)}, bf16[1,2,48,1024]{3,2,1,0:T(8,128)(2,1)S(1)}, u32[]{:S(2)}, u32[]{:S(2)}) collective-permute-start(bf16[1,2,48,1024]{3,2,1,0:T(8,128)(2,1)S(1)} %collective-permute-done.3.refs_2_.refs_8_.refs_24_), channel_id=1, source_target_pairs={{0,24},{8,0},{16,8},{24,16},{1,25},{9,1},{17,9},{25,17},{2,26},{10... | collective-permute-start | bytes 589832 | tf_op jit(solution)/shard_map/last_y1/ppermute | solution.py:20
  49.7 4.6 %collective-permute-done.10.refs_6_.refs_28_ = bf16[1,2,48,1024]{3,2,1,0:T(8,128)(2,1)S(1)} collective-permute-done((bf16[1,2,48,1024]{3,2,1,0:T(8,128)(2,1)S(1)}, bf16[1,2,48,1024]{3,2,1,0:T(8,128)(2,1)S(1)}, u32[]{:S(2)}, u32[]{:S(2)}) %collective-permute-start.10) | collective-permute-done | bytes 196640 | tf_op jit(solution)/shard_map/last_z/ppermute | solution.py:15
  54.3 2.4 %collective-permute-done.12.refs_5_.refs_27_ = bf16[1,2,48,1024]{3,2,1,0:T(8,128)(2,1)S(1)} collective-permute-done((bf16[1,2,48,1024]{3,2,1,0:T(8,128)(2,1)S(1)}, bf16[1,2,48,1024]{3,2,1,0:T(8,128)(2,1)S(1)}, u32[]{:S(2)}, u32[]{:S(2)}) %collective-permute-start.12) | collective-permute-done | bytes 196640 | tf_op jit(solution)/shard_map/back_d/ppermute | solution.py:15
  56.7 1.7 %collective-permute-start.13 = (bf16[1,2,48,1024]{3,2,1,0:T(8,128)(2,1)S(1)}, bf16[1,2,48,1024]{3,2,1,0:T(8,128)(2,1)S(1)}, u32[]{:S(2)}, u32[]{:S(2)}) collective-permute-start(bf16[1,2,48,1024]{3,2,1,0:T(8,128)(2,1)S(1)} %collective-permute-done.10.refs_6_.refs_28_), channel_id=1, source_target_pairs={{0,1},{1,0},{2,3},{3,2},{4,5},{5,4},{6,7},{7,6},{8,9},{9,8},{10,11... | collective-permute-start | bytes 589832 | tf_op jit(solution)/shard_map/last_d/ppermute | solution.py:15
  58.7 2.5 %cross_far.5 = bf16[2,144,384]{2,1,0:T(8,128)(2,1)S(1)} custom-call(s32[1]{0:T(128)} %bitcast.place_ref, bf16[3,2,48,1024]{3,2,1,0:T(8,128)(2,1)S(1)} %get-tuple-element.36.refs_0_.refs_8_.refs_11_.refs_19_.refs_22_.refs_30_, bf16[3,2,48,1024]{3,2,1,0:T(8,128)(2,1)S(1)} %collective-permute-done.1.refs_1_.refs_12_.refs_23_, ...), custom_call_target="tpu_custom_call" | custom-call | flops 1 | bytes 1 | tf_op jit(solution)/shard_map/cross_far/pallas_call | solution.py:185
  61.2 2.1 %collective-permute-start.21 = (bf16[2,144,384]{2,1,0:T(8,128)(2,1)S(1)}, bf16[2,144,384]{2,1,0:T(8,128)(2,1)S(1)}, u32[]{:S(2)}, u32[]{:S(2)}) collective-permute-start(bf16[2,144,384]{2,1,0:T(8,128)(2,1)S(1)} %cross_far.5), channel_id=1, source_target_pairs={{0,4},{1,5},{2,6},{3,7},{4,0},{5,1},{6,2},{7,3},{8,12},{9,13},{10,... | collective-permute-start | bytes 663560 | tf_op jit(solution)/shard_map/came0/ppermute | solution.py:15
  63.3 2.5 %cross_far.4 = bf16[2,144,384]{2,1,0:T(8,128)(2,1)S(1)} custom-call(s32[1]{0:T(128)} %bitcast.place_ref, bf16[3,2,48,1024]{3,2,1,0:T(8,128)(2,1)S(1)} %get-tuple-element.36.refs_0_.refs_8_.refs_11_.refs_19_.refs_22_.refs_30_, bf16[3,2,48,1024]{3,2,1,0:T(8,128)(2,1)S(1)} %collective-permute-done.1.refs_1_.refs_12_.refs_23_, ...), custom_call_target="tpu_custom_call" | custom-call | flops 1 | bytes 1 | tf_op jit(solution)/shard_map/cross_far/pallas_call | solution.py:185
  65.8 1.0 %collective-permute-start.20 = (bf16[2,144,384]{2,1,0:T(8,128)(2,1)S(1)}, bf16[2,144,384]{2,1,0:T(8,128)(2,1)S(1)}, u32[]{:S(2)}, u32[]{:S(2)}) collective-permute-start(bf16[2,144,384]{2,1,0:T(8,128)(2,1)S(1)} %cross_far.4), channel_id=1, source_target_pairs={{0,4},{1,5},{2,6},{3,7},{4,0},{5,1},{6,2},{7,3},{8,12},{9,13},{10,... | collective-permute-start | bytes 663560 | tf_op jit(solution)/shard_map/came1/ppermute | solution.py:15
  66.7 2.5 %cross_far.3 = bf16[2,144,384]{2,1,0:T(8,128)(2,1)S(1)} custom-call(s32[1]{0:T(128)} %bitcast.place_ref, bf16[3,2,48,1024]{3,2,1,0:T(8,128)(2,1)S(1)} %get-tuple-element.36.refs_0_.refs_8_.refs_11_.refs_19_.refs_22_.refs_30_, bf16[3,2,48,1024]{3,2,1,0:T(8,128)(2,1)S(1)} %collective-permute-done.1.refs_1_.refs_12_.refs_23_, ...), custom_call_target="tpu_custom_call" | custom-call | flops 1 | bytes 1 | tf_op jit(solution)/shard_map/cross_far/pallas_call | solution.py:185
  69.2 1.7 %collective-permute-start.19 = (bf16[2,144,384]{2,1,0:T(8,128)(2,1)S(1)}, bf16[2,144,384]{2,1,0:T(8,128)(2,1)S(1)}, u32[]{:S(2)}, u32[]{:S(2)}) collective-permute-start(bf16[2,144,384]{2,1,0:T(8,128)(2,1)S(1)} %cross_far.3), channel_id=1, source_target_pairs={{0,2},{1,3},{2,0},{3,1},{4,6},{5,7},{6,4},{7,5},{8,10},{9,11},{10,... | collective-permute-start | bytes 663560 | tf_op jit(solution)/shard_map/came2/ppermute | solution.py:15
  70.9 8.1 %cross_near.1.refs_2_ = f32[6,2,144,384]{3,2,1,0:T(8,128)} custom-call(s32[1]{0:T(128)} %bitcast.place_ref, bf16[3,2,48,1024]{3,2,1,0:T(8,128)(2,1)S(1)} %get-tuple-element.36.refs_0_.refs_8_.refs_11_.refs_19_.refs_22_.refs_30_, bf16[3,2,48,1024]{3,2,1,0:T(8,128)(2,1)S(1)} %collective-permute-done.1.refs_1_.refs_12_.refs_23_, ...), custom_call_target="tpu_custom_call" | custom-call | flops 1 | bytes 1 | tf_op jit(solution)/shard_map/cross_near/pallas_call | solution.py:185
  79.1 1.3 %collective-permute-done.20.refs_0_ = bf16[2,144,384]{2,1,0:T(8,128)(2,1)S(1)} collective-permute-done((bf16[2,144,384]{2,1,0:T(8,128)(2,1)S(1)}, bf16[2,144,384]{2,1,0:T(8,128)(2,1)S(1)}, u32[]{:S(2)}, u32[]{:S(2)}) %collective-permute-start.20) | collective-permute-done | bytes 221216 | tf_op jit(solution)/shard_map/came1/ppermute | solution.py:15
  80.3 1.5 %place.2.refs_1_ = f32[6,2,144,384]{3,2,1,0:T(8,128)} custom-call(s32[1]{0:T(128)} %bitcast.place_ref, bf16[2,144,384]{2,1,0:T(8,128)(2,1)S(1)} %collective-permute-done.20.refs_0_, bf16[2,144,384]{2,1,0:T(8,128)(2,1)S(1)} %collective-permute-done.21.refs_1_, f32[6,2,144,384]{3,2,1,0:T(8,128)} %cross_near.1.refs_2_), custom_call_target="tpu_custom_call", output_to_operand_aliasing={{}: (3, {})} | custom-call | flops 1 | bytes 1 | tf_op jit(solution)/shard_map/place/pallas_call | solution.py:229
  81.8 1.1 %place.3 = f32[6,2,144,384]{3,2,1,0:T(8,128)} custom-call(s32[1]{0:T(128)} %bitcast.place_ref, bf16[2,144,384]{2,1,0:T(8,128)(2,1)S(1)} %collective-permute-done.19.refs_0_, f32[6,2,144,384]{3,2,1,0:T(8,128)} %place.2.refs_1_), custom_call_target="tpu_custom_call", output_to_operand_aliasing={{}: (2, {})} | custom-call | flops 1 | bytes 1 | tf_op jit(solution)/shard_map/place/pallas_call | solution.py:229
  (23 shorter events, 3.3 us)
Async XLA Ops:
  0.0 1.7 %copy-start = (f32[6,2,48,1024]{3,2,1,0:T(8,128)S(1)}, f32[6,2,48,1024]{3,2,1,0:T(8,128)}, u32[]{:S(2)}) copy-start(f32[6,2,48,1024]{3,2,1,0:T(8,128)} %spectra_ref.1) | copy-start | bytes 7077892
  1.7 0.9 %copy-start.1 = (s32[48,1024]{1,0:T(8,128)S(1)}, s32[48,1024]{1,0:T(8,128)}, u32[]{:S(2)}) copy-start(s32[48,1024]{1,0:T(8,128)} %valid_ref.1) | copy-start | bytes 589828
  3.3 16.4 %collective-permute-start.2 = (bf16[3,2,48,1024]{3,2,1,0:T(8,128)(2,1)S(1)}, bf16[3,2,48,1024]{3,2,1,0:T(8,128)(2,1)S(1)}, u32[]{:S(2)}, u32[]{:S(2)}) collective-permute-start(bf16[3,2,48,1024]{3,2,1,0:T(8,128)(2,1)S(1)} %get-tuple-element.36.refs_0_.refs_8_.refs_11_.refs_19_.refs_22_.refs_30_), channel_id=1, source_target_pairs={{0,16},{8,24},{16,0},{24,8},{1,17},{9,25},{17,1},{25,9},{2,18},{10... | collective-permute-start | bytes 1769480 | tf_op jit(solution)/shard_map/own_y2/ppermute | solution.py:20
  6.4 19.1 %collective-permute-start.5 = (bf16[2,2,48,1024]{3,2,1,0:T(8,128)(2,1)S(1)}, bf16[2,2,48,1024]{3,2,1,0:T(8,128)(2,1)S(1)}, u32[]{:S(2)}, u32[]{:S(2)}) collective-permute-start(bf16[2,2,48,1024]{3,2,1,0:T(8,128)(2,1)S(1)} %get-tuple-element.45), channel_id=1, source_target_pairs={{0,2},{1,3},{2,0},{3,1},{4,6},{5,7},{6,4},{7,5},{8,10},{9,11},{10,... | collective-permute-start | bytes 1179656 | tf_op jit(solution)/shard_map/front_z/ppermute | solution.py:15
  7.9 23.3 %collective-permute-start.1 = (bf16[3,2,48,1024]{3,2,1,0:T(8,128)(2,1)S(1)}, bf16[3,2,48,1024]{3,2,1,0:T(8,128)(2,1)S(1)}, u32[]{:S(2)}, u32[]{:S(2)}) collective-permute-start(bf16[3,2,48,1024]{3,2,1,0:T(8,128)(2,1)S(1)} %get-tuple-element.36.refs_0_.refs_8_.refs_11_.refs_19_.refs_22_.refs_30_), channel_id=1, source_target_pairs={{0,1},{1,0},{2,3},{3,2},{4,5},{5,4},{6,7},{7,6},{8,9},{9,8},{10,11... | collective-permute-start | bytes 1769480 | tf_op jit(solution)/shard_map/own_x/ppermute | solution.py:15
  9.4 19.3 %collective-permute-start = (bf16[2,2,48,1024]{3,2,1,0:T(8,128)(2,1)S(1)}, bf16[2,2,48,1024]{3,2,1,0:T(8,128)(2,1)S(1)}, u32[]{:S(2)}, u32[]{:S(2)}) collective-permute-start(bf16[2,2,48,1024]{3,2,1,0:T(8,128)(2,1)S(1)} %get-tuple-element.38), channel_id=1, source_target_pairs={{0,4},{1,5},{2,6},{3,7},{4,0},{5,1},{6,2},{7,3},{8,12},{9,13},{10,... | collective-permute-start | bytes 1179656 | tf_op jit(solution)/shard_map/got/ppermute | solution.py:15
  12.0 23.2 %collective-permute-start.14 = (bf16[3,2,48,1024]{3,2,1,0:T(8,128)(2,1)S(1)}, bf16[3,2,48,1024]{3,2,1,0:T(8,128)(2,1)S(1)}, u32[]{:S(2)}, u32[]{:S(2)}) collective-permute-start(bf16[3,2,48,1024]{3,2,1,0:T(8,128)(2,1)S(1)} %get-tuple-element.36.refs_0_.refs_8_.refs_11_.refs_19_.refs_22_.refs_30_), channel_id=1, source_target_pairs={{0,24},{8,0},{16,8},{24,16},{1,25},{9,1},{17,9},{25,17},{2,26},{10... | collective-permute-start | bytes 1769480 | tf_op jit(solution)/shard_map/own_y1/ppermute | solution.py:20
  19.7 9.9 %collective-permute-start.3 = (bf16[1,2,48,1024]{3,2,1,0:T(8,128)(2,1)S(1)}, bf16[1,2,48,1024]{3,2,1,0:T(8,128)(2,1)S(1)}, u32[]{:S(2)}, u32[]{:S(2)}) collective-permute-start(bf16[1,2,48,1024]{3,2,1,0:T(8,128)(2,1)S(1)} %get-tuple-element.42), channel_id=1, source_target_pairs={{0,2},{1,3},{2,0},{3,1},{4,6},{5,7},{6,4},{7,5},{8,10},{9,11},{10,... | collective-permute-start | bytes 589832 | tf_op jit(solution)/shard_map/last/ppermute | solution.py:15
  25.5 11.1 %collective-permute-start.6 = (bf16[2,2,48,1024]{3,2,1,0:T(8,128)(2,1)S(1)}, bf16[2,2,48,1024]{3,2,1,0:T(8,128)(2,1)S(1)}, u32[]{:S(2)}, u32[]{:S(2)}) collective-permute-start(bf16[2,2,48,1024]{3,2,1,0:T(8,128)(2,1)S(1)} %collective-permute-done.5.refs_2_.refs_13_), channel_id=1, source_target_pairs={{0,1},{1,0},{2,3},{3,2},{4,5},{5,4},{6,7},{7,6},{8,9},{9,8},{10,11... | collective-permute-start | bytes 1179656 | tf_op jit(solution)/shard_map/front_d/ppermute | solution.py:15
  29.6 13.8 %collective-permute-start.4 = (bf16[2,2,48,1024]{3,2,1,0:T(8,128)(2,1)S(1)}, bf16[2,2,48,1024]{3,2,1,0:T(8,128)(2,1)S(1)}, u32[]{:S(2)}, u32[]{:S(2)}) collective-permute-start(bf16[2,2,48,1024]{3,2,1,0:T(8,128)(2,1)S(1)} %collective-permute-done.refs_4_.refs_8_.refs_15_), channel_id=1, source_target_pairs={{0,2},{1,3},{2,0},{3,1},{4,6},{5,7},{6,4},{7,5},{8,10},{9,11},{10,... | collective-permute-start | bytes 1179656 | tf_op jit(solution)/shard_map/got_z/ppermute | solution.py:15
  31.2 15.4 %collective-permute-start.11 = (bf16[2,2,48,1024]{3,2,1,0:T(8,128)(2,1)S(1)}, bf16[2,2,48,1024]{3,2,1,0:T(8,128)(2,1)S(1)}, u32[]{:S(2)}, u32[]{:S(2)}) collective-permute-start(bf16[2,2,48,1024]{3,2,1,0:T(8,128)(2,1)S(1)} %collective-permute-done.refs_4_.refs_8_.refs_15_), channel_id=1, source_target_pairs={{0,1},{1,0},{2,3},{3,2},{4,5},{5,4},{6,7},{7,6},{8,9},{9,8},{10,11... | collective-permute-start | bytes 1179656 | tf_op jit(solution)/shard_map/got_x/ppermute | solution.py:15
  32.7 12.3 %collective-permute-start.9 = (bf16[1,2,48,1024]{3,2,1,0:T(8,128)(2,1)S(1)}, bf16[1,2,48,1024]{3,2,1,0:T(8,128)(2,1)S(1)}, u32[]{:S(2)}, u32[]{:S(2)}) collective-permute-start(bf16[1,2,48,1024]{3,2,1,0:T(8,128)(2,1)S(1)} %get-tuple-element.48), channel_id=1, source_target_pairs={{0,4},{1,5},{2,6},{3,7},{4,0},{5,1},{6,2},{7,3},{8,12},{9,13},{10,... | collective-permute-start | bytes 589832 | tf_op jit(solution)/shard_map/back_z/ppermute | solution.py:15
  35.2 12.2 %collective-permute-start.17 = (bf16[2,2,48,1024]{3,2,1,0:T(8,128)(2,1)S(1)}, bf16[2,2,48,1024]{3,2,1,0:T(8,128)(2,1)S(1)}, u32[]{:S(2)}, u32[]{:S(2)}) collective-permute-start(bf16[2,2,48,1024]{3,2,1,0:T(8,128)(2,1)S(1)} %collective-permute-done.refs_4_.refs_8_.refs_15_), channel_id=1, source_target_pairs={{0,16},{8,24},{16,0},{24,8},{1,17},{9,25},{17,1},{25,9},{2,18},{10... | collective-permute-start | bytes 1179656 | tf_op jit(solution)/shard_map/got_y2/ppermute | solution.py:20
  36.6 10.9 %collective-permute-start.15 = (bf16[2,2,48,1024]{3,2,1,0:T(8,128)(2,1)S(1)}, bf16[2,2,48,1024]{3,2,1,0:T(8,128)(2,1)S(1)}, u32[]{:S(2)}, u32[]{:S(2)}) collective-permute-start(bf16[2,2,48,1024]{3,2,1,0:T(8,128)(2,1)S(1)} %collective-permute-done.refs_4_.refs_8_.refs_15_), channel_id=1, source_target_pairs={{0,24},{8,0},{16,8},{24,16},{1,25},{9,1},{17,9},{25,17},{2,26},{10... | collective-permute-start | bytes 1179656 | tf_op jit(solution)/shard_map/got_y1/ppermute | solution.py:20
  43.3 15.1 %collective-permute-start.7 = (bf16[2,2,48,1024]{3,2,1,0:T(8,128)(2,1)S(1)}, bf16[2,2,48,1024]{3,2,1,0:T(8,128)(2,1)S(1)}, u32[]{:S(2)}, u32[]{:S(2)}) collective-permute-start(bf16[2,2,48,1024]{3,2,1,0:T(8,128)(2,1)S(1)} %collective-permute-done.4.refs_6_.refs_17_), channel_id=1, source_target_pairs={{0,1},{1,0},{2,3},{3,2},{4,5},{5,4},{6,7},{7,6},{8,9},{9,8},{10,11... | collective-permute-start | bytes 1179656 | tf_op jit(solution)/shard_map/got_d/ppermute | solution.py:15
  44.9 9.4 %collective-permute-start.10 = (bf16[1,2,48,1024]{3,2,1,0:T(8,128)(2,1)S(1)}, bf16[1,2,48,1024]{3,2,1,0:T(8,128)(2,1)S(1)}, u32[]{:S(2)}, u32[]{:S(2)}) collective-permute-start(bf16[1,2,48,1024]{3,2,1,0:T(8,128)(2,1)S(1)} %collective-permute-done.3.refs_2_.refs_8_.refs_24_), channel_id=1, source_target_pairs={{0,4},{1,5},{2,6},{3,7},{4,0},{5,1},{6,2},{7,3},{8,12},{9,13},{10,... | collective-permute-start | bytes 589832 | tf_op jit(solution)/shard_map/last_z/ppermute | solution.py:15
  46.6 10.1 %collective-permute-start.12 = (bf16[1,2,48,1024]{3,2,1,0:T(8,128)(2,1)S(1)}, bf16[1,2,48,1024]{3,2,1,0:T(8,128)(2,1)S(1)}, u32[]{:S(2)}, u32[]{:S(2)}) collective-permute-start(bf16[1,2,48,1024]{3,2,1,0:T(8,128)(2,1)S(1)} %collective-permute-done.9.refs_4_.refs_26_), channel_id=1, source_target_pairs={{0,1},{1,0},{2,3},{3,2},{4,5},{5,4},{6,7},{7,6},{8,9},{9,8},{10,11... | collective-permute-start | bytes 589832 | tf_op jit(solution)/shard_map/back_d/ppermute | solution.py:15
  47.5 18.3 %collective-permute-start.18 = (bf16[1,2,48,1024]{3,2,1,0:T(8,128)(2,1)S(1)}, bf16[1,2,48,1024]{3,2,1,0:T(8,128)(2,1)S(1)}, u32[]{:S(2)}, u32[]{:S(2)}) collective-permute-start(bf16[1,2,48,1024]{3,2,1,0:T(8,128)(2,1)S(1)} %collective-permute-done.3.refs_2_.refs_8_.refs_24_), channel_id=1, source_target_pairs={{0,16},{8,24},{16,0},{24,8},{1,17},{9,25},{17,1},{25,9},{2,18},{10... | collective-permute-start | bytes 589832 | tf_op jit(solution)/shard_map/last_y2/ppermute | solution.py:20
  48.0 18.7 %collective-permute-start.16 = (bf16[1,2,48,1024]{3,2,1,0:T(8,128)(2,1)S(1)}, bf16[1,2,48,1024]{3,2,1,0:T(8,128)(2,1)S(1)}, u32[]{:S(2)}, u32[]{:S(2)}) collective-permute-start(bf16[1,2,48,1024]{3,2,1,0:T(8,128)(2,1)S(1)} %collective-permute-done.3.refs_2_.refs_8_.refs_24_), channel_id=1, source_target_pairs={{0,24},{8,0},{16,8},{24,16},{1,25},{9,1},{17,9},{25,17},{2,26},{10... | collective-permute-start | bytes 589832 | tf_op jit(solution)/shard_map/last_y1/ppermute | solution.py:20
  56.7 10.0 %collective-permute-start.13 = (bf16[1,2,48,1024]{3,2,1,0:T(8,128)(2,1)S(1)}, bf16[1,2,48,1024]{3,2,1,0:T(8,128)(2,1)S(1)}, u32[]{:S(2)}, u32[]{:S(2)}) collective-permute-start(bf16[1,2,48,1024]{3,2,1,0:T(8,128)(2,1)S(1)} %collective-permute-done.10.refs_6_.refs_28_), channel_id=1, source_target_pairs={{0,1},{1,0},{2,3},{3,2},{4,5},{5,4},{6,7},{7,6},{8,9},{9,8},{10,11... | collective-permute-start | bytes 589832 | tf_op jit(solution)/shard_map/last_d/ppermute | solution.py:15
  58.4 8.3 %collective-permute-start.8 = (bf16[1,2,48,1024]{3,2,1,0:T(8,128)(2,1)S(1)}, bf16[1,2,48,1024]{3,2,1,0:T(8,128)(2,1)S(1)}, u32[]{:S(2)}, u32[]{:S(2)}) collective-permute-start(bf16[1,2,48,1024]{3,2,1,0:T(8,128)(2,1)S(1)} %collective-permute-done.3.refs_2_.refs_8_.refs_24_), channel_id=1, source_target_pairs={{0,1},{1,0},{2,3},{3,2},{4,5},{5,4},{6,7},{7,6},{8,9},{9,8},{10,11... | collective-permute-start | bytes 589832 | tf_op jit(solution)/shard_map/last_x/ppermute | solution.py:15
  61.2 17.9 %collective-permute-start.21 = (bf16[2,144,384]{2,1,0:T(8,128)(2,1)S(1)}, bf16[2,144,384]{2,1,0:T(8,128)(2,1)S(1)}, u32[]{:S(2)}, u32[]{:S(2)}) collective-permute-start(bf16[2,144,384]{2,1,0:T(8,128)(2,1)S(1)} %cross_far.5), channel_id=1, source_target_pairs={{0,4},{1,5},{2,6},{3,7},{4,0},{5,1},{6,2},{7,3},{8,12},{9,13},{10,... | collective-permute-start | bytes 663560 | tf_op jit(solution)/shard_map/came0/ppermute | solution.py:15
  65.8 14.6 %collective-permute-start.20 = (bf16[2,144,384]{2,1,0:T(8,128)(2,1)S(1)}, bf16[2,144,384]{2,1,0:T(8,128)(2,1)S(1)}, u32[]{:S(2)}, u32[]{:S(2)}) collective-permute-start(bf16[2,144,384]{2,1,0:T(8,128)(2,1)S(1)} %cross_far.4), channel_id=1, source_target_pairs={{0,4},{1,5},{2,6},{3,7},{4,0},{5,1},{6,2},{7,3},{8,12},{9,13},{10,... | collective-permute-start | bytes 663560 | tf_op jit(solution)/shard_map/came1/ppermute | solution.py:15
  69.2 12.6 %collective-permute-start.19 = (bf16[2,144,384]{2,1,0:T(8,128)(2,1)S(1)}, bf16[2,144,384]{2,1,0:T(8,128)(2,1)S(1)}, u32[]{:S(2)}, u32[]{:S(2)}) collective-permute-start(bf16[2,144,384]{2,1,0:T(8,128)(2,1)S(1)} %cross_far.3), channel_id=1, source_target_pairs={{0,2},{1,3},{2,0},{3,1},{4,6},{5,7},{6,4},{7,5},{8,10},{9,11},{10,... | collective-permute-start | bytes 663560 | tf_op jit(solution)/shard_map/came2/ppermute | solution.py:15
